TPU v7x, 32 devices: a whole 2x2x4 slice. The times are simulated.
32 devices in a mesh: sec: 4 (over x, core), seq: 8 (over z, y).
Axes of the slice: x: 2, y: 2, z: 4, core: 2. Of those that a mesh axis runs over, the one named last changes fastest.
Arguments:
- student_qkv: bfloat16 [1024, 3, 2560], P('seq', None, 'sec'), may hold values from -19 to 19
- target_qkv: bfloat16 [1024, 3, 2560], P('seq', None, 'sec'), may hold values from -19 to 19
- clip_lengths: int32 [4], replicated, may hold values from 1 to 384, 1024 in all
Outputs:
- student_grads: bfloat16 [1024, 3, 2560], P('seq', None, 'sec')
- target_out: bfloat16 [1024, 2560], P('seq', 'sec')
Inputs may be any that keep to these rules, and one draw needn't show every extreme that they name: `clip_lengths`: the clip lengths sum to 1024, and the longest clip has exactly 384 tokens.
All inputs are finite; a program needn't handle non-finite values.
Results may differ from a plain program's by a relative error of at most 0.012.
Values may be sent and summed in bfloat16 or wider, within the bound.
No kernel may reach another device: no remote copies, remote signals or barrier semaphores. Data moves between devices by JAX's collectives and lax.ppermute only.
A program may use at most 64 MiB of HBM per device.

v0:
```python
import math

import jax
import jax.numpy as jnp
from jax import lax
from jax.sharding import PartitionSpec as P

H = 20
HS = 128
REACH = 3


EPS = 1e-05
HIGHEST_PRECISION = lax.Precision.HIGHEST


def passed_along(value, axis, steps):
    count = lax.axis_size(axis)
    initial, last = (max(0, -steps), min(count, count - steps))
    return lax.ppermute(value, axis, [(source, source + steps) for source in range(initial, last)])


def clip_ids(bounds, positions, total_rows):
    counted = jnp.sum((bounds[None, :] <= positions[:, None]).astype(jnp.int32), axis=1)
    inside = (positions >= 0) & (positions < total_rows)
    local_index = jnp.arange(positions.shape[0], dtype=jnp.int32)
    return jnp.where(inside, counted, -1 - local_index)


def collect(own_rows, send_down, send_up):
    lower_blocks = []
    upper_blocks = []
    lower_block = own_rows
    upper_block = own_rows
    for distance in range(REACH):
        lower_block = send_down(lower_block)
        upper_block = send_up(upper_block)
        lower_blocks.insert(0, lower_block)
        upper_blocks.append(upper_block)
    return jnp.concatenate(lower_blocks + [own_rows] + upper_blocks, axis=0)


def attend(queries, keys_window, values_window, allowed, score_scale):
    scores = (
        jnp.einsum("qhd,khd->hqk", queries, keys_window, preferred_element_type=jnp.float32)
        * score_scale
    )
    scores = jnp.where(allowed[None], scores, -jnp.inf)
    row_peak = jnp.max(scores, axis=2)
    exponent = jnp.exp(scores - row_peak[:, :, None])
    row_total = jnp.sum(exponent, axis=2)
    probability = exponent / row_total[:, :, None]
    weights = probability.astype(jnp.bfloat16)
    output = jnp.einsum("hqk,khd->qhd", weights, values_window, preferred_element_type=jnp.float32)
    return (output, probability, weights, row_peak, row_total)


def per_device(student_qkv, target_qkv, clip_lengths):
    tok_rows = student_qkv.shape[0]
    feat_width = student_qkv.shape[2]
    head_count = feat_width // HS
    rim_rows = REACH * tok_rows
    window_rows = tok_rows + 2 * rim_rows
    score_scale = 1.0 / math.sqrt(HS)
    total_rows = tok_rows * lax.axis_size("seq")
    first_row = lax.axis_index("seq") * tok_rows
    bounds = jnp.cumsum(clip_lengths)
    own_ids = clip_ids(bounds, first_row + jnp.arange(tok_rows, dtype=jnp.int32), total_rows)
    window_ids = clip_ids(
        bounds, first_row - rim_rows + jnp.arange(window_rows, dtype=jnp.int32), total_rows
    )
    allowed = own_ids[:, None] == window_ids[None, :]

    def heads_of(rows):
        return rows.reshape(rows.shape[0], head_count, HS)

    key_pairs = jnp.concatenate([student_qkv[:, 1:], target_qkv[:, 1:]], axis=1)
    nearby = collect(
        key_pairs,
        lambda piece: passed_along(piece, "seq", 1),
        lambda piece: passed_along(piece, "seq", -1),
    )
    student_keys = heads_of(nearby[:, 0])
    student_values = heads_of(nearby[:, 1])
    target_keys = heads_of(nearby[:, 2])
    target_values = heads_of(nearby[:, 3])
    student_queries = heads_of(student_qkv[:, 0])
    student_out, probability, weights, row_peak, row_total = attend(
        student_queries, student_keys, student_values, allowed, score_scale
    )
    target_out = attend(
        heads_of(target_qkv[:, 0]), target_keys, target_values, allowed, score_scale
    )[0]
    difference = student_out - target_out
    row_squares = jnp.sum(difference * difference, axis=(1, 2))
    clip_index = jnp.arange(clip_lengths.shape[0], dtype=jnp.int32)
    one_hot = (own_ids[:, None] == clip_index[None, :]).astype(jnp.float32)
    partial_sums = jnp.dot(row_squares, one_hot, precision=HIGHEST_PRECISION)
    clip_totals = lax.psum(partial_sums, ("sec", "seq"))
    token_total = jnp.dot(one_hot, clip_totals, precision=HIGHEST_PRECISION)
    clip_size = jnp.sum(allowed.astype(jnp.float32), axis=1)
    factor = lax.rsqrt(token_total / (clip_size * (H * HS)) + EPS)
    out_grad = (difference * factor[:, None, None]).astype(jnp.bfloat16)
    delta_sum = jnp.sum(out_grad.astype(jnp.float32) * student_out, axis=2)
    grad_prob = jnp.einsum(
        "qhd,khd->hqk", out_grad, student_values, preferred_element_type=jnp.float32
    )
    grad_score = (probability * (grad_prob - delta_sum.T[:, :, None]) * score_scale).astype(
        jnp.bfloat16
    )
    grad_query = jnp.einsum(
        "hqk,khd->qhd", grad_score, student_keys, preferred_element_type=jnp.float32
    )
    grad_query = grad_query.reshape(tok_rows, feat_width)
    window_key = jnp.einsum(
        "hqk,qhd->khd", grad_score, student_queries, preferred_element_type=jnp.float32
    )
    window_value = jnp.einsum("hqk,qhd->khd", weights, out_grad, preferred_element_type=jnp.float32)
    window_grads = jnp.stack(
        [
            window_key.reshape(window_rows, feat_width),
            window_value.reshape(window_rows, feat_width),
        ],
        axis=1,
    )
    lower_part = window_grads[:rim_rows].reshape(REACH, tok_rows, 2, feat_width)
    upper_part = window_grads[rim_rows + tok_rows :].reshape(REACH, tok_rows, 2, feat_width)
    from_above = lower_part[0]
    for distance in range(1, REACH + 1):
        from_above = passed_along(from_above, "seq", -1)
        if distance < REACH:
            from_above = from_above + lower_part[distance]
    from_below = upper_part[REACH - 1]
    for distance in range(1, REACH + 1):
        from_below = passed_along(from_below, "seq", 1)
        if distance < REACH:
            from_below = from_below + upper_part[REACH - 1 - distance]
    own_grads = window_grads[rim_rows : rim_rows + tok_rows] + from_above + from_below
    grad_key = own_grads[:, 0]
    grad_value = own_grads[:, 1]
    student_grads = jnp.stack([grad_query, grad_key, grad_value], axis=1).astype(jnp.bfloat16)
    return (student_grads, target_out.astype(jnp.bfloat16).reshape(tok_rows, feat_width))


def solution(mesh):
    return jax.shard_map(
        per_device,
        mesh=mesh,
        in_specs=(P("seq", None, "sec"), P("seq", None, "sec"), P()),
        out_specs=(P("seq", None, "sec"), P("seq", "sec")),
        check_vma=False,
    )
```

profile of v0, /device:TPU:18, one launch (start us, length us, event | category | flops | bytes accessed | tf_op | source)
XLA Modules:
  0.0 267.0 jit_solution(6148437519469374786)
XLA Ops:
  3.2 3.4 %collective-permute-start = (bf16[128,4,640]{0,2,1:T(8,128)(2,1)S(1)}, bf16[128,4,640]{0,2,1:T(8,128)(2,1)S(1)}, u32[]{:S(2)}, u32[]{:S(2)}) collective-permute-start(bf16[128,4,640]{0,2,1:T(8,128)(2,1)S(1)} %pad_maximum_fusion.1), channel_id=1, source_target_pairs={{0,1},{1,2},{2,3},{3,4},{4,5},{5,6},{6,7},{8,9},{9,10},{10,11},{11... | collective-permute-start | bytes 1966088 | tf_op jit(solution)/shard_map/ppermute | solution.py:20
  6.6 3.3 %collective-permute-start.3 = (bf16[128,4,640]{0,2,1:T(8,128)(2,1)S(1)}, bf16[128,4,640]{0,2,1:T(8,128)(2,1)S(1)}, u32[]{:S(2)}, u32[]{:S(2)}) collective-permute-start(bf16[128,4,640]{0,2,1:T(8,128)(2,1)S(1)} %pad_maximum_fusion.1), channel_id=1, source_target_pairs={{1,0},{2,1},{3,2},{4,3},{5,4},{6,5},{7,6},{9,8},{10,9},{11,10},{12... | collective-permute-start | bytes 1966088 | tf_op jit(solution)/shard_map/ppermute | solution.py:20
  9.9 24.7 %collective-permute-done = bf16[128,4,640]{0,2,1:T(8,128)(2,1)S(1)} collective-permute-done((bf16[128,4,640]{0,2,1:T(8,128)(2,1)S(1)}, bf16[128,4,640]{0,2,1:T(8,128)(2,1)S(1)}, u32[]{:S(2)}, u32[]{:S(2)}) %collective-permute-start) | collective-permute-done | bytes 655392 | tf_op jit(solution)/shard_map/ppermute | solution.py:20
  34.6 4.4 %collective-permute-start.1 = (bf16[128,4,640]{0,2,1:T(8,128)(2,1)S(1)}, bf16[128,4,640]{0,2,1:T(8,128)(2,1)S(1)}, u32[]{:S(2)}, u32[]{:S(2)}) collective-permute-start(bf16[128,4,640]{0,2,1:T(8,128)(2,1)S(1)} %collective-permute-done), channel_id=1, source_target_pairs={{0,1},{1,2},{2,3},{3,4},{4,5},{5,6},{6,7},{8,9},{9,10},{10,11},{11... | collective-permute-start | bytes 1966088 | tf_op jit(solution)/shard_map/ppermute | solution.py:20
  45.9 20.3 %collective-permute-done.1 = bf16[128,4,640]{0,2,1:T(8,128)(2,1)S(1)} collective-permute-done((bf16[128,4,640]{0,2,1:T(8,128)(2,1)S(1)}, bf16[128,4,640]{0,2,1:T(8,128)(2,1)S(1)}, u32[]{:S(2)}, u32[]{:S(2)}) %collective-permute-start.1) | collective-permute-done | bytes 655392 | tf_op jit(solution)/shard_map/ppermute | solution.py:20
  66.2 4.4 %collective-permute-start.2 = (bf16[128,4,640]{0,2,1:T(8,128)(2,1)S(1)}, bf16[128,4,640]{0,2,1:T(8,128)(2,1)S(1)}, u32[]{:S(2)}, u32[]{:S(2)}) collective-permute-start(bf16[128,4,640]{0,2,1:T(8,128)(2,1)S(1)} %collective-permute-done.1), channel_id=1, source_target_pairs={{0,1},{1,2},{2,3},{3,4},{4,5},{5,6},{6,7},{8,9},{9,10},{10,11},{11... | collective-permute-start | bytes 1966088 | tf_op jit(solution)/shard_map/ppermute | solution.py:20
  73.5 23.2 %collective-permute-done.2 = bf16[128,4,640]{0,2,1:T(8,128)(2,1)S(1)} collective-permute-done((bf16[128,4,640]{0,2,1:T(8,128)(2,1)S(1)}, bf16[128,4,640]{0,2,1:T(8,128)(2,1)S(1)}, u32[]{:S(2)}, u32[]{:S(2)}) %collective-permute-start.2) | collective-permute-done | bytes 655392 | tf_op jit(solution)/shard_map/ppermute | solution.py:20
  99.3 2.7 fusion.47
  101.9 3.4 %convolution_bitcast_fusion = f32[128,5,128]{0,2,1:T(8,128)} fusion(bf16[896,5,128]{0,2,1:T(8,128)(2,1)} %bitcast.94, f32[5,128]{1,0:T(8,128)} %fusion.47, pred[128,896]{0,1:T(8,128)(4,1)S(1)} %broadcast_compare_fusion, bf16[896,5,128]{0,2,1:T(8,128)(2,1)S(1)} %bitcast.93, bf16[128,5,128]{0,2,1:T(8,128)(2,1)} %bitcast.102), kind=kOutput, calls=%fused_computation.22 | convolution fusion | flops 296470016 | bytes 2902528 | tf_op jit(solution)/shard_map/hqk,khd->qhd/dot_general | solution.py:54
  105.3 3.3 %fusion.48 = (f32[5,128]{1,0:T(8,128)S(1)}, f32[5,128,896]{1,2,0:T(8,128)}) fusion(pred[128,896]{0,1:T(8,128)(4,1)S(1)} %broadcast_compare_fusion, bf16[896,5,128]{0,2,1:T(8,128)(2,1)S(1)} %bitcast.85, bf16[128,5,128]{0,2,1:T(8,128)(2,1)} %bitcast.95), kind=kOutput, calls=%fused_computation.88 | convolution fusion | flops 149095296 | bytes 3721728 | tf_op jit(solution)/shard_map/sub | solution.py:50
  108.6 3.1 %multiply_reduce_fusion.1 = (f32[128]{0:T(128)S(1)}, f32[128,5,128]{0,2,1:T(8,128)S(1)}, bf16[128,5,128]{0,2,1:T(8,128)(2,1)}, f32[128,5,128]{0,2,1:T(8,128)S(1)}) fusion(f32[128,5,128]{0,2,1:T(8,128)} %convolution_bitcast_fusion, bf16[896,5,128]{0,2,1:T(8,128)(2,1)S(1)} %bitcast.90, f32[5,128]{1,0:T(8,128)S(1)} %get-tuple-element.17, ...), kind=kOutput, calls=%fused_computation.57 | convolution fusion | flops 296797568 | bytes 3722240 | tf_op jit(solution)/shard_map/hqk,khd->qhd/dot_general | solution.py:54
  112.2 40.6 %psum.7 = f32[4]{0:T(128)S(1)} all-reduce(f32[4]{0:T(128)S(1)} %convolution_bitcast_fusion.3), channel_id=1, replica_groups=mesh['sec'=4,'seq'=8] {'sec','seq'}, use_global_device_ids=true, to_apply=%region_8.9 | all-reduce | flops 4 | bytes 32 | tf_op jit(solution)/shard_map/psum | solution.py:99
  158.1 2.8 %multiply_convert_fusion = bf16[5,128,896]{1,2,0:T(8,128)(2,1)S(1)} fusion(bf16[896,5,128]{0,2,1:T(8,128)(2,1)} %bitcast.91, f32[5,128]{1,0:T(8,128)S(1)} %bitcast.103, f32[5,128,896]{1,2,0:T(8,128)} %get-tuple-element.18, f32[5,128]{1,0:T(8,128)S(1)} %copy-done.15, f32[128,5,128]{0,2,1:T(8,128)} %copy-done.6, f32[128]{0:T(128)S(1)} %copy-done.12), kind=kOutput, calls=%fused_computation.16 | convolution fusion | flops 149831680 | bytes 4920832 | tf_op jit(solution)/shard_map/qhd,khd->hqk/dot_general | solution.py:105
  163.9 3.1 %copy.57 = f32[896,1,640]{2,0,1:T(8,128)} copy(f32[896,1,640]{0,2,1:T(8,128)} %bitcast.84) | data formatting | bytes 4587520 | tf_op jit(solution)/shard_map/stack;reshape | solution.py:119
  168.2 2.9 %collective-permute-start.6 = (f32[128,2,640]{2,0,1:T(8,128)S(1)}, f32[128,2,640]{2,0,1:T(8,128)S(1)}, u32[]{:S(2)}, u32[]{:S(2)}) collective-permute-start(f32[128,2,640]{2,0,1:T(8,128)S(1)} %fusion.20), channel_id=1, source_target_pairs={{1,0},{2,1},{3,2},{4,3},{5,4},{6,5},{7,6},{9,8},{10,9},{11,10},{12... | collective-permute-start | bytes 1966088 | tf_op jit(solution)/shard_map/ppermute | solution.py:20
  171.1 14.1 %collective-permute-done.6 = f32[128,2,640]{2,0,1:T(8,128)S(1)} collective-permute-done((f32[128,2,640]{2,0,1:T(8,128)S(1)}, f32[128,2,640]{2,0,1:T(8,128)S(1)}, u32[]{:S(2)}, u32[]{:S(2)}) %collective-permute-start.6) | collective-permute-done | bytes 655392 | tf_op jit(solution)/shard_map/ppermute | solution.py:20
  185.3 4.4 %collective-permute-start.7 = (f32[128,2,640]{2,0,1:T(8,128)S(1)}, f32[128,2,640]{2,0,1:T(8,128)S(1)}, u32[]{:S(2)}, u32[]{:S(2)}) collective-permute-start(f32[128,2,640]{2,0,1:T(8,128)S(1)} %fusion.22), channel_id=1, source_target_pairs={{1,0},{2,1},{3,2},{4,3},{5,4},{6,5},{7,6},{9,8},{10,9},{11,10},{12... | collective-permute-start | bytes 1966088 | tf_op jit(solution)/shard_map/ppermute | solution.py:20
  189.7 12.2 %collective-permute-done.7 = f32[128,2,640]{2,0,1:T(8,128)S(1)} collective-permute-done((f32[128,2,640]{2,0,1:T(8,128)S(1)}, f32[128,2,640]{2,0,1:T(8,128)S(1)}, u32[]{:S(2)}, u32[]{:S(2)}) %collective-permute-start.7) | collective-permute-done | bytes 655392 | tf_op jit(solution)/shard_map/ppermute | solution.py:20
  202.9 4.5 %collective-permute-start.9 = (f32[128,2,640]{2,0,1:T(8,128)S(1)}, f32[128,2,640]{2,0,1:T(8,128)S(1)}, u32[]{:S(2)}, u32[]{:S(2)}) collective-permute-start(f32[128,2,640]{2,0,1:T(8,128)S(1)} %get-tuple-element.11), channel_id=1, source_target_pairs={{0,1},{1,2},{2,3},{3,4},{4,5},{5,6},{6,7},{8,9},{9,10},{10,11},{11... | collective-permute-start | bytes 1966088 | tf_op jit(solution)/shard_map/ppermute | solution.py:20
  207.4 12.8 %collective-permute-done.9 = f32[128,2,640]{2,0,1:T(8,128)S(1)} collective-permute-done((f32[128,2,640]{2,0,1:T(8,128)S(1)}, f32[128,2,640]{2,0,1:T(8,128)S(1)}, u32[]{:S(2)}, u32[]{:S(2)}) %collective-permute-start.9) | collective-permute-done | bytes 655392 | tf_op jit(solution)/shard_map/ppermute | solution.py:20
  222.9 4.3 %collective-permute-start.8 = (f32[128,2,640]{2,0,1:T(8,128)}, f32[128,2,640]{2,0,1:T(8,128)}, u32[]{:S(2)}, u32[]{:S(2)}) collective-permute-start(f32[128,2,640]{2,0,1:T(8,128)} %get-tuple-element.10), channel_id=1, source_target_pairs={{1,0},{2,1},{3,2},{4,3},{5,4},{6,5},{7,6},{9,8},{10,9},{11,10},{12... | collective-permute-start | bytes 1966088 | tf_op jit(solution)/shard_map/ppermute | solution.py:20
  227.2 20.0 %collective-permute-done.10 = f32[128,2,640]{2,0,1:T(8,128)S(1)} collective-permute-done((f32[128,2,640]{2,0,1:T(8,128)S(1)}, f32[128,2,640]{2,0,1:T(8,128)S(1)}, u32[]{:S(2)}, u32[]{:S(2)}) %collective-permute-start.10) | collective-permute-done | bytes 655392 | tf_op jit(solution)/shard_map/ppermute | solution.py:20
  248.2 4.4 %collective-permute-start.11 = (f32[128,2,640]{2,0,1:T(8,128)}, f32[128,2,640]{2,0,1:T(8,128)}, u32[]{:S(2)}, u32[]{:S(2)}) collective-permute-start(f32[128,2,640]{2,0,1:T(8,128)} %fusion.26), channel_id=1, source_target_pairs={{0,1},{1,2},{2,3},{3,4},{4,5},{5,6},{6,7},{8,9},{9,10},{10,11},{11... | collective-permute-start | bytes 1966088 | tf_op jit(solution)/shard_map/ppermute | solution.py:20
  256.5 8.2 %collective-permute-done.11 = f32[128,2,640]{2,0,1:T(8,128)} collective-permute-done((f32[128,2,640]{2,0,1:T(8,128)}, f32[128,2,640]{2,0,1:T(8,128)}, u32[]{:S(2)}, u32[]{:S(2)}) %collective-permute-start.11) | collective-permute-done | bytes 655392 | tf_op jit(solution)/shard_map/ppermute | solution.py:20
  (82 shorter events, 35.5 us)
Async XLA Ops:
  1.6 40.7 %slice-start = ((bf16[128,3,640]{2,0,1:T(8,128)(2,1)}), bf16[128,1,640]{2,0,1:T(8,128)(2,1)S(1)}, s32[]{:S(2)}) async-start(bf16[128,3,640]{2,0,1:T(8,128)(2,1)} %param.3), calls=%async_computation | async-start | bytes 327680 | tf_op jit(solution)/shard_map/slice | solution.py:87
  1.6 41.5 %copy-start.13 = (s32[4]{0:T(128)S(1)}, s32[4]{0:T(128)}, u32[]{:S(2)}) copy-start(s32[4]{0:T(128)} %param.5) | copy-start | bytes 52
  3.2 31.4 %collective-permute-start = (bf16[128,4,640]{0,2,1:T(8,128)(2,1)S(1)}, bf16[128,4,640]{0,2,1:T(8,128)(2,1)S(1)}, u32[]{:S(2)}, u32[]{:S(2)}) collective-permute-start(bf16[128,4,640]{0,2,1:T(8,128)(2,1)S(1)} %pad_maximum_fusion.1), channel_id=1, source_target_pairs={{0,1},{1,2},{2,3},{3,4},{4,5},{5,6},{6,7},{8,9},{9,10},{10,11},{11... | collective-permute-start | bytes 1966088 | tf_op jit(solution)/shard_map/ppermute | solution.py:20
  6.6 36.9 %collective-permute-start.3 = (bf16[128,4,640]{0,2,1:T(8,128)(2,1)S(1)}, bf16[128,4,640]{0,2,1:T(8,128)(2,1)S(1)}, u32[]{:S(2)}, u32[]{:S(2)}) collective-permute-start(bf16[128,4,640]{0,2,1:T(8,128)(2,1)S(1)} %pad_maximum_fusion.1), channel_id=1, source_target_pairs={{1,0},{2,1},{3,2},{4,3},{5,4},{6,5},{7,6},{9,8},{10,9},{11,10},{12... | collective-permute-start | bytes 1966088 | tf_op jit(solution)/shard_map/ppermute | solution.py:20
  34.6 31.5 %collective-permute-start.1 = (bf16[128,4,640]{0,2,1:T(8,128)(2,1)S(1)}, bf16[128,4,640]{0,2,1:T(8,128)(2,1)S(1)}, u32[]{:S(2)}, u32[]{:S(2)}) collective-permute-start(bf16[128,4,640]{0,2,1:T(8,128)(2,1)S(1)} %collective-permute-done), channel_id=1, source_target_pairs={{0,1},{1,2},{2,3},{3,4},{4,5},{5,6},{6,7},{8,9},{9,10},{10,11},{11... | collective-permute-start | bytes 1966088 | tf_op jit(solution)/shard_map/ppermute | solution.py:20
  43.5 27.7 %collective-permute-start.4 = (bf16[128,4,640]{0,2,1:T(8,128)(2,1)S(1)}, bf16[128,4,640]{0,2,1:T(8,128)(2,1)S(1)}, u32[]{:S(2)}, u32[]{:S(2)}) collective-permute-start(bf16[128,4,640]{0,2,1:T(8,128)(2,1)S(1)} %collective-permute-done.3), channel_id=1, source_target_pairs={{1,0},{2,1},{3,2},{4,3},{5,4},{6,5},{7,6},{9,8},{10,9},{11,10},{12... | collective-permute-start | bytes 1966088 | tf_op jit(solution)/shard_map/ppermute | solution.py:20
  66.2 30.6 %collective-permute-start.2 = (bf16[128,4,640]{0,2,1:T(8,128)(2,1)S(1)}, bf16[128,4,640]{0,2,1:T(8,128)(2,1)S(1)}, u32[]{:S(2)}, u32[]{:S(2)}) collective-permute-start(bf16[128,4,640]{0,2,1:T(8,128)(2,1)S(1)} %collective-permute-done.1), channel_id=1, source_target_pairs={{0,1},{1,2},{2,3},{3,4},{4,5},{5,6},{6,7},{8,9},{9,10},{10,11},{11... | collective-permute-start | bytes 1966088 | tf_op jit(solution)/shard_map/ppermute | solution.py:20
  71.2 26.5 %collective-permute-start.5 = (bf16[128,4,640]{0,2,1:T(8,128)(2,1)S(1)}, bf16[128,4,640]{0,2,1:T(8,128)(2,1)S(1)}, u32[]{:S(2)}, u32[]{:S(2)}) collective-permute-start(bf16[128,4,640]{0,2,1:T(8,128)(2,1)S(1)} %collective-permute-done.4), channel_id=1, source_target_pairs={{1,0},{2,1},{3,2},{4,3},{5,4},{6,5},{7,6},{9,8},{10,9},{11,10},{12... | collective-permute-start | bytes 1966088 | tf_op jit(solution)/shard_map/ppermute | solution.py:20
  99.3 9.4 %copy-start.3 = (bf16[896,1,640]{0,2,1:T(8,128)(2,1)}, bf16[896,1,640]{0,2,1:T(8,128)(2,1)S(1)}, u32[]{:S(2)}) copy-start(bf16[896,1,640]{0,2,1:T(8,128)(2,1)S(1)} %get-tuple-element.14) | copy-start | bytes 3440644
  105.3 3.3 %copy-start.4 = (bf16[128,1,640]{0,2,1:T(8,128)(2,1)S(1)}, bf16[128,1,640]{0,2,1:T(8,128)(2,1)}, u32[]{:S(2)}) copy-start(bf16[128,1,640]{0,2,1:T(8,128)(2,1)} %copy.75) | copy-start | bytes 491524
  108.6 44.3 %copy-start.14 = (f32[5,128]{1,0:T(8,128)}, f32[5,128]{1,0:T(8,128)S(1)}, u32[]{:S(2)}) copy-start(f32[5,128]{1,0:T(8,128)S(1)} %get-tuple-element.17) | copy-start | bytes 7684
  108.6 3.1 %copy-start.10 = (s32[128]{0:T(128)S(1)}, s32[128]{0:T(128)}, u32[]{:S(2)}) copy-start(s32[128]{0:T(128)} %copy-done.9) | copy-start | bytes 1540
  108.6 3.3 %copy-start.8 = (s32[896]{0:T(1024)S(1)}, s32[896]{0:T(1024)}, u32[]{:S(2)}) copy-start(s32[896]{0:T(1024)} %copy-done.7) | copy-start | bytes 10756
  111.7 43.9 %copy-start.6 = (f32[128,5,128]{0,2,1:T(8,128)}, f32[128,5,128]{0,2,1:T(8,128)S(1)}, u32[]{:S(2)}) copy-start(f32[128,5,128]{0,2,1:T(8,128)S(1)} %get-tuple-element.9) | copy-start | bytes 983044
  152.9 2.7 %copy-start.11 = (f32[128]{0:T(128)}, f32[128]{0:T(128)S(1)}, u32[]{:S(2)}) copy-start(f32[128]{0:T(128)S(1)} %fusion.12) | copy-start | bytes 1540
  158.1 3.8 %copy-start.5 = (bf16[128,1,640]{0,2,1:T(8,128)(2,1)S(1)}, bf16[128,1,640]{0,2,1:T(8,128)(2,1)}, u32[]{:S(2)}) copy-start(bf16[128,1,640]{0,2,1:T(8,128)(2,1)} %copy.75) | copy-start | bytes 491524
  167.0 18.1 %copy-start = (f32[896,1,640]{2,0,1:T(8,128)S(1)}, f32[896,1,640]{2,0,1:T(8,128)}, u32[]{:S(2)}) copy-start(f32[896,1,640]{2,0,1:T(8,128)} %copy.57) | copy-start | bytes 6881284
  168.2 17.0 %collective-permute-start.6 = (f32[128,2,640]{2,0,1:T(8,128)S(1)}, f32[128,2,640]{2,0,1:T(8,128)S(1)}, u32[]{:S(2)}, u32[]{:S(2)}) collective-permute-start(f32[128,2,640]{2,0,1:T(8,128)S(1)} %fusion.20), channel_id=1, source_target_pairs={{1,0},{2,1},{3,2},{4,3},{5,4},{6,5},{7,6},{9,8},{10,9},{11,10},{12... | collective-permute-start | bytes 1966088 | tf_op jit(solution)/shard_map/ppermute | solution.py:20
  185.3 16.6 %collective-permute-start.7 = (f32[128,2,640]{2,0,1:T(8,128)S(1)}, f32[128,2,640]{2,0,1:T(8,128)S(1)}, u32[]{:S(2)}, u32[]{:S(2)}) collective-permute-start(f32[128,2,640]{2,0,1:T(8,128)S(1)} %fusion.22), channel_id=1, source_target_pairs={{1,0},{2,1},{3,2},{4,3},{5,4},{6,5},{7,6},{9,8},{10,9},{11,10},{12... | collective-permute-start | bytes 1966088 | tf_op jit(solution)/shard_map/ppermute | solution.py:20
  202.9 17.3 %collective-permute-start.9 = (f32[128,2,640]{2,0,1:T(8,128)S(1)}, f32[128,2,640]{2,0,1:T(8,128)S(1)}, u32[]{:S(2)}, u32[]{:S(2)}) collective-permute-start(f32[128,2,640]{2,0,1:T(8,128)S(1)} %get-tuple-element.11), channel_id=1, source_target_pairs={{0,1},{1,2},{2,3},{3,4},{4,5},{5,6},{6,7},{8,9},{9,10},{10,11},{11... | collective-permute-start | bytes 1966088 | tf_op jit(solution)/shard_map/ppermute | solution.py:20
  220.3 26.9 %collective-permute-start.10 = (f32[128,2,640]{2,0,1:T(8,128)S(1)}, f32[128,2,640]{2,0,1:T(8,128)S(1)}, u32[]{:S(2)}, u32[]{:S(2)}) collective-permute-start(f32[128,2,640]{2,0,1:T(8,128)S(1)} %fusion.15), channel_id=1, source_target_pairs={{0,1},{1,2},{2,3},{3,4},{4,5},{5,6},{6,7},{8,9},{9,10},{10,11},{11... | collective-permute-start | bytes 1966088 | tf_op jit(solution)/shard_map/ppermute | solution.py:20
  222.9 29.7 %copy-start.2 = (bf16[5,128,896]{1,2,0:T(8,128)(2,1)S(1)}, bf16[5,128,896]{1,2,0:T(8,128)(2,1)}, u32[]{:S(2)}) copy-start(bf16[5,128,896]{1,2,0:T(8,128)(2,1)} %copy-done.1) | copy-start | bytes 3440644
  222.9 33.6 %collective-permute-start.8 = (f32[128,2,640]{2,0,1:T(8,128)}, f32[128,2,640]{2,0,1:T(8,128)}, u32[]{:S(2)}, u32[]{:S(2)}) collective-permute-start(f32[128,2,640]{2,0,1:T(8,128)} %get-tuple-element.10), channel_id=1, source_target_pairs={{1,0},{2,1},{3,2},{4,3},{5,4},{6,5},{7,6},{9,8},{10,9},{11,10},{12... | collective-permute-start | bytes 1966088 | tf_op jit(solution)/shard_map/ppermute | solution.py:20
  248.2 16.5 %collective-permute-start.11 = (f32[128,2,640]{2,0,1:T(8,128)}, f32[128,2,640]{2,0,1:T(8,128)}, u32[]{:S(2)}, u32[]{:S(2)}) collective-permute-start(f32[128,2,640]{2,0,1:T(8,128)} %fusion.26), channel_id=1, source_target_pairs={{0,1},{1,2},{2,3},{3,4},{4,5},{5,6},{6,7},{8,9},{9,10},{10,11},{11... | collective-permute-start | bytes 1966088 | tf_op jit(solution)/shard_map/ppermute | solution.py:20
  (5 other events, 7.1 us)
where the time goes:
time: 269 us; the launch traced here: 267 us
  waiting for transfers between devices  136 us (51%)
  starting transfers between devices  43.2 us (16%)
  blocking collectives  40.6 us (15%)
  matrix products  21.3 us (8%)
  local copies, waits for them, and re-layouts  18.7 us (7%)
  other arithmetic  6.62 us (2%)
    ppermute x12, waiting for transfers between devices, passed_along(): lax.ppermute(value, axis, [(source, source + steps) for source in range(i...  136 us
    ppermute x12, starting transfers between devices, passed_along(): lax.ppermute(value, axis, [(source, source + steps) for source in range(i...  43.2 us
    psum x1, blocking collectives, per_device(): clip_totals = lax.psum(partial_sums, ('sec', 'seq'))  40.6 us
    unnamed x42, local copies, waits for them, and re-layouts  6.9 us
    dot_general x2, matrix products, attend(): jnp.einsum('hqk,khd->qhd', weights, values_window, preferred_element_type...  6.48 us
    sub x2, matrix products, attend(): exponent = jnp.exp(scores - row_peak[:, :, None])  5.96 us
    another operation x2, local copies, waits for them, and re-layouts, per_device(): jnp.stack([window_key.reshape(window_rows, feat_width), window_value.resh...  5.53 us
  transfers between devices with their start and end apart: 12, of which 8 were waited for; matrix products, arithmetic and copies ran while one was open for 4% of the time, Pallas kernels for 0%

commit v1 on v0

v1 whole, which is shorter than its diff:
```python
import functools
import math

import jax
import jax.numpy as jnp
from jax import lax
from jax.experimental import pallas as pl
from jax.experimental.pallas import tpu as pltpu
from jax.sharding import PartitionSpec as P

H = 20
HS = 128
MOST = 384
EPS = 1e-05

GROUP = 8
OWNERS = ((0, 2, 4, 5, 7), (1, 2, 3, 5, 6))
ROUNDS = (4, 1, 5, 2, 6, 3, 7)
QUERY_TILE = 256
VMEM_BYTES = 48 * 1024 * 1024

BF16 = jnp.bfloat16
F32 = jnp.float32
ROWS_BY_ROWS = (((1,), (1,)), ((), ()))
VMEM = pl.BlockSpec(memory_space=pltpu.VMEM)
SMEM = pl.BlockSpec(memory_space=pltpu.SMEM)


def owner_code(owners):
    return sum((head + 1) << (3 * place) for head, place in enumerate(owners))


def place_and_code():
    place = lax.rem(lax.axis_index("seq"), GROUP)
    odd = lax.rem(lax.axis_index("sec"), 2) == 1
    code = jnp.where(odd, owner_code(OWNERS[1]), owner_code(OWNERS[0])).astype(jnp.int32)
    return place, code


def head_at(code, place):
    return lax.bitwise_and(lax.shift_right_logical(code, 3 * place), 7) - 1


def columns_of(head):
    return pl.ds(pl.multiple_of(head * HS, HS), HS)


def pack_kernel(student_ref, target_ref, *slots):
    place, code = place_and_code()
    for k in range(GROUP):
        head = head_at(code, lax.bitwise_xor(place, k))

        @pl.when(head >= 0)
        def _():
            slots[k][:3] = student_ref[:, :, columns_of(head)]
            slots[k][3:] = target_ref[:, :, columns_of(head)]


def clip_bounds(lengths_ref, count):
    bounds, total = [], jnp.int32(0)
    for clip in range(count):
        total = total + lengths_ref[clip]
        bounds.append(total)
    return bounds


def head_kernel(clip_count, extra, lengths_ref, *refs):
    slots = refs[: GROUP + extra]
    outs = refs[GROUP + extra : 2 * (GROUP + extra)]
    totals_ref, data, turned, ids_ref, grads = refs[2 * (GROUP + extra) :]
    place, code = place_and_code()
    rows = slots[0].shape[1]
    tokens = (GROUP + extra) * rows
    scale = 1.0 / math.sqrt(HS)
    to_log2 = scale * math.log2(math.e)
    totals_ref[...] = jnp.zeros_like(totals_ref)

    def rows_of(slot):
        block = lax.bitwise_xor(place, slot) if slot < GROUP else slot
        return pl.ds(pl.multiple_of(block * rows, rows), rows)

    @pl.when(head_at(code, place) >= 0)
    def _():
        group_start = lax.div(lax.axis_index("seq"), GROUP) * (GROUP * rows)
        bounds = clip_bounds(lengths_ref, clip_count)
        for slot in range(GROUP + extra):
            where = rows_of(slot)
            for part in range(6):
                data[part, where, :] = slots[slot][part]
            for turn, part in enumerate((1, 2, 5)):
                turned[turn, :, where] = slots[slot][part].T
        key_place = group_start + lax.broadcasted_iota(jnp.int32, (tokens, HS), 0)
        query_place = group_start + lax.broadcasted_iota(jnp.int32, (1, tokens), 1)
        key_ids = jnp.zeros((tokens, HS), jnp.int32)
        query_ids = jnp.zeros((1, tokens), jnp.int32)
        query_first = jnp.zeros((1, tokens), jnp.int32)
        for bound in bounds:
            key_ids = key_ids + (key_place >= bound).astype(jnp.int32)
            query_ids = query_ids + (query_place >= bound).astype(jnp.int32)
            query_first = jnp.where(query_place >= bound, bound, query_first)
        ids_ref[...] = key_ids
        owned = (query_first >= group_start) & (query_first < group_start + GROUP * rows)
        grads[1] = jnp.zeros((tokens, HS), F32)
        grads[2] = jnp.zeros((tokens, HS), F32)
        clip_iota = lax.broadcasted_iota(jnp.int32, (totals_ref.shape[0], 1), 0)

        def attend(part, turn, mine, keys, allowed):
            scores = lax.dot_general(
                data[part + 1, keys, :], data[part, mine, :], ROWS_BY_ROWS, preferred_element_type=F32
            )
            scores = jnp.where(allowed, scores, -jnp.inf)
            peak = jnp.max(scores, axis=0, keepdims=True)
            exponent = jnp.exp2((scores - peak) * to_log2)
            inverse = 1.0 / jnp.sum(exponent, axis=0, keepdims=True)
            weights = exponent.astype(BF16)
            out = jnp.dot(turned[turn, :, keys], weights, preferred_element_type=F32) * inverse
            return out, exponent, weights, inverse

        for first in range(0, tokens, QUERY_TILE):
            width = min(QUERY_TILE, tokens - first)
            mine = slice(first, first + width)
            keys = slice(max(0, first - MOST), min(tokens, first + width + MOST))
            key_tile = ids_ref[keys, :]
            key_tile = jnp.concatenate([key_tile] * (width // HS), axis=1)
            allowed = key_tile == query_ids[:, mine]
            target, _, _, _ = attend(3, 2, mine, keys, allowed)
            student, exponent, weights, inverse = attend(0, 1, mine, keys, allowed)
            diff = student - target
            if extra:
                diff = jnp.where(owned[:, mine], diff, 0.0)
                target = jnp.where(owned[:, mine], target, 0.0)
            squares = jnp.sum(diff * diff, axis=0, keepdims=True)
            counted = jnp.where(clip_iota == query_ids[:, mine], squares, 0.0)
            totals_ref[...] += jnp.sum(counted, axis=1, keepdims=True)
            gradient = (diff * inverse).astype(BF16)
            delta = jnp.sum(gradient.astype(F32) * student, axis=0, keepdims=True)
            slope = jnp.dot(data[2, keys, :], gradient, preferred_element_type=F32)
            dscores = (exponent * (slope - delta)).astype(BF16)
            dquery = jnp.dot(turned[0, :, keys], dscores, preferred_element_type=F32)
            grads[0, mine, :] = (dquery * scale).T
            grads[1, keys, :] += jnp.dot(dscores, data[0, mine, :], preferred_element_type=F32)
            grads[2, keys, :] += lax.dot_general(
                weights, gradient, ROWS_BY_ROWS, preferred_element_type=F32
            )
            grads[3, mine, :] = target.T
        for slot in range(GROUP + extra):
            where = rows_of(slot)
            outs[slot][0] = grads[0, where, :].astype(BF16)
            outs[slot][1] = (grads[1, where, :] * scale).astype(BF16)
            outs[slot][2] = grads[2, where, :].astype(BF16)
            outs[slot][3] = grads[3, where, :].astype(BF16)


def finish_kernel(clip_count, head_count, extra, lengths_ref, totals_ref, *refs):
    slots, extras, (grads_ref, target_ref) = refs[:GROUP], refs[GROUP:-2], refs[-2:]
    place, code = place_and_code()
    rows = slots[0].shape[1]
    first = lax.axis_index("seq") * rows
    token = first + lax.broadcasted_iota(jnp.int32, (rows, HS), 0)
    factor = jnp.zeros((rows, HS), F32)
    begin = jnp.int32(0)
    for clip in range(clip_count):
        length = lengths_ref[clip]
        size = length.astype(F32) * (H * HS)
        value = lax.rsqrt(totals_ref[clip : clip + 1, :] / size + EPS)
        factor = jnp.where((token >= begin) & (token < begin + length), value, factor)
        begin = begin + length
    for k in range(GROUP):
        head = head_at(code, lax.bitwise_xor(place, k))

        @pl.when(head >= 0)
        def _():
            cols = columns_of(head)
            for part in range(3):
                grads_ref[part, :, cols] = (slots[k][part].astype(F32) * factor).astype(BF16)
            target_ref[:, cols] = slots[k][3]

    for head in range(head_count if extra else 0):
        cols = slice(head * HS, (head + 1) * HS)
        for part in range(3):
            more = (extras[head][part].astype(F32) * factor).astype(BF16)
            grads_ref[part, :, cols] = grads_ref[part, :, cols] + more
        target_ref[:, cols] = target_ref[:, cols] + extras[head][3]


def both_axes(sec_count, seq_count, pairs_of):
    pairs = []
    for sec in range(sec_count):
        for start in range(0, seq_count, GROUP):
            for source, target in pairs_of(OWNERS[sec % 2], start):
                if source < seq_count and target < seq_count:
                    pairs.append((sec * seq_count + source, sec * seq_count + target))
    return pairs


def per_device(sec_count, seq_count, student_qkv, target_qkv, clip_lengths):
    rows, _, width = student_qkv.shape
    head_count = width // HS
    clip_count = clip_lengths.shape[0]
    total_rows = -(-clip_count // 8) * 8
    extra = MOST // rows if seq_count > GROUP else 0
    axes = ("sec", "seq")
    pairs = functools.partial(both_axes, sec_count, seq_count)
    params = pltpu.CompilerParams(vmem_limit_bytes=VMEM_BYTES)

    packed = pl.pallas_call(
        pack_kernel,
        out_shape=[jax.ShapeDtypeStruct((6, rows, HS), BF16)] * GROUP,
        in_specs=[VMEM] * 2,
        out_specs=[VMEM] * GROUP,
        compiler_params=params,
        name="pack",
    )(jnp.transpose(student_qkv, (1, 0, 2)), jnp.transpose(target_qkv, (1, 0, 2)))

    gathered = [packed[0]] + [None] * (GROUP - 1)
    for k in ROUNDS:
        gathered[k] = lax.ppermute(
            packed[k], axes, pairs(lambda owners, start: [(start + (d ^ k), start + d) for d in owners])
        )
    for block in range(extra):
        pieces = []
        for head in range(head_count):
            cols = slice(head * HS, (head + 1) * HS)
            piece = jnp.concatenate([student_qkv[:, :, cols], target_qkv[:, :, cols]], axis=1)
            pieces.append(
                lax.ppermute(
                    jnp.transpose(piece, (1, 0, 2)),
                    axes,
                    pairs(lambda owners, start: [(start + GROUP + block, start + owners[head])]),
                )
            )
        gathered.append(sum(pieces[1:], pieces[0]))

    tokens = (GROUP + extra) * rows
    *results, totals = pl.pallas_call(
        functools.partial(head_kernel, clip_count, extra),
        out_shape=[jax.ShapeDtypeStruct((4, rows, HS), BF16)] * (GROUP + extra)
        + [jax.ShapeDtypeStruct((total_rows, HS), F32)],
        in_specs=[SMEM] + [VMEM] * (GROUP + extra),
        out_specs=[VMEM] * (GROUP + extra + 1),
        scratch_shapes=[
            pltpu.VMEM((6, tokens, HS), BF16),
            pltpu.VMEM((3, HS, tokens), BF16),
            pltpu.VMEM((tokens, HS), jnp.int32),
            pltpu.VMEM((4, tokens, HS), F32),
        ],
        compiler_params=params,
        name="heads",
    )(clip_lengths, *gathered)

    returned = [results[0]] + [None] * (GROUP - 1)
    for k in ROUNDS:
        returned[k] = lax.ppermute(
            results[k], axes, pairs(lambda owners, start: [(start + d, start + (d ^ k)) for d in owners])
        )
    extras = []
    for head in range(head_count if extra else 0):
        pieces = [
            lax.ppermute(
                results[GROUP + block],
                axes,
                pairs(lambda owners, start: [(start + owners[head], start + GROUP + block)]),
            )
            for block in range(extra)
        ]
        extras.append(sum(pieces[1:], pieces[0]))
    for axis, count in (("sec", sec_count), ("seq", seq_count)):
        step = 1
        while step < count:
            totals = totals + lax.ppermute(totals, axis, [(s, s ^ step) for s in range(count)])
            step *= 2

    grads, target_out = pl.pallas_call(
        functools.partial(finish_kernel, clip_count, head_count, extra),
        out_shape=[
            jax.ShapeDtypeStruct((3, rows, width), BF16),
            jax.ShapeDtypeStruct((rows, width), BF16),
        ],
        in_specs=[SMEM] + [VMEM] * (1 + GROUP + len(extras)),
        out_specs=[VMEM] * 2,
        compiler_params=params,
        name="finish",
    )(clip_lengths, totals, *returned, *extras)
    return jnp.transpose(grads, (1, 0, 2)), target_out


def solution(mesh):
    return jax.shard_map(
        functools.partial(per_device, mesh.shape["sec"], mesh.shape["seq"]),
        mesh=mesh,
        in_specs=(P("seq", None, "sec"), P("seq", None, "sec"), P()),
        out_specs=(P("seq", None, "sec"), P("seq", "sec")),
        check_vma=False,
    )
```

time: 269 us -> 89.7 us (0.33)
  the two profiles are of different devices: /device:TPU:18 before, /device:TPU:10 now
where the time goes in v1:
time: 89.7 us; the launch traced here: 89.2 us
  starting transfers between devices  46.9 us (52%)
  waiting for transfers between devices  29.3 us (33%)
  Pallas kernels  9.98 us (11%)
  local copies, waits for them, and re-layouts  2.06 us (2%)
    ppermute x7, starting transfers between devices, per_device(): lax.ppermute(packed[k], axes, pairs(lambda owners, start: [(start + (d ^...  21.6 us
    ppermute x7, starting transfers between devices, per_device(): lax.ppermute(results[k], axes, pairs(lambda owners, start: [(start + d, s...  18 us
    ppermute x7, waiting for transfers between devices, per_device(): lax.ppermute(packed[k], axes, pairs(lambda owners, start: [(start + (d ^...  11.9 us
    ppermute x5, waiting for transfers between devices, per_device(): lax.ppermute(totals, axis, [(s, s ^ step) for s in range(count)])  9.57 us
    pallas_call x1, Pallas kernels, per_device(): pl.pallas_call(functools.partial(head_kernel, clip_count, extra), out_sha...  8.2 us
    ppermute x7, waiting for transfers between devices, per_device(): lax.ppermute(results[k], axes, pairs(lambda owners, start: [(start + d, s...  7.79 us
    ppermute x5, starting transfers between devices, per_device(): lax.ppermute(totals, axis, [(s, s ^ step) for s in range(count)])  7.32 us
    unnamed x6, local copies, waits for them, and re-layouts  2.06 us
  transfers between devices with their start and end apart: 19, of which 10 were waited for; matrix products, arithmetic and copies ran while one was open for 0% of the time, Pallas kernels for 0%

profile of v1, /device:TPU:10, one launch (start us, length us, event | category | flops | bytes accessed | tf_op | source)
XLA Modules:
  0.0 89.2 jit_solution(11034710191093611480)
XLA Ops:
  2.9 1.3 %collective-permute-start = (bf16[6,128,128]{2,1,0:T(8,128)(2,1)S(1)}, bf16[6,128,128]{2,1,0:T(8,128)(2,1)S(1)}, u32[]{:S(2)}, u32[]{:S(2)}) collective-permute-start(bf16[6,128,128]{2,1,0:T(8,128)(2,1)S(1)} %get-tuple-element.22), channel_id=1, source_target_pairs={{1,0},{3,2},{5,4},{4,5},{6,7},{8,9},{11,10},{10,11},{12,13},{15,14... | collective-permute-start | bytes 589832 | tf_op jit(solution)/shard_map/ppermute | solution.py:217
  4.2 2.4 %collective-permute-start.1 = (bf16[6,128,128]{2,1,0:T(8,128)(2,1)S(1)}, bf16[6,128,128]{2,1,0:T(8,128)(2,1)S(1)}, u32[]{:S(2)}, u32[]{:S(2)}) collective-permute-start(bf16[6,128,128]{2,1,0:T(8,128)(2,1)S(1)} %get-tuple-element.23), channel_id=1, source_target_pairs={{2,0},{0,2},{6,4},{7,5},{5,7},{11,9},{8,10},{9,11},{15,13},{12,14}... | collective-permute-start | bytes 589832 | tf_op jit(solution)/shard_map/ppermute | solution.py:217
  6.6 1.3 %collective-permute-start.2 = (bf16[6,128,128]{2,1,0:T(8,128)(2,1)S(1)}, bf16[6,128,128]{2,1,0:T(8,128)(2,1)S(1)}, u32[]{:S(2)}, u32[]{:S(2)}) collective-permute-start(bf16[6,128,128]{2,1,0:T(8,128)(2,1)S(1)} %get-tuple-element.24), channel_id=1, source_target_pairs={{3,0},{1,2},{7,4},{6,5},{4,7},{10,9},{9,10},{8,11},{14,13},{13,14}... | collective-permute-start | bytes 589832 | tf_op jit(solution)/shard_map/ppermute | solution.py:217
  9.2 7.5 %collective-permute-start.4 = (bf16[6,128,128]{2,1,0:T(8,128)(2,1)S(1)}, bf16[6,128,128]{2,1,0:T(8,128)(2,1)S(1)}, u32[]{:S(2)}, u32[]{:S(2)}) collective-permute-start(bf16[6,128,128]{2,1,0:T(8,128)(2,1)S(1)} %get-tuple-element.26), channel_id=1, source_target_pairs={{5,0},{7,2},{1,4},{0,5},{2,7},{12,9},{15,10},{14,11},{8,13},{11,14... | collective-permute-start | bytes 589832 | tf_op jit(solution)/shard_map/ppermute | solution.py:217
  16.7 2.1 %collective-permute-start.5 = (bf16[6,128,128]{2,1,0:T(8,128)(2,1)S(1)}, bf16[6,128,128]{2,1,0:T(8,128)(2,1)S(1)}, u32[]{:S(2)}, u32[]{:S(2)}) collective-permute-start(bf16[6,128,128]{2,1,0:T(8,128)(2,1)S(1)} %get-tuple-element.27), channel_id=1, source_target_pairs={{6,0},{4,2},{2,4},{3,5},{1,7},{15,9},{12,10},{13,11},{11,13},{8,14... | collective-permute-start | bytes 589832 | tf_op jit(solution)/shard_map/ppermute | solution.py:217
  18.9 5.7 %collective-permute-start.6 = (bf16[6,128,128]{2,1,0:T(8,128)(2,1)S(1)}, bf16[6,128,128]{2,1,0:T(8,128)(2,1)S(1)}, u32[]{:S(2)}, u32[]{:S(2)}) collective-permute-start(bf16[6,128,128]{2,1,0:T(8,128)(2,1)S(1)} %get-tuple-element.28), channel_id=1, source_target_pairs={{7,0},{5,2},{3,4},{2,5},{0,7},{14,9},{13,10},{12,11},{10,13},{9,14... | collective-permute-start | bytes 589832 | tf_op jit(solution)/shard_map/ppermute | solution.py:217
  24.7 7.6 %collective-permute-done.4.refs_5_ = bf16[6,128,128]{2,1,0:T(8,128)(2,1)S(1)} collective-permute-done((bf16[6,128,128]{2,1,0:T(8,128)(2,1)S(1)}, bf16[6,128,128]{2,1,0:T(8,128)(2,1)S(1)}, u32[]{:S(2)}, u32[]{:S(2)}) %collective-permute-start.4) | collective-permute-done | bytes 196640 | tf_op jit(solution)/shard_map/ppermute | solution.py:217
  32.3 3.2 %collective-permute-done.5.refs_6_ = bf16[6,128,128]{2,1,0:T(8,128)(2,1)S(1)} collective-permute-done((bf16[6,128,128]{2,1,0:T(8,128)(2,1)S(1)}, bf16[6,128,128]{2,1,0:T(8,128)(2,1)S(1)}, u32[]{:S(2)}, u32[]{:S(2)}) %collective-permute-start.5) | collective-permute-done | bytes 196640 | tf_op jit(solution)/shard_map/ppermute | solution.py:217
  36.6 8.2 %heads.1 = (bf16[4,128,128]{2,1,0:T(8,128)(2,1)S(1)}, bf16[4,128,128]{2,1,0:T(8,128)(2,1)S(1)}, bf16[4,128,128]{2,1,0:T(8,128)(2,1)S(1)}, bf16[4,128,128]{2,1,0:...) custom-call(s32[4]{0:T(128)S(1)} %copy-done.2, ...), custom_call_target="tpu_custom_call" | custom-call | tf_op jit(solution)/shard_map/heads/pallas_call | solution.py:235
  44.8 1.3 %collective-permute-start.12 = (bf16[4,128,128]{2,1,0:T(8,128)(2,1)S(1)}, bf16[4,128,128]{2,1,0:T(8,128)(2,1)S(1)}, u32[]{:S(2)}, u32[]{:S(2)}) collective-permute-start(bf16[4,128,128]{2,1,0:T(8,128)(2,1)S(1)} %get-tuple-element.31), channel_id=1, source_target_pairs={{0,1},{2,3},{4,5},{5,4},{7,6},{9,8},{10,11},{11,10},{13,12},{14,15... | collective-permute-start | bytes 393224 | tf_op jit(solution)/shard_map/ppermute | solution.py:253
  46.1 1.9 %collective-permute-start.13 = (bf16[4,128,128]{2,1,0:T(8,128)(2,1)S(1)}, bf16[4,128,128]{2,1,0:T(8,128)(2,1)S(1)}, u32[]{:S(2)}, u32[]{:S(2)}) collective-permute-start(bf16[4,128,128]{2,1,0:T(8,128)(2,1)S(1)} %get-tuple-element.32), channel_id=1, source_target_pairs={{0,2},{2,0},{4,6},{5,7},{7,5},{9,11},{10,8},{11,9},{13,15},{14,12}... | collective-permute-start | bytes 393224 | tf_op jit(solution)/shard_map/ppermute | solution.py:253
  48.0 2.4 %collective-permute-start.7 = (f32[8,128]{1,0:T(8,128)S(1)}, f32[8,128]{1,0:T(8,128)S(1)}, u32[]{:S(2)}, u32[]{:S(2)}) collective-permute-start(f32[8,128]{1,0:T(8,128)S(1)} %get-tuple-element.29), channel_id=1, source_target_pairs={{0,8},{8,0},{16,24},{24,16},{1,9},{9,1},{17,25},{25,17},{2,10},{10... | collective-permute-start | bytes 12296 | tf_op jit(solution)/shard_map/ppermute | solution.py:270
  51.8 3.1 %collective-permute-done.8 = f32[8,128]{1,0:T(8,128)S(1)} collective-permute-done((f32[8,128]{1,0:T(8,128)S(1)}, f32[8,128]{1,0:T(8,128)S(1)}, u32[]{:S(2)}, u32[]{:S(2)}) %collective-permute-start.8) | collective-permute-done | bytes 4128 | tf_op jit(solution)/shard_map/ppermute | solution.py:270
  55.8 2.7 %collective-permute-done.9 = f32[8,128]{1,0:T(8,128)S(1)} collective-permute-done((f32[8,128]{1,0:T(8,128)S(1)}, f32[8,128]{1,0:T(8,128)S(1)}, u32[]{:S(2)}, u32[]{:S(2)}) %collective-permute-start.9) | collective-permute-done | bytes 4128 | tf_op jit(solution)/shard_map/ppermute | solution.py:270
  59.1 3.0 %collective-permute-done.10 = f32[8,128]{1,0:T(8,128)S(1)} collective-permute-done((f32[8,128]{1,0:T(8,128)S(1)}, f32[8,128]{1,0:T(8,128)S(1)}, u32[]{:S(2)}, u32[]{:S(2)}) %collective-permute-start.10) | collective-permute-done | bytes 4128 | tf_op jit(solution)/shard_map/ppermute | solution.py:270
  62.1 2.8 %collective-permute-start.11 = (f32[8,128]{1,0:T(8,128)S(1)}, f32[8,128]{1,0:T(8,128)S(1)}, u32[]{:S(2)}, u32[]{:S(2)}) collective-permute-start(f32[8,128]{1,0:T(8,128)S(1)} %add.18), channel_id=1, source_target_pairs={{0,4},{1,5},{2,6},{3,7},{4,0},{5,1},{6,2},{7,3},{8,12},{9,13},{10,... | collective-permute-start | bytes 12296 | tf_op jit(solution)/shard_map/ppermute | solution.py:270
  64.9 3.4 %collective-permute-start.14 = (bf16[4,128,128]{2,1,0:T(8,128)(2,1)S(1)}, bf16[4,128,128]{2,1,0:T(8,128)(2,1)S(1)}, u32[]{:S(2)}, u32[]{:S(2)}) collective-permute-start(bf16[4,128,128]{2,1,0:T(8,128)(2,1)S(1)} %get-tuple-element.33), channel_id=1, source_target_pairs={{0,3},{2,1},{4,7},{5,6},{7,4},{9,10},{10,9},{11,8},{13,14},{14,13}... | collective-permute-start | bytes 393224 | tf_op jit(solution)/shard_map/ppermute | solution.py:253
  68.3 1.3 %collective-permute-start.15 = (bf16[4,128,128]{2,1,0:T(8,128)(2,1)S(1)}, bf16[4,128,128]{2,1,0:T(8,128)(2,1)S(1)}, u32[]{:S(2)}, u32[]{:S(2)}) collective-permute-start(bf16[4,128,128]{2,1,0:T(8,128)(2,1)S(1)} %get-tuple-element.34), channel_id=1, source_target_pairs={{0,4},{2,6},{4,0},{5,1},{7,3},{9,13},{10,14},{11,15},{13,9},{14,10... | collective-permute-start | bytes 393224 | tf_op jit(solution)/shard_map/ppermute | solution.py:253
  69.6 4.8 %collective-permute-start.16 = (bf16[4,128,128]{2,1,0:T(8,128)(2,1)S(1)}, bf16[4,128,128]{2,1,0:T(8,128)(2,1)S(1)}, u32[]{:S(2)}, u32[]{:S(2)}) collective-permute-start(bf16[4,128,128]{2,1,0:T(8,128)(2,1)S(1)} %get-tuple-element.35), channel_id=1, source_target_pairs={{0,5},{2,7},{4,1},{5,0},{7,2},{9,12},{10,15},{11,14},{13,8},{14,11... | collective-permute-start | bytes 393224 | tf_op jit(solution)/shard_map/ppermute | solution.py:253
  74.4 2.5 %collective-permute-start.17 = (bf16[4,128,128]{2,1,0:T(8,128)(2,1)S(1)}, bf16[4,128,128]{2,1,0:T(8,128)(2,1)S(1)}, u32[]{:S(2)}, u32[]{:S(2)}) collective-permute-start(bf16[4,128,128]{2,1,0:T(8,128)(2,1)S(1)} %get-tuple-element.36), channel_id=1, source_target_pairs={{0,6},{2,4},{4,2},{5,3},{7,1},{9,15},{10,12},{11,13},{13,11},{14,8... | collective-permute-start | bytes 393224 | tf_op jit(solution)/shard_map/ppermute | solution.py:253
  76.9 2.8 %collective-permute-start.18 = (bf16[4,128,128]{2,1,0:T(8,128)(2,1)S(1)}, bf16[4,128,128]{2,1,0:T(8,128)(2,1)S(1)}, u32[]{:S(2)}, u32[]{:S(2)}) collective-permute-start(bf16[4,128,128]{2,1,0:T(8,128)(2,1)S(1)} %get-tuple-element.37), channel_id=1, source_target_pairs={{0,7},{2,5},{4,3},{5,2},{7,0},{9,14},{10,13},{11,12},{13,10},{14,9... | collective-permute-start | bytes 393224 | tf_op jit(solution)/shard_map/ppermute | solution.py:253
  80.5 2.9 %collective-permute-done.17.refs_6_ = bf16[4,128,128]{2,1,0:T(8,128)(2,1)S(1)} collective-permute-done((bf16[4,128,128]{2,1,0:T(8,128)(2,1)S(1)}, bf16[4,128,128]{2,1,0:T(8,128)(2,1)S(1)}, u32[]{:S(2)}, u32[]{:S(2)}) %collective-permute-start.17) | collective-permute-done | bytes 131104 | tf_op jit(solution)/shard_map/ppermute | solution.py:253
  83.4 4.2 %collective-permute-done.18.refs_7_ = bf16[4,128,128]{2,1,0:T(8,128)(2,1)S(1)} collective-permute-done((bf16[4,128,128]{2,1,0:T(8,128)(2,1)S(1)}, bf16[4,128,128]{2,1,0:T(8,128)(2,1)S(1)}, u32[]{:S(2)}, u32[]{:S(2)}) %collective-permute-start.18) | collective-permute-done | bytes 131104 | tf_op jit(solution)/shard_map/ppermute | solution.py:253
  87.6 1.6 %finish.1 = (bf16[3,128,640]{2,1,0:T(8,128)(2,1)}, bf16[128,640]{1,0:T(8,128)(2,1)}) custom-call(s32[4]{0:T(128)S(1)} %copy-done.2, f32[8,128]{1,0:T(8,128)S(1)} %add.19.totals_ref, bf16[4,128,128]{2,1,0:T(8,128)(2,1)S(1)} %get-tuple-element.30.refs_0_, bf16[4,128,128]{2,1,0:T(8,128)(2,1)S(1)} %collective-permute-done.12.refs_1_, ...), custom_call_target="tpu_custom_call" | custom-call | tf_op jit(solution)/shard_map/finish/pallas_call | solution.py:273
  (28 shorter events, 8.3 us)
Async XLA Ops:
  0.6 1.0 %copy-start = (bf16[128,3,640]{2,0,1:T(8,128)(2,1)S(1)}, bf16[128,3,640]{2,0,1:T(8,128)(2,1)}, u32[]{:S(2)}) copy-start(bf16[128,3,640]{2,0,1:T(8,128)(2,1)} %param.3) | copy-start | bytes 1474564
  1.7 1.0 %copy-start.1 = (bf16[128,3,640]{2,0,1:T(8,128)(2,1)S(1)}, bf16[128,3,640]{2,0,1:T(8,128)(2,1)}, u32[]{:S(2)}) copy-start(bf16[128,3,640]{2,0,1:T(8,128)(2,1)} %param.4) | copy-start | bytes 1474564
  2.9 13.8 %collective-permute-start = (bf16[6,128,128]{2,1,0:T(8,128)(2,1)S(1)}, bf16[6,128,128]{2,1,0:T(8,128)(2,1)S(1)}, u32[]{:S(2)}, u32[]{:S(2)}) collective-permute-start(bf16[6,128,128]{2,1,0:T(8,128)(2,1)S(1)} %get-tuple-element.22), channel_id=1, source_target_pairs={{1,0},{3,2},{5,4},{4,5},{6,7},{8,9},{11,10},{10,11},{12,13},{15,14... | collective-permute-start | bytes 589832 | tf_op jit(solution)/shard_map/ppermute | solution.py:217
  4.2 14.7 %collective-permute-start.1 = (bf16[6,128,128]{2,1,0:T(8,128)(2,1)S(1)}, bf16[6,128,128]{2,1,0:T(8,128)(2,1)S(1)}, u32[]{:S(2)}, u32[]{:S(2)}) collective-permute-start(bf16[6,128,128]{2,1,0:T(8,128)(2,1)S(1)} %get-tuple-element.23), channel_id=1, source_target_pairs={{2,0},{0,2},{6,4},{7,5},{5,7},{11,9},{8,10},{9,11},{15,13},{12,14}... | collective-permute-start | bytes 589832 | tf_op jit(solution)/shard_map/ppermute | solution.py:217
  6.6 18.1 %collective-permute-start.2 = (bf16[6,128,128]{2,1,0:T(8,128)(2,1)S(1)}, bf16[6,128,128]{2,1,0:T(8,128)(2,1)S(1)}, u32[]{:S(2)}, u32[]{:S(2)}) collective-permute-start(bf16[6,128,128]{2,1,0:T(8,128)(2,1)S(1)} %get-tuple-element.24), channel_id=1, source_target_pairs={{3,0},{1,2},{7,4},{6,5},{4,7},{10,9},{9,10},{8,11},{14,13},{13,14}... | collective-permute-start | bytes 589832 | tf_op jit(solution)/shard_map/ppermute | solution.py:217
  7.9 16.8 %collective-permute-start.3 = (bf16[6,128,128]{2,1,0:T(8,128)(2,1)S(1)}, bf16[6,128,128]{2,1,0:T(8,128)(2,1)S(1)}, u32[]{:S(2)}, u32[]{:S(2)}) collective-permute-start(bf16[6,128,128]{2,1,0:T(8,128)(2,1)S(1)} %get-tuple-element.25), channel_id=1, source_target_pairs={{4,0},{6,2},{0,4},{1,5},{3,7},{13,9},{14,10},{15,11},{9,13},{10,14... | collective-permute-start | bytes 589832 | tf_op jit(solution)/shard_map/ppermute | solution.py:217
  9.2 23.1 %collective-permute-start.4 = (bf16[6,128,128]{2,1,0:T(8,128)(2,1)S(1)}, bf16[6,128,128]{2,1,0:T(8,128)(2,1)S(1)}, u32[]{:S(2)}, u32[]{:S(2)}) collective-permute-start(bf16[6,128,128]{2,1,0:T(8,128)(2,1)S(1)} %get-tuple-element.26), channel_id=1, source_target_pairs={{5,0},{7,2},{1,4},{0,5},{2,7},{12,9},{15,10},{14,11},{8,13},{11,14... | collective-permute-start | bytes 589832 | tf_op jit(solution)/shard_map/ppermute | solution.py:217
  16.7 18.7 %collective-permute-start.5 = (bf16[6,128,128]{2,1,0:T(8,128)(2,1)S(1)}, bf16[6,128,128]{2,1,0:T(8,128)(2,1)S(1)}, u32[]{:S(2)}, u32[]{:S(2)}) collective-permute-start(bf16[6,128,128]{2,1,0:T(8,128)(2,1)S(1)} %get-tuple-element.27), channel_id=1, source_target_pairs={{6,0},{4,2},{2,4},{3,5},{1,7},{15,9},{12,10},{13,11},{11,13},{8,14... | collective-permute-start | bytes 589832 | tf_op jit(solution)/shard_map/ppermute | solution.py:217
  18.9 17.7 %copy-start.2 = (s32[4]{0:T(128)S(1)}, s32[4]{0:T(128)}, u32[]{:S(2)}) copy-start(s32[4]{0:T(128)} %lengths_ref.3) | copy-start | bytes 52
  18.9 17.7 %collective-permute-start.6 = (bf16[6,128,128]{2,1,0:T(8,128)(2,1)S(1)}, bf16[6,128,128]{2,1,0:T(8,128)(2,1)S(1)}, u32[]{:S(2)}, u32[]{:S(2)}) collective-permute-start(bf16[6,128,128]{2,1,0:T(8,128)(2,1)S(1)} %get-tuple-element.28), channel_id=1, source_target_pairs={{7,0},{5,2},{3,4},{2,5},{0,7},{14,9},{13,10},{12,11},{10,13},{9,14... | collective-permute-start | bytes 589832 | tf_op jit(solution)/shard_map/ppermute | solution.py:217
  44.8 29.7 %collective-permute-start.12 = (bf16[4,128,128]{2,1,0:T(8,128)(2,1)S(1)}, bf16[4,128,128]{2,1,0:T(8,128)(2,1)S(1)}, u32[]{:S(2)}, u32[]{:S(2)}) collective-permute-start(bf16[4,128,128]{2,1,0:T(8,128)(2,1)S(1)} %get-tuple-element.31), channel_id=1, source_target_pairs={{0,1},{2,3},{4,5},{5,4},{7,6},{9,8},{10,11},{11,10},{13,12},{14,15... | collective-permute-start | bytes 393224 | tf_op jit(solution)/shard_map/ppermute | solution.py:253
  46.1 30.9 %collective-permute-start.13 = (bf16[4,128,128]{2,1,0:T(8,128)(2,1)S(1)}, bf16[4,128,128]{2,1,0:T(8,128)(2,1)S(1)}, u32[]{:S(2)}, u32[]{:S(2)}) collective-permute-start(bf16[4,128,128]{2,1,0:T(8,128)(2,1)S(1)} %get-tuple-element.32), channel_id=1, source_target_pairs={{0,2},{2,0},{4,6},{5,7},{7,5},{9,11},{10,8},{11,9},{13,15},{14,12}... | collective-permute-start | bytes 393224 | tf_op jit(solution)/shard_map/ppermute | solution.py:253
  48.0 3.3 %collective-permute-start.7 = (f32[8,128]{1,0:T(8,128)S(1)}, f32[8,128]{1,0:T(8,128)S(1)}, u32[]{:S(2)}, u32[]{:S(2)}) collective-permute-start(f32[8,128]{1,0:T(8,128)S(1)} %get-tuple-element.29), channel_id=1, source_target_pairs={{0,8},{8,0},{16,24},{24,16},{1,9},{9,1},{17,25},{25,17},{2,10},{10... | collective-permute-start | bytes 12296 | tf_op jit(solution)/shard_map/ppermute | solution.py:270
  51.3 3.6 %collective-permute-start.8 = (f32[8,128]{1,0:T(8,128)S(1)}, f32[8,128]{1,0:T(8,128)S(1)}, u32[]{:S(2)}, u32[]{:S(2)}) collective-permute-start(f32[8,128]{1,0:T(8,128)S(1)} %add.15), channel_id=1, source_target_pairs={{0,16},{8,24},{16,0},{24,8},{1,17},{9,25},{17,1},{25,9},{2,18},{10... | collective-permute-start | bytes 12296 | tf_op jit(solution)/shard_map/ppermute | solution.py:270
  54.9 3.6 %collective-permute-start.9 = (f32[8,128]{1,0:T(8,128)S(1)}, f32[8,128]{1,0:T(8,128)S(1)}, u32[]{:S(2)}, u32[]{:S(2)}) collective-permute-start(f32[8,128]{1,0:T(8,128)S(1)} %add.16), channel_id=1, source_target_pairs={{0,1},{1,0},{2,3},{3,2},{4,5},{5,4},{6,7},{7,6},{8,9},{9,8},{10,11... | collective-permute-start | bytes 12296 | tf_op jit(solution)/shard_map/ppermute | solution.py:270
  58.5 3.6 %collective-permute-start.10 = (f32[8,128]{1,0:T(8,128)S(1)}, f32[8,128]{1,0:T(8,128)S(1)}, u32[]{:S(2)}, u32[]{:S(2)}) collective-permute-start(f32[8,128]{1,0:T(8,128)S(1)} %add.17), channel_id=1, source_target_pairs={{0,2},{1,3},{2,0},{3,1},{4,6},{5,7},{6,4},{7,5},{8,10},{9,11},{10,... | collective-permute-start | bytes 12296 | tf_op jit(solution)/shard_map/ppermute | solution.py:270
  62.1 7.5 %collective-permute-start.11 = (f32[8,128]{1,0:T(8,128)S(1)}, f32[8,128]{1,0:T(8,128)S(1)}, u32[]{:S(2)}, u32[]{:S(2)}) collective-permute-start(f32[8,128]{1,0:T(8,128)S(1)} %add.18), channel_id=1, source_target_pairs={{0,4},{1,5},{2,6},{3,7},{4,0},{5,1},{6,2},{7,3},{8,12},{9,13},{10,... | collective-permute-start | bytes 12296 | tf_op jit(solution)/shard_map/ppermute | solution.py:270
  64.9 14.9 %collective-permute-start.14 = (bf16[4,128,128]{2,1,0:T(8,128)(2,1)S(1)}, bf16[4,128,128]{2,1,0:T(8,128)(2,1)S(1)}, u32[]{:S(2)}, u32[]{:S(2)}) collective-permute-start(bf16[4,128,128]{2,1,0:T(8,128)(2,1)S(1)} %get-tuple-element.33), channel_id=1, source_target_pairs={{0,3},{2,1},{4,7},{5,6},{7,4},{9,10},{10,9},{11,8},{13,14},{14,13}... | collective-permute-start | bytes 393224 | tf_op jit(solution)/shard_map/ppermute | solution.py:253
  68.3 11.5 %collective-permute-start.15 = (bf16[4,128,128]{2,1,0:T(8,128)(2,1)S(1)}, bf16[4,128,128]{2,1,0:T(8,128)(2,1)S(1)}, u32[]{:S(2)}, u32[]{:S(2)}) collective-permute-start(bf16[4,128,128]{2,1,0:T(8,128)(2,1)S(1)} %get-tuple-element.34), channel_id=1, source_target_pairs={{0,4},{2,6},{4,0},{5,1},{7,3},{9,13},{10,14},{11,15},{13,9},{14,10... | collective-permute-start | bytes 393224 | tf_op jit(solution)/shard_map/ppermute | solution.py:253
  69.6 10.9 %collective-permute-start.16 = (bf16[4,128,128]{2,1,0:T(8,128)(2,1)S(1)}, bf16[4,128,128]{2,1,0:T(8,128)(2,1)S(1)}, u32[]{:S(2)}, u32[]{:S(2)}) collective-permute-start(bf16[4,128,128]{2,1,0:T(8,128)(2,1)S(1)} %get-tuple-element.35), channel_id=1, source_target_pairs={{0,5},{2,7},{4,1},{5,0},{7,2},{9,12},{10,15},{11,14},{13,8},{14,11... | collective-permute-start | bytes 393224 | tf_op jit(solution)/shard_map/ppermute | solution.py:253
  74.4 8.9 %collective-permute-start.17 = (bf16[4,128,128]{2,1,0:T(8,128)(2,1)S(1)}, bf16[4,128,128]{2,1,0:T(8,128)(2,1)S(1)}, u32[]{:S(2)}, u32[]{:S(2)}) collective-permute-start(bf16[4,128,128]{2,1,0:T(8,128)(2,1)S(1)} %get-tuple-element.36), channel_id=1, source_target_pairs={{0,6},{2,4},{4,2},{5,3},{7,1},{9,15},{10,12},{11,13},{13,11},{14,8... | collective-permute-start | bytes 393224 | tf_op jit(solution)/shard_map/ppermute | solution.py:253
  76.9 10.6 %collective-permute-start.18 = (bf16[4,128,128]{2,1,0:T(8,128)(2,1)S(1)}, bf16[4,128,128]{2,1,0:T(8,128)(2,1)S(1)}, u32[]{:S(2)}, u32[]{:S(2)}) collective-permute-start(bf16[4,128,128]{2,1,0:T(8,128)(2,1)S(1)} %get-tuple-element.37), channel_id=1, source_target_pairs={{0,7},{2,5},{4,3},{5,2},{7,0},{9,14},{10,13},{11,12},{13,10},{14,9... | collective-permute-start | bytes 393224 | tf_op jit(solution)/shard_map/ppermute | solution.py:253

commit v2 on v1

--- a/solution.py
+++ b/solution.py
@@ -15,9 +15,11 @@
 
 GROUP = 8
 OWNERS = ((0, 2, 4, 5, 7), (1, 2, 3, 5, 6))
-ROUNDS = (4, 1, 5, 2, 6, 3, 7)
+ROUNDS_IN = (4, 3, 5, 1, 7, 6, 2)
+ROUNDS_OUT = (4, 3, 5, 7, 6, 2, 1)
 QUERY_TILE = 256
-VMEM_BYTES = 48 * 1024 * 1024
+HEADS_VMEM = 40 * 1024 * 1024
+SMALL_VMEM = 8 * 1024 * 1024
 
 BF16 = jnp.bfloat16
 F32 = jnp.float32
@@ -45,15 +47,30 @@
     return pl.ds(pl.multiple_of(head * HS, HS), HS)
 
 
-def pack_kernel(student_ref, target_ref, *slots):
+def pack_kernel(student_ref, target_ref, *refs):
+    slots, sems = in_slot_order(refs, ROUNDS_IN), refs[GROUP]
     place, code = place_and_code()
-    for k in range(GROUP):
-        head = head_at(code, lax.bitwise_xor(place, k))
-
-        @pl.when(head >= 0)
-        def _():
-            slots[k][:3] = student_ref[:, :, columns_of(head)]
-            slots[k][3:] = target_ref[:, :, columns_of(head)]
+
+    def copies(k, head):
+        return [
+            pltpu.make_async_copy(
+                view.at[:, :, columns_of(head)], slots[k].at[pl.ds(3 * i, 3)], sems.at[k, i]
+            )
+            for i, view in enumerate((student_ref, target_ref))
+        ]
+
+    for step in ("start", "wait"):
+        for k in ROUNDS_IN + (0,):
+            head = head_at(code, lax.bitwise_xor(place, k))
+
+            @pl.when(head >= 0)
+            def _():
+                for copy in copies(k, head):
+                    copy.start() if step == "start" else copy.wait()
+
+
+def in_slot_order(refs, rounds):
+    return [refs[((0,) + rounds).index(k)] for k in range(GROUP)]
 
 
 def clip_bounds(lengths_ref, count):
@@ -65,15 +82,18 @@
 
 
 def head_kernel(clip_count, extra, lengths_ref, *refs):
-    slots = refs[: GROUP + extra]
-    outs = refs[GROUP + extra : 2 * (GROUP + extra)]
-    totals_ref, data, turned, ids_ref, grads = refs[2 * (GROUP + extra) :]
+    slots = in_slot_order(refs, ROUNDS_IN) + list(refs[GROUP : GROUP + extra])
+    refs = refs[GROUP + extra :]
+    outs = in_slot_order(refs, ROUNDS_OUT) + list(refs[GROUP : GROUP + extra])
+    data, turned, ids_ref, grads, totals_ref = refs[GROUP + extra :]
     place, code = place_and_code()
     rows = slots[0].shape[1]
     tokens = (GROUP + extra) * rows
     scale = 1.0 / math.sqrt(HS)
     to_log2 = scale * math.log2(math.e)
     totals_ref[...] = jnp.zeros_like(totals_ref)
+    clip_rows = totals_ref.shape[0]
+    outs[0][4 * rows :] = jnp.zeros((2 * clip_rows, HS), BF16)
 
     def rows_of(slot):
         block = lax.bitwise_xor(place, slot) if slot < GROUP else slot
@@ -143,18 +163,34 @@
                 weights, gradient, ROWS_BY_ROWS, preferred_element_type=F32
             )
             grads[3, mine, :] = target.T
+        high = totals_ref[...].astype(BF16)
+        low = (totals_ref[...] - high.astype(F32)).astype(BF16)
         for slot in range(GROUP + extra):
             where = rows_of(slot)
-            outs[slot][0] = grads[0, where, :].astype(BF16)
-            outs[slot][1] = (grads[1, where, :] * scale).astype(BF16)
-            outs[slot][2] = grads[2, where, :].astype(BF16)
-            outs[slot][3] = grads[3, where, :].astype(BF16)
-
-
-def finish_kernel(clip_count, head_count, extra, lengths_ref, totals_ref, *refs):
-    slots, extras, (grads_ref, target_ref) = refs[:GROUP], refs[GROUP:-2], refs[-2:]
+            for part, factor in enumerate((1.0, scale, 1.0, 1.0)):
+                block = grads[part, where, :]
+                block = block if factor == 1.0 else block * factor
+                outs[slot][part * rows : (part + 1) * rows] = block.astype(BF16)
+            outs[slot][4 * rows : 4 * rows + clip_rows] = high
+            outs[slot][4 * rows + clip_rows :] = low
+
+
+def sum_kernel(*refs):
+    out = refs[-1]
+    clip_rows = out.shape[0]
+    total = jnp.zeros(out.shape, F32)
+    for slot in refs[:-1]:
+        start = slot.shape[0] - 2 * clip_rows
+        total = total + slot[start : start + clip_rows].astype(F32)
+        total = total + slot[start + clip_rows :].astype(F32)
+    out[...] = total
+
+
+def finish_kernel(clip_count, head_count, extra, lengths_ref, mine_ref, other_ref, *refs):
+    slots, extras, (grads_ref, target_ref) = in_slot_order(refs, ROUNDS_OUT), refs[GROUP:-2], refs[-2:]
     place, code = place_and_code()
-    rows = slots[0].shape[1]
+    rows = target_ref.shape[0]
+    totals = mine_ref[...] + other_ref[...]
     first = lax.axis_index("seq") * rows
     token = first + lax.broadcasted_iota(jnp.int32, (rows, HS), 0)
     factor = jnp.zeros((rows, HS), F32)
@@ -162,7 +198,7 @@
     for clip in range(clip_count):
         length = lengths_ref[clip]
         size = length.astype(F32) * (H * HS)
-        value = lax.rsqrt(totals_ref[clip : clip + 1, :] / size + EPS)
+        value = lax.rsqrt(totals[clip : clip + 1, :] / size + EPS)
         factor = jnp.where((token >= begin) & (token < begin + length), value, factor)
         begin = begin + length
     for k in range(GROUP):
@@ -172,15 +208,17 @@
         def _():
             cols = columns_of(head)
             for part in range(3):
-                grads_ref[part, :, cols] = (slots[k][part].astype(F32) * factor).astype(BF16)
-            target_ref[:, cols] = slots[k][3]
+                block = slots[k][part * rows : (part + 1) * rows].astype(F32)
+                grads_ref[part, :, cols] = (block * factor).astype(BF16)
+            target_ref[:, cols] = slots[k][3 * rows : 4 * rows]
 
     for head in range(head_count if extra else 0):
         cols = slice(head * HS, (head + 1) * HS)
         for part in range(3):
-            more = (extras[head][part].astype(F32) * factor).astype(BF16)
+            more = extras[head][part * rows : (part + 1) * rows].astype(F32)
+            more = (more * factor).astype(BF16)
             grads_ref[part, :, cols] = grads_ref[part, :, cols] + more
-        target_ref[:, cols] = target_ref[:, cols] + extras[head][3]
+        target_ref[:, cols] = target_ref[:, cols] + extras[head][3 * rows : 4 * rows]
 
 
 def both_axes(sec_count, seq_count, pairs_of):
@@ -197,25 +235,28 @@
     rows, _, width = student_qkv.shape
     head_count = width // HS
     clip_count = clip_lengths.shape[0]
-    total_rows = -(-clip_count // 8) * 8
+    clip_rows = -(-clip_count // 8) * 8
     extra = MOST // rows if seq_count > GROUP else 0
     axes = ("sec", "seq")
     pairs = functools.partial(both_axes, sec_count, seq_count)
-    params = pltpu.CompilerParams(vmem_limit_bytes=VMEM_BYTES)
+    small = pltpu.CompilerParams(vmem_limit_bytes=SMALL_VMEM)
 
     packed = pl.pallas_call(
         pack_kernel,
         out_shape=[jax.ShapeDtypeStruct((6, rows, HS), BF16)] * GROUP,
-        in_specs=[VMEM] * 2,
+        in_specs=[pl.BlockSpec(memory_space=pltpu.HBM)] * 2,
         out_specs=[VMEM] * GROUP,
-        compiler_params=params,
+        scratch_shapes=[pltpu.SemaphoreType.DMA((GROUP, 2))],
+        compiler_params=small,
         name="pack",
     )(jnp.transpose(student_qkv, (1, 0, 2)), jnp.transpose(target_qkv, (1, 0, 2)))
 
-    gathered = [packed[0]] + [None] * (GROUP - 1)
-    for k in ROUNDS:
-        gathered[k] = lax.ppermute(
-            packed[k], axes, pairs(lambda owners, start: [(start + (d ^ k), start + d) for d in owners])
+    gathered = [packed[0]]
+    for k, mine in zip(ROUNDS_IN, packed[1:]):
+        gathered.append(
+            lax.ppermute(
+                mine, axes, pairs(lambda owners, start: [(start + (d ^ k), start + d) for d in owners])
+            )
         )
     for block in range(extra):
         pieces = []
@@ -232,26 +273,29 @@
         gathered.append(sum(pieces[1:], pieces[0]))
 
     tokens = (GROUP + extra) * rows
-    *results, totals = pl.pallas_call(
+    payload = jax.ShapeDtypeStruct((4 * rows + 2 * clip_rows, HS), BF16)
+    results = pl.pallas_call(
         functools.partial(head_kernel, clip_count, extra),
-        out_shape=[jax.ShapeDtypeStruct((4, rows, HS), BF16)] * (GROUP + extra)
-        + [jax.ShapeDtypeStruct((total_rows, HS), F32)],
+        out_shape=[payload] * (GROUP + extra),
         in_specs=[SMEM] + [VMEM] * (GROUP + extra),
-        out_specs=[VMEM] * (GROUP + extra + 1),
+        out_specs=[VMEM] * (GROUP + extra),
         scratch_shapes=[
             pltpu.VMEM((6, tokens, HS), BF16),
             pltpu.VMEM((3, HS, tokens), BF16),
             pltpu.VMEM((tokens, HS), jnp.int32),
             pltpu.VMEM((4, tokens, HS), F32),
+            pltpu.VMEM((clip_rows, HS), F32),
         ],
-        compiler_params=params,
+        compiler_params=pltpu.CompilerParams(vmem_limit_bytes=HEADS_VMEM),
         name="heads",
     )(clip_lengths, *gathered)
 
-    returned = [results[0]] + [None] * (GROUP - 1)
-    for k in ROUNDS:
-        returned[k] = lax.ppermute(
-            results[k], axes, pairs(lambda owners, start: [(start + d, start + (d ^ k)) for d in owners])
+    returned = [results[0]]
+    for k, mine in zip(ROUNDS_OUT, results[1:]):
+        returned.append(
+            lax.ppermute(
+                mine, axes, pairs(lambda owners, start: [(start + d, start + (d ^ k)) for d in owners])
+            )
         )
     extras = []
     for head in range(head_count if extra else 0):
@@ -264,11 +308,26 @@
             for block in range(extra)
         ]
         extras.append(sum(pieces[1:], pieces[0]))
-    for axis, count in (("sec", sec_count), ("seq", seq_count)):
-        step = 1
-        while step < count:
-            totals = totals + lax.ppermute(totals, axis, [(s, s ^ step) for s in range(count)])
-            step *= 2
+    totals = pl.pallas_call(
+        sum_kernel,
+        out_shape=jax.ShapeDtypeStruct((clip_rows, HS), F32),
+        in_specs=[VMEM] * GROUP,
+        out_specs=VMEM,
+        compiler_params=small,
+        name="totals",
+    )(*returned)
+
+    def over(totals, axis, count, step):
+        return lax.ppermute(totals, axis, [(s, s ^ step) for s in range(count)])
+
+    step = GROUP
+    while step < seq_count:
+        totals = totals + over(totals, "seq", seq_count, step)
+        step *= 2
+    step = 1
+    while 2 * step < sec_count:
+        totals = totals + over(totals, "sec", sec_count, step)
+        step *= 2
 
     grads, target_out = pl.pallas_call(
         functools.partial(finish_kernel, clip_count, head_count, extra),
@@ -276,11 +335,11 @@
             jax.ShapeDtypeStruct((3, rows, width), BF16),
             jax.ShapeDtypeStruct((rows, width), BF16),
         ],
-        in_specs=[SMEM] + [VMEM] * (1 + GROUP + len(extras)),
+        in_specs=[SMEM] + [VMEM] * (2 + GROUP + len(extras)),
         out_specs=[VMEM] * 2,
-        compiler_params=params,
+        compiler_params=small,
         name="finish",
-    )(clip_lengths, totals, *returned, *extras)
+    )(clip_lengths, totals, over(totals, "sec", sec_count, step), *returned, *extras)
     return jnp.transpose(grads, (1, 0, 2)), target_out
 
 

time: 89.7 us -> 69.2 us (0.77)
  the two profiles are of different devices: /device:TPU:10 before, /device:TPU:18 now
where the time goes in v2:
time: 69.2 us; the launch traced here: 68.7 us
  starting transfers between devices  37 us (53%)
  waiting for transfers between devices  18.6 us (27%)
  Pallas kernels  10.2 us (15%)
  local copies, waits for them, and re-layouts  2.06 us (3%)
  between operations  0.84 us (1%)
    ppermute x7, starting transfers between devices, per_device(): lax.ppermute(mine, axes, pairs(lambda owners, start: [(start + d, start +...  18.6 us
    ppermute x7, starting transfers between devices, per_device(): lax.ppermute(mine, axes, pairs(lambda owners, start: [(start + (d ^ k), s...  18 us
    ppermute x7, waiting for transfers between devices, per_device(): lax.ppermute(mine, axes, pairs(lambda owners, start: [(start + (d ^ k), s...  9.87 us
    pallas_call x1, Pallas kernels, per_device(): pl.pallas_call(functools.partial(head_kernel, clip_count, extra), out_sha...  8.19 us
    ppermute x2, waiting for transfers between devices, over(): return lax.ppermute(totals, axis, [(s, s ^ step) for s in range(count)])  4.39 us
    ppermute x7, waiting for transfers between devices, per_device(): lax.ppermute(mine, axes, pairs(lambda owners, start: [(start + d, start +...  4.34 us
    unnamed x6, local copies, waits for them, and re-layouts  2.06 us
    pallas_call x1, Pallas kernels, per_device(): pl.pallas_call(functools.partial(finish_kernel, clip_count, head_count, e...  1.57 us
  transfers between devices with their start and end apart: 16, of which 7 were waited for; matrix products, arithmetic and copies ran while one was open for 0% of the time, Pallas kernels for 0%

profile of v2, /device:TPU:18, one launch (start us, length us, event | category | flops | bytes accessed | tf_op | source)
XLA Modules:
  0.0 68.7 jit_solution(21086962593515827)
XLA Ops:
  1.7 1.0 %copy-done.1 = bf16[128,3,640]{2,0,1:T(8,128)(2,1)S(1)} copy-done((bf16[128,3,640]{2,0,1:T(8,128)(2,1)S(1)}, bf16[128,3,640]{2,0,1:T(8,128)(2,1)}, u32[]{:S(2)}) %copy-start.1) | copy-done | bytes 491544
  3.1 2.2 %collective-permute-start = (bf16[6,128,128]{2,1,0:T(8,128)(2,1)S(1)}, bf16[6,128,128]{2,1,0:T(8,128)(2,1)S(1)}, u32[]{:S(2)}, u32[]{:S(2)}) collective-permute-start(bf16[6,128,128]{2,1,0:T(8,128)(2,1)S(1)} %get-tuple-element.21), channel_id=1, source_target_pairs={{4,0},{6,2},{0,4},{1,5},{3,7},{13,9},{14,10},{15,11},{9,13},{10,14... | collective-permute-start | bytes 589832 | tf_op jit(solution)/shard_map/ppermute | solution.py:257
  5.3 3.5 %collective-permute-start.1 = (bf16[6,128,128]{2,1,0:T(8,128)(2,1)S(1)}, bf16[6,128,128]{2,1,0:T(8,128)(2,1)S(1)}, u32[]{:S(2)}, u32[]{:S(2)}) collective-permute-start(bf16[6,128,128]{2,1,0:T(8,128)(2,1)S(1)} %get-tuple-element.22), channel_id=1, source_target_pairs={{3,0},{1,2},{7,4},{6,5},{4,7},{10,9},{9,10},{8,11},{14,13},{13,14}... | collective-permute-start | bytes 589832 | tf_op jit(solution)/shard_map/ppermute | solution.py:257
  8.8 1.3 %collective-permute-start.2 = (bf16[6,128,128]{2,1,0:T(8,128)(2,1)S(1)}, bf16[6,128,128]{2,1,0:T(8,128)(2,1)S(1)}, u32[]{:S(2)}, u32[]{:S(2)}) collective-permute-start(bf16[6,128,128]{2,1,0:T(8,128)(2,1)S(1)} %get-tuple-element.23), channel_id=1, source_target_pairs={{5,0},{7,2},{1,4},{0,5},{2,7},{12,9},{15,10},{14,11},{8,13},{11,14... | collective-permute-start | bytes 589832 | tf_op jit(solution)/shard_map/ppermute | solution.py:257
  10.1 4.4 %collective-permute-start.3 = (bf16[6,128,128]{2,1,0:T(8,128)(2,1)S(1)}, bf16[6,128,128]{2,1,0:T(8,128)(2,1)S(1)}, u32[]{:S(2)}, u32[]{:S(2)}) collective-permute-start(bf16[6,128,128]{2,1,0:T(8,128)(2,1)S(1)} %get-tuple-element.24), channel_id=1, source_target_pairs={{1,0},{3,2},{5,4},{4,5},{6,7},{8,9},{11,10},{10,11},{12,13},{15,14... | collective-permute-start | bytes 589832 | tf_op jit(solution)/shard_map/ppermute | solution.py:257
  14.5 1.3 %collective-permute-start.4 = (bf16[6,128,128]{2,1,0:T(8,128)(2,1)S(1)}, bf16[6,128,128]{2,1,0:T(8,128)(2,1)S(1)}, u32[]{:S(2)}, u32[]{:S(2)}) collective-permute-start(bf16[6,128,128]{2,1,0:T(8,128)(2,1)S(1)} %get-tuple-element.25), channel_id=1, source_target_pairs={{7,0},{5,2},{3,4},{2,5},{0,7},{14,9},{13,10},{12,11},{10,13},{9,14... | collective-permute-start | bytes 589832 | tf_op jit(solution)/shard_map/ppermute | solution.py:257
  15.8 4.0 %collective-permute-start.5 = (bf16[6,128,128]{2,1,0:T(8,128)(2,1)S(1)}, bf16[6,128,128]{2,1,0:T(8,128)(2,1)S(1)}, u32[]{:S(2)}, u32[]{:S(2)}) collective-permute-start(bf16[6,128,128]{2,1,0:T(8,128)(2,1)S(1)} %get-tuple-element.26), channel_id=1, source_target_pairs={{6,0},{4,2},{2,4},{3,5},{1,7},{15,9},{12,10},{13,11},{11,13},{8,14... | collective-permute-start | bytes 589832 | tf_op jit(solution)/shard_map/ppermute | solution.py:257
  19.9 1.3 %collective-permute-start.6 = (bf16[6,128,128]{2,1,0:T(8,128)(2,1)S(1)}, bf16[6,128,128]{2,1,0:T(8,128)(2,1)S(1)}, u32[]{:S(2)}, u32[]{:S(2)}) collective-permute-start(bf16[6,128,128]{2,1,0:T(8,128)(2,1)S(1)} %get-tuple-element.27), channel_id=1, source_target_pairs={{2,0},{0,2},{6,4},{7,5},{5,7},{11,9},{8,10},{9,11},{15,13},{12,14}... | collective-permute-start | bytes 589832 | tf_op jit(solution)/shard_map/ppermute | solution.py:257
  21.2 2.6 %collective-permute-done.2.refs_3_ = bf16[6,128,128]{2,1,0:T(8,128)(2,1)S(1)} collective-permute-done((bf16[6,128,128]{2,1,0:T(8,128)(2,1)S(1)}, bf16[6,128,128]{2,1,0:T(8,128)(2,1)S(1)}, u32[]{:S(2)}, u32[]{:S(2)}) %collective-permute-start.2) | collective-permute-done | bytes 196640 | tf_op jit(solution)/shard_map/ppermute | solution.py:257
  23.8 6.1 %collective-permute-done.4.refs_5_ = bf16[6,128,128]{2,1,0:T(8,128)(2,1)S(1)} collective-permute-done((bf16[6,128,128]{2,1,0:T(8,128)(2,1)S(1)}, bf16[6,128,128]{2,1,0:T(8,128)(2,1)S(1)}, u32[]{:S(2)}, u32[]{:S(2)}) %collective-permute-start.4) | collective-permute-done | bytes 196640 | tf_op jit(solution)/shard_map/ppermute | solution.py:257
  29.9 1.1 %collective-permute-done.5.refs_6_ = bf16[6,128,128]{2,1,0:T(8,128)(2,1)S(1)} collective-permute-done((bf16[6,128,128]{2,1,0:T(8,128)(2,1)S(1)}, bf16[6,128,128]{2,1,0:T(8,128)(2,1)S(1)}, u32[]{:S(2)}, u32[]{:S(2)}) %collective-permute-start.5) | collective-permute-done | bytes 196640 | tf_op jit(solution)/shard_map/ppermute | solution.py:257
  31.0 8.2 %heads.1 = (bf16[528,128]{1,0:T(8,128)(2,1)S(1)}, bf16[528,128]{1,0:T(8,128)(2,1)S(1)}, bf16[528,128]{1,0:T(8,128)(2,1)S(1)}, bf16[528,128]{1,0:T(8,128)(2,1)S(1...) custom-call(s32[4]{0:T(128)S(1)} %copy-done.2, ...), custom_call_target="tpu_custom_call" | custom-call | tf_op jit(solution)/shard_map/heads/pallas_call | solution.py:277
  39.2 1.9 %collective-permute-start.7 = (bf16[528,128]{1,0:T(8,128)(2,1)S(1)}, bf16[528,128]{1,0:T(8,128)(2,1)S(1)}, u32[]{:S(2)}, u32[]{:S(2)}) collective-permute-start(bf16[528,128]{1,0:T(8,128)(2,1)S(1)} %get-tuple-element.29), channel_id=1, source_target_pairs={{0,4},{2,6},{4,0},{5,1},{7,3},{9,13},{10,14},{11,15},{13,9},{14,10... | collective-permute-start | bytes 405512 | tf_op jit(solution)/shard_map/ppermute | solution.py:296
  41.2 1.9 %collective-permute-start.8 = (bf16[528,128]{1,0:T(8,128)(2,1)S(1)}, bf16[528,128]{1,0:T(8,128)(2,1)S(1)}, u32[]{:S(2)}, u32[]{:S(2)}) collective-permute-start(bf16[528,128]{1,0:T(8,128)(2,1)S(1)} %get-tuple-element.30), channel_id=1, source_target_pairs={{0,3},{2,1},{4,7},{5,6},{7,4},{9,10},{10,9},{11,8},{13,14},{14,13}... | collective-permute-start | bytes 405512 | tf_op jit(solution)/shard_map/ppermute | solution.py:296
  43.1 1.3 %collective-permute-start.9 = (bf16[528,128]{1,0:T(8,128)(2,1)S(1)}, bf16[528,128]{1,0:T(8,128)(2,1)S(1)}, u32[]{:S(2)}, u32[]{:S(2)}) collective-permute-start(bf16[528,128]{1,0:T(8,128)(2,1)S(1)} %get-tuple-element.31), channel_id=1, source_target_pairs={{0,5},{2,7},{4,1},{5,0},{7,2},{9,12},{10,15},{11,14},{13,8},{14,11... | collective-permute-start | bytes 405512 | tf_op jit(solution)/shard_map/ppermute | solution.py:296
  44.4 1.3 %collective-permute-start.10 = (bf16[528,128]{1,0:T(8,128)(2,1)S(1)}, bf16[528,128]{1,0:T(8,128)(2,1)S(1)}, u32[]{:S(2)}, u32[]{:S(2)}) collective-permute-start(bf16[528,128]{1,0:T(8,128)(2,1)S(1)} %get-tuple-element.32), channel_id=1, source_target_pairs={{0,7},{2,5},{4,3},{5,2},{7,0},{9,14},{10,13},{11,12},{13,10},{14,9... | collective-permute-start | bytes 405512 | tf_op jit(solution)/shard_map/ppermute | solution.py:296
  45.7 8.3 %collective-permute-start.11 = (bf16[528,128]{1,0:T(8,128)(2,1)S(1)}, bf16[528,128]{1,0:T(8,128)(2,1)S(1)}, u32[]{:S(2)}, u32[]{:S(2)}) collective-permute-start(bf16[528,128]{1,0:T(8,128)(2,1)S(1)} %get-tuple-element.33), channel_id=1, source_target_pairs={{0,6},{2,4},{4,2},{5,3},{7,1},{9,15},{10,12},{11,13},{13,11},{14,8... | collective-permute-start | bytes 405512 | tf_op jit(solution)/shard_map/ppermute | solution.py:296
  54.1 1.3 %collective-permute-start.12 = (bf16[528,128]{1,0:T(8,128)(2,1)S(1)}, bf16[528,128]{1,0:T(8,128)(2,1)S(1)}, u32[]{:S(2)}, u32[]{:S(2)}) collective-permute-start(bf16[528,128]{1,0:T(8,128)(2,1)S(1)} %get-tuple-element.34), channel_id=1, source_target_pairs={{0,2},{2,0},{4,6},{5,7},{7,5},{9,11},{10,8},{11,9},{13,15},{14,12}... | collective-permute-start | bytes 405512 | tf_op jit(solution)/shard_map/ppermute | solution.py:296
  55.4 2.5 %collective-permute-start.13 = (bf16[528,128]{1,0:T(8,128)(2,1)S(1)}, bf16[528,128]{1,0:T(8,128)(2,1)S(1)}, u32[]{:S(2)}, u32[]{:S(2)}) collective-permute-start(bf16[528,128]{1,0:T(8,128)(2,1)S(1)} %get-tuple-element.35), channel_id=1, source_target_pairs={{0,1},{2,3},{4,5},{5,4},{7,6},{9,8},{10,11},{11,10},{13,12},{14,15... | collective-permute-start | bytes 405512 | tf_op jit(solution)/shard_map/ppermute | solution.py:296
  57.9 2.9 %collective-permute-done.11.refs_5_ = bf16[528,128]{1,0:T(8,128)(2,1)S(1)} collective-permute-done((bf16[528,128]{1,0:T(8,128)(2,1)S(1)}, bf16[528,128]{1,0:T(8,128)(2,1)S(1)}, u32[]{:S(2)}, u32[]{:S(2)}) %collective-permute-start.11) | collective-permute-done | bytes 135200 | tf_op jit(solution)/shard_map/ppermute | solution.py:296
  60.9 1.4 %collective-permute-done.13.refs_7_ = bf16[528,128]{1,0:T(8,128)(2,1)S(1)} collective-permute-done((bf16[528,128]{1,0:T(8,128)(2,1)S(1)}, bf16[528,128]{1,0:T(8,128)(2,1)S(1)}, u32[]{:S(2)}, u32[]{:S(2)}) %collective-permute-start.13) | collective-permute-done | bytes 135200 | tf_op jit(solution)/shard_map/ppermute | solution.py:296
  62.4 1.2 %collective-permute-done.14 = f32[8,128]{1,0:T(8,128)S(1)} collective-permute-done((f32[8,128]{1,0:T(8,128)S(1)}, f32[8,128]{1,0:T(8,128)S(1)}, u32[]{:S(2)}, u32[]{:S(2)}) %collective-permute-start.14) | collective-permute-done | bytes 4128 | tf_op jit(solution)/shard_map/ppermute | solution.py:321
  63.9 3.2 %collective-permute-done.15.other_ref = f32[8,128]{1,0:T(8,128)S(1)} collective-permute-done((f32[8,128]{1,0:T(8,128)S(1)}, f32[8,128]{1,0:T(8,128)S(1)}, u32[]{:S(2)}, u32[]{:S(2)}) %collective-permute-start.15) | collective-permute-done | bytes 4128 | tf_op jit(solution)/shard_map/ppermute | solution.py:321
  67.1 1.6 %finish.1 = (bf16[3,128,640]{2,1,0:T(8,128)(2,1)}, bf16[128,640]{1,0:T(8,128)(2,1)}) custom-call(s32[4]{0:T(128)S(1)} %copy-done.2, f32[8,128]{1,0:T(8,128)S(1)} %add.3.mine_ref, f32[8,128]{1,0:T(8,128)S(1)} %collective-permute-done.15.other_ref, bf16[528,128]{1,0:T(8,128)(2,1)S(1)} %get-tuple-element.28.refs_0_, ...), custom_call_target="tpu_custom_call" | custom-call | tf_op jit(solution)/shard_map/finish/pallas_call | solution.py:332
  (19 shorter events, 1.9 us)
Async XLA Ops:
  0.6 1.0 %copy-start = (bf16[128,3,640]{2,0,1:T(8,128)(2,1)S(1)}, bf16[128,3,640]{2,0,1:T(8,128)(2,1)}, u32[]{:S(2)}) copy-start(bf16[128,3,640]{2,0,1:T(8,128)(2,1)} %param.3) | copy-start | bytes 1474564
  1.7 1.0 %copy-start.1 = (bf16[128,3,640]{2,0,1:T(8,128)(2,1)S(1)}, bf16[128,3,640]{2,0,1:T(8,128)(2,1)}, u32[]{:S(2)}) copy-start(bf16[128,3,640]{2,0,1:T(8,128)(2,1)} %param.4) | copy-start | bytes 1474564
  3.1 12.7 %collective-permute-start = (bf16[6,128,128]{2,1,0:T(8,128)(2,1)S(1)}, bf16[6,128,128]{2,1,0:T(8,128)(2,1)S(1)}, u32[]{:S(2)}, u32[]{:S(2)}) collective-permute-start(bf16[6,128,128]{2,1,0:T(8,128)(2,1)S(1)} %get-tuple-element.21), channel_id=1, source_target_pairs={{4,0},{6,2},{0,4},{1,5},{3,7},{13,9},{14,10},{15,11},{9,13},{10,14... | collective-permute-start | bytes 589832 | tf_op jit(solution)/shard_map/ppermute | solution.py:257
  5.3 14.5 %collective-permute-start.1 = (bf16[6,128,128]{2,1,0:T(8,128)(2,1)S(1)}, bf16[6,128,128]{2,1,0:T(8,128)(2,1)S(1)}, u32[]{:S(2)}, u32[]{:S(2)}) collective-permute-start(bf16[6,128,128]{2,1,0:T(8,128)(2,1)S(1)} %get-tuple-element.22), channel_id=1, source_target_pairs={{3,0},{1,2},{7,4},{6,5},{4,7},{10,9},{9,10},{8,11},{14,13},{13,14}... | collective-permute-start | bytes 589832 | tf_op jit(solution)/shard_map/ppermute | solution.py:257
  8.8 15.0 %collective-permute-start.2 = (bf16[6,128,128]{2,1,0:T(8,128)(2,1)S(1)}, bf16[6,128,128]{2,1,0:T(8,128)(2,1)S(1)}, u32[]{:S(2)}, u32[]{:S(2)}) collective-permute-start(bf16[6,128,128]{2,1,0:T(8,128)(2,1)S(1)} %get-tuple-element.23), channel_id=1, source_target_pairs={{5,0},{7,2},{1,4},{0,5},{2,7},{12,9},{15,10},{14,11},{8,13},{11,14... | collective-permute-start | bytes 589832 | tf_op jit(solution)/shard_map/ppermute | solution.py:257
  10.1 13.7 %collective-permute-start.3 = (bf16[6,128,128]{2,1,0:T(8,128)(2,1)S(1)}, bf16[6,128,128]{2,1,0:T(8,128)(2,1)S(1)}, u32[]{:S(2)}, u32[]{:S(2)}) collective-permute-start(bf16[6,128,128]{2,1,0:T(8,128)(2,1)S(1)} %get-tuple-element.24), channel_id=1, source_target_pairs={{1,0},{3,2},{5,4},{4,5},{6,7},{8,9},{11,10},{10,11},{12,13},{15,14... | collective-permute-start | bytes 589832 | tf_op jit(solution)/shard_map/ppermute | solution.py:257
  14.5 15.4 %collective-permute-start.4 = (bf16[6,128,128]{2,1,0:T(8,128)(2,1)S(1)}, bf16[6,128,128]{2,1,0:T(8,128)(2,1)S(1)}, u32[]{:S(2)}, u32[]{:S(2)}) collective-permute-start(bf16[6,128,128]{2,1,0:T(8,128)(2,1)S(1)} %get-tuple-element.25), channel_id=1, source_target_pairs={{7,0},{5,2},{3,4},{2,5},{0,7},{14,9},{13,10},{12,11},{10,13},{9,14... | collective-permute-start | bytes 589832 | tf_op jit(solution)/shard_map/ppermute | solution.py:257
  15.8 15.2 %collective-permute-start.5 = (bf16[6,128,128]{2,1,0:T(8,128)(2,1)S(1)}, bf16[6,128,128]{2,1,0:T(8,128)(2,1)S(1)}, u32[]{:S(2)}, u32[]{:S(2)}) collective-permute-start(bf16[6,128,128]{2,1,0:T(8,128)(2,1)S(1)} %get-tuple-element.26), channel_id=1, source_target_pairs={{6,0},{4,2},{2,4},{3,5},{1,7},{15,9},{12,10},{13,11},{11,13},{8,14... | collective-permute-start | bytes 589832 | tf_op jit(solution)/shard_map/ppermute | solution.py:257
  19.8 11.2 %copy-start.2 = (s32[4]{0:T(128)S(1)}, s32[4]{0:T(128)}, u32[]{:S(2)}) copy-start(s32[4]{0:T(128)} %lengths_ref.3) | copy-start | bytes 52
  19.9 11.2 %collective-permute-start.6 = (bf16[6,128,128]{2,1,0:T(8,128)(2,1)S(1)}, bf16[6,128,128]{2,1,0:T(8,128)(2,1)S(1)}, u32[]{:S(2)}, u32[]{:S(2)}) collective-permute-start(bf16[6,128,128]{2,1,0:T(8,128)(2,1)S(1)} %get-tuple-element.27), channel_id=1, source_target_pairs={{2,0},{0,2},{6,4},{7,5},{5,7},{11,9},{8,10},{9,11},{15,13},{12,14}... | collective-permute-start | bytes 589832 | tf_op jit(solution)/shard_map/ppermute | solution.py:257
  39.2 14.8 %collective-permute-start.7 = (bf16[528,128]{1,0:T(8,128)(2,1)S(1)}, bf16[528,128]{1,0:T(8,128)(2,1)S(1)}, u32[]{:S(2)}, u32[]{:S(2)}) collective-permute-start(bf16[528,128]{1,0:T(8,128)(2,1)S(1)} %get-tuple-element.29), channel_id=1, source_target_pairs={{0,4},{2,6},{4,0},{5,1},{7,3},{9,13},{10,14},{11,15},{13,9},{14,10... | collective-permute-start | bytes 405512 | tf_op jit(solution)/shard_map/ppermute | solution.py:296
  41.2 14.2 %collective-permute-start.8 = (bf16[528,128]{1,0:T(8,128)(2,1)S(1)}, bf16[528,128]{1,0:T(8,128)(2,1)S(1)}, u32[]{:S(2)}, u32[]{:S(2)}) collective-permute-start(bf16[528,128]{1,0:T(8,128)(2,1)S(1)} %get-tuple-element.30), channel_id=1, source_target_pairs={{0,3},{2,1},{4,7},{5,6},{7,4},{9,10},{10,9},{11,8},{13,14},{14,13}... | collective-permute-start | bytes 405512 | tf_op jit(solution)/shard_map/ppermute | solution.py:296
  43.1 14.8 %collective-permute-start.9 = (bf16[528,128]{1,0:T(8,128)(2,1)S(1)}, bf16[528,128]{1,0:T(8,128)(2,1)S(1)}, u32[]{:S(2)}, u32[]{:S(2)}) collective-permute-start(bf16[528,128]{1,0:T(8,128)(2,1)S(1)} %get-tuple-element.31), channel_id=1, source_target_pairs={{0,5},{2,7},{4,1},{5,0},{7,2},{9,12},{10,15},{11,14},{13,8},{14,11... | collective-permute-start | bytes 405512 | tf_op jit(solution)/shard_map/ppermute | solution.py:296
  44.4 13.5 %collective-permute-start.10 = (bf16[528,128]{1,0:T(8,128)(2,1)S(1)}, bf16[528,128]{1,0:T(8,128)(2,1)S(1)}, u32[]{:S(2)}, u32[]{:S(2)}) collective-permute-start(bf16[528,128]{1,0:T(8,128)(2,1)S(1)} %get-tuple-element.32), channel_id=1, source_target_pairs={{0,7},{2,5},{4,3},{5,2},{7,0},{9,14},{10,13},{11,12},{13,10},{14,9... | collective-permute-start | bytes 405512 | tf_op jit(solution)/shard_map/ppermute | solution.py:296
  45.7 15.2 %collective-permute-start.11 = (bf16[528,128]{1,0:T(8,128)(2,1)S(1)}, bf16[528,128]{1,0:T(8,128)(2,1)S(1)}, u32[]{:S(2)}, u32[]{:S(2)}) collective-permute-start(bf16[528,128]{1,0:T(8,128)(2,1)S(1)} %get-tuple-element.33), channel_id=1, source_target_pairs={{0,6},{2,4},{4,2},{5,3},{7,1},{9,15},{10,12},{11,13},{13,11},{14,8... | collective-permute-start | bytes 405512 | tf_op jit(solution)/shard_map/ppermute | solution.py:296
  54.1 6.8 %collective-permute-start.12 = (bf16[528,128]{1,0:T(8,128)(2,1)S(1)}, bf16[528,128]{1,0:T(8,128)(2,1)S(1)}, u32[]{:S(2)}, u32[]{:S(2)}) collective-permute-start(bf16[528,128]{1,0:T(8,128)(2,1)S(1)} %get-tuple-element.34), channel_id=1, source_target_pairs={{0,2},{2,0},{4,6},{5,7},{7,5},{9,11},{10,8},{11,9},{13,15},{14,12}... | collective-permute-start | bytes 405512 | tf_op jit(solution)/shard_map/ppermute | solution.py:296
  55.4 6.9 %collective-permute-start.13 = (bf16[528,128]{1,0:T(8,128)(2,1)S(1)}, bf16[528,128]{1,0:T(8,128)(2,1)S(1)}, u32[]{:S(2)}, u32[]{:S(2)}) collective-permute-start(bf16[528,128]{1,0:T(8,128)(2,1)S(1)} %get-tuple-element.35), channel_id=1, source_target_pairs={{0,1},{2,3},{4,5},{5,4},{7,6},{9,8},{10,11},{11,10},{13,12},{14,15... | collective-permute-start | bytes 405512 | tf_op jit(solution)/shard_map/ppermute | solution.py:296
  62.3 1.2 %collective-permute-start.14 = (f32[8,128]{1,0:T(8,128)S(1)}, f32[8,128]{1,0:T(8,128)S(1)}, u32[]{:S(2)}, u32[]{:S(2)}) collective-permute-start(f32[8,128]{1,0:T(8,128)S(1)} %totals.1), channel_id=1, source_target_pairs={{0,8},{8,0},{16,24},{24,16},{1,9},{9,1},{17,25},{25,17},{2,10},{10... | collective-permute-start | bytes 12296 | tf_op jit(solution)/shard_map/ppermute | solution.py:321
  63.5 3.6 %collective-permute-start.15 = (f32[8,128]{1,0:T(8,128)S(1)}, f32[8,128]{1,0:T(8,128)S(1)}, u32[]{:S(2)}, u32[]{:S(2)}) collective-permute-start(f32[8,128]{1,0:T(8,128)S(1)} %add.3.mine_ref), channel_id=1, source_target_pairs={{0,16},{8,24},{16,0},{24,8},{1,17},{9,25},{17,1},{25,9},{2,18},{10... | collective-permute-start | bytes 12296 | tf_op jit(solution)/shard_map/ppermute | solution.py:321

commit v3 on v2

--- a/solution.py
+++ b/solution.py
@@ -17,7 +17,8 @@
 OWNERS = ((0, 2, 4, 5, 7), (1, 2, 3, 5, 6))
 ROUNDS_IN = (4, 3, 5, 1, 7, 6, 2)
 ROUNDS_OUT = (4, 3, 5, 7, 6, 2, 1)
-QUERY_TILE = 256
+QUERY_TILE = 512
+LANES = 128
 HEADS_VMEM = 40 * 1024 * 1024
 SMALL_VMEM = 8 * 1024 * 1024
 
@@ -73,22 +74,13 @@
     return [refs[((0,) + rounds).index(k)] for k in range(GROUP)]
 
 
-def clip_bounds(lengths_ref, count):
-    bounds, total = [], jnp.int32(0)
-    for clip in range(count):
-        total = total + lengths_ref[clip]
-        bounds.append(total)
-    return bounds
-
-
 def head_kernel(clip_count, extra, lengths_ref, *refs):
     slots = in_slot_order(refs, ROUNDS_IN) + list(refs[GROUP : GROUP + extra])
     refs = refs[GROUP + extra :]
     outs = in_slot_order(refs, ROUNDS_OUT) + list(refs[GROUP : GROUP + extra])
-    data, turned, ids_ref, grads, totals_ref = refs[GROUP + extra :]
+    data, turned, grads, totals_ref = refs[GROUP + extra :]
     place, code = place_and_code()
     rows = slots[0].shape[1]
-    tokens = (GROUP + extra) * rows
     scale = 1.0 / math.sqrt(HS)
     to_log2 = scale * math.log2(math.e)
     totals_ref[...] = jnp.zeros_like(totals_ref)
@@ -99,78 +91,98 @@
         block = lax.bitwise_xor(place, slot) if slot < GROUP else slot
         return pl.ds(pl.multiple_of(block * rows, rows), rows)
 
+    def clip_pass(blocks, clip, start, length):
+        size = blocks * LANES
+        first = pl.multiple_of(lax.div(start, LANES) * LANES, LANES)
+        window = pl.ds(first, size)
+        start = start - first
+        key_row = lax.broadcasted_iota(jnp.int32, (LANES, LANES), 0)
+        query_column = lax.broadcasted_iota(jnp.int32, (1, size), 1)
+        inside = (query_column >= start) & (query_column < start + length)
+
+        def masked(scores):
+            parts = [scores[i * LANES : (i + 1) * LANES] for i in range(blocks)]
+            for i in sorted({0, blocks - 1}):
+                row = key_row + i * LANES
+                allowed = (row >= start) & (row < start + length)
+                allowed = jnp.concatenate([allowed] * (scores.shape[1] // LANES), axis=1)
+                parts[i] = jnp.where(allowed, parts[i], -jnp.inf)
+            return jnp.concatenate(parts, axis=0) if blocks > 1 else parts[0]
+
+        def attend(part, turn, mine):
+            scores = lax.dot_general(
+                data[part + 1, window, :], data[part, mine, :], ROWS_BY_ROWS, preferred_element_type=F32
+            )
+            scores = masked(scores)
+            peak = jnp.max(scores, axis=0, keepdims=True)
+            exponent = jnp.exp2((scores - peak) * to_log2)
+            inverse = 1.0 / jnp.sum(exponent, axis=0, keepdims=True)
+            weights = exponent.astype(BF16)
+            out = jnp.dot(turned[turn, :, window], weights, preferred_element_type=F32) * inverse
+            return out, exponent, weights, inverse
+
+        dkey = dvalue = total = None
+        for begin in range(0, size, QUERY_TILE):
+            width = min(QUERY_TILE, size - begin)
+            mine = pl.ds(first + begin, width)
+            columns = slice(begin, begin + width)
+            target, _, _, _ = attend(3, 2, mine)
+            student, exponent, weights, inverse = attend(0, 1, mine)
+            target = jnp.where(inside[:, columns], target, 0.0)
+            diff = jnp.where(inside[:, columns], student - target, 0.0)
+            squares = jnp.sum(diff * diff, axis=1, keepdims=True)
+            total = squares if total is None else total + squares
+            gradient = (diff * inverse).astype(BF16)
+            delta = jnp.sum(gradient.astype(F32) * student, axis=0, keepdims=True)
+            slope = jnp.dot(data[2, window, :], gradient, preferred_element_type=F32)
+            dscores = (exponent * (slope - delta)).astype(BF16)
+            dquery = jnp.dot(turned[0, :, window], dscores, preferred_element_type=F32)
+            key_part = jnp.dot(dscores, data[0, mine, :], preferred_element_type=F32)
+            value_part = lax.dot_general(weights, gradient, ROWS_BY_ROWS, preferred_element_type=F32)
+            grads[0, mine, :] += (dquery * scale).T
+            grads[3, mine, :] += target.T
+            dkey = key_part if dkey is None else dkey + key_part
+            dvalue = value_part if dvalue is None else dvalue + value_part
+        grads[1, window, :] += dkey * scale
+        grads[2, window, :] += dvalue
+        clip_iota = lax.broadcasted_iota(jnp.int32, (clip_rows, 1), 0)
+        total = jnp.sum(total, axis=0, keepdims=True)
+        totals_ref[...] += jnp.where(clip_iota == clip, total, 0.0)
+
     @pl.when(head_at(code, place) >= 0)
     def _():
         group_start = lax.div(lax.axis_index("seq"), GROUP) * (GROUP * rows)
-        bounds = clip_bounds(lengths_ref, clip_count)
         for slot in range(GROUP + extra):
             where = rows_of(slot)
             for part in range(6):
                 data[part, where, :] = slots[slot][part]
             for turn, part in enumerate((1, 2, 5)):
                 turned[turn, :, where] = slots[slot][part].T
-        key_place = group_start + lax.broadcasted_iota(jnp.int32, (tokens, HS), 0)
-        query_place = group_start + lax.broadcasted_iota(jnp.int32, (1, tokens), 1)
-        key_ids = jnp.zeros((tokens, HS), jnp.int32)
-        query_ids = jnp.zeros((1, tokens), jnp.int32)
-        query_first = jnp.zeros((1, tokens), jnp.int32)
-        for bound in bounds:
-            key_ids = key_ids + (key_place >= bound).astype(jnp.int32)
-            query_ids = query_ids + (query_place >= bound).astype(jnp.int32)
-            query_first = jnp.where(query_place >= bound, bound, query_first)
-        ids_ref[...] = key_ids
-        owned = (query_first >= group_start) & (query_first < group_start + GROUP * rows)
-        grads[1] = jnp.zeros((tokens, HS), F32)
-        grads[2] = jnp.zeros((tokens, HS), F32)
-        clip_iota = lax.broadcasted_iota(jnp.int32, (totals_ref.shape[0], 1), 0)
-
-        def attend(part, turn, mine, keys, allowed):
-            scores = lax.dot_general(
-                data[part + 1, keys, :], data[part, mine, :], ROWS_BY_ROWS, preferred_element_type=F32
-            )
-            scores = jnp.where(allowed, scores, -jnp.inf)
-            peak = jnp.max(scores, axis=0, keepdims=True)
-            exponent = jnp.exp2((scores - peak) * to_log2)
-            inverse = 1.0 / jnp.sum(exponent, axis=0, keepdims=True)
-            weights = exponent.astype(BF16)
-            out = jnp.dot(turned[turn, :, keys], weights, preferred_element_type=F32) * inverse
-            return out, exponent, weights, inverse
-
-        for first in range(0, tokens, QUERY_TILE):
-            width = min(QUERY_TILE, tokens - first)
-            mine = slice(first, first + width)
-            keys = slice(max(0, first - MOST), min(tokens, first + width + MOST))
-            key_tile = ids_ref[keys, :]
-            key_tile = jnp.concatenate([key_tile] * (width // HS), axis=1)
-            allowed = key_tile == query_ids[:, mine]
-            target, _, _, _ = attend(3, 2, mine, keys, allowed)
-            student, exponent, weights, inverse = attend(0, 1, mine, keys, allowed)
-            diff = student - target
-            if extra:
-                diff = jnp.where(owned[:, mine], diff, 0.0)
-                target = jnp.where(owned[:, mine], target, 0.0)
-            squares = jnp.sum(diff * diff, axis=0, keepdims=True)
-            counted = jnp.where(clip_iota == query_ids[:, mine], squares, 0.0)
-            totals_ref[...] += jnp.sum(counted, axis=1, keepdims=True)
-            gradient = (diff * inverse).astype(BF16)
-            delta = jnp.sum(gradient.astype(F32) * student, axis=0, keepdims=True)
-            slope = jnp.dot(data[2, keys, :], gradient, preferred_element_type=F32)
-            dscores = (exponent * (slope - delta)).astype(BF16)
-            dquery = jnp.dot(turned[0, :, keys], dscores, preferred_element_type=F32)
-            grads[0, mine, :] = (dquery * scale).T
-            grads[1, keys, :] += jnp.dot(dscores, data[0, mine, :], preferred_element_type=F32)
-            grads[2, keys, :] += lax.dot_general(
-                weights, gradient, ROWS_BY_ROWS, preferred_element_type=F32
-            )
-            grads[3, mine, :] = target.T
+        grads[...] = jnp.zeros_like(grads)
+
+        def one_clip(clip, begin):
+            length = lengths_ref[clip]
+            start = begin - group_start
+
+            @pl.when((start >= 0) & (start < GROUP * rows))
+            def _():
+                lead = lax.rem(start, LANES)
+                blocks = lax.div(lead + length + LANES - 1, LANES)
+                for count in range(1, MOST // LANES + 2):
+
+                    @pl.when(blocks == count)
+                    def _():
+                        clip_pass(count, clip, start, length)
+
+            return begin + length
+
+        lax.fori_loop(0, clip_count, one_clip, jnp.int32(0))
         high = totals_ref[...].astype(BF16)
         low = (totals_ref[...] - high.astype(F32)).astype(BF16)
         for slot in range(GROUP + extra):
             where = rows_of(slot)
-            for part, factor in enumerate((1.0, scale, 1.0, 1.0)):
-                block = grads[part, where, :]
-                block = block if factor == 1.0 else block * factor
-                outs[slot][part * rows : (part + 1) * rows] = block.astype(BF16)
+            for part in range(4):
+                outs[slot][part * rows : (part + 1) * rows] = grads[part, where, :].astype(BF16)
             outs[slot][4 * rows : 4 * rows + clip_rows] = high
             outs[slot][4 * rows + clip_rows :] = low
 
@@ -249,7 +261,10 @@
         scratch_shapes=[pltpu.SemaphoreType.DMA((GROUP, 2))],
         compiler_params=small,
         name="pack",
-    )(jnp.transpose(student_qkv, (1, 0, 2)), jnp.transpose(target_qkv, (1, 0, 2)))
+    )(
+        pltpu.with_memory_space_constraint(jnp.transpose(student_qkv, (1, 0, 2)), pltpu.HBM),
+        pltpu.with_memory_space_constraint(jnp.transpose(target_qkv, (1, 0, 2)), pltpu.HBM),
+    )
 
     gathered = [packed[0]]
     for k, mine in zip(ROUNDS_IN, packed[1:]):
@@ -282,7 +297,6 @@
         scratch_shapes=[
             pltpu.VMEM((6, tokens, HS), BF16),
             pltpu.VMEM((3, HS, tokens), BF16),
-            pltpu.VMEM((tokens, HS), jnp.int32),
             pltpu.VMEM((4, tokens, HS), F32),
             pltpu.VMEM((clip_rows, HS), F32),
         ],

time: 69.2 us -> 66.7 us (0.964)
  local copies, waits for them, and re-layouts: 2.06 us -> 0.01 us
    unnamed x6 -> x2, local copies, waits for them, and re-layouts: 2.06 us -> 0.01 us
    pallas_call x1, Pallas kernels: 8.19 us -> 6.9 us  [per_device(): pl.pallas_call(functools.partial(head_kernel, clip_count, extra), out_sha...]
    pallas_call x1, Pallas kernels: 0.39 us -> 1.47 us  [per_device(): pl.pallas_call(pack_kernel, out_shape=[jax.ShapeDtypeStruct((6, rows, HS)...]
where the time goes in v3:
time: 66.7 us; the launch traced here: 66.5 us
  starting transfers between devices  37.1 us (56%)
  waiting for transfers between devices  18.6 us (28%)
  Pallas kernels  9.96 us (15%)
  between operations  0.83 us (1%)
    ppermute x7, starting transfers between devices, per_device(): lax.ppermute(mine, axes, pairs(lambda owners, start: [(start + d, start +...  18.6 us
    ppermute x7, starting transfers between devices, per_device(): lax.ppermute(mine, axes, pairs(lambda owners, start: [(start + (d ^ k), s...  18 us
    ppermute x7, waiting for transfers between devices, per_device(): lax.ppermute(mine, axes, pairs(lambda owners, start: [(start + (d ^ k), s...  9.88 us
    pallas_call x1, Pallas kernels, per_device(): pl.pallas_call(functools.partial(head_kernel, clip_count, extra), out_sha...  6.9 us
    ppermute x2, waiting for transfers between devices, over(): return lax.ppermute(totals, axis, [(s, s ^ step) for s in range(count)])  4.38 us
    ppermute x7, waiting for transfers between devices, per_device(): lax.ppermute(mine, axes, pairs(lambda owners, start: [(start + d, start +...  4.34 us
    pallas_call x1, Pallas kernels, per_device(): pl.pallas_call(functools.partial(finish_kernel, clip_count, head_count, e...  1.57 us
    pallas_call x1, Pallas kernels, per_device(): pl.pallas_call(pack_kernel, out_shape=[jax.ShapeDtypeStruct((6, rows, HS)...  1.47 us
  transfers between devices with their start and end apart: 16, of which 7 were waited for; matrix products, arithmetic and copies ran while one was open for 0% of the time, Pallas kernels for 0%

profile of v3, /device:TPU:18, one launch (start us, length us, event | category | flops | bytes accessed | tf_op | source)
XLA Modules:
  0.0 66.5 jit_solution(14493059847740480103)
XLA Ops:
  0.6 1.5 %pack.1 = (bf16[6,128,128]{2,1,0:T(8,128)(2,1)S(1)}, bf16[6,128,128]{2,1,0:T(8,128)(2,1)S(1)}, bf16[6,128,128]{2,1,0:T(8,128)(2,1)S(1)}, bf16[6,128,128]{2,1,0:T...) custom-call(bf16[3,128,640]{2,1,0:T(8,128)(2,1)} %bitcast.3, ...), custom_call_target="tpu_custom_call" | custom-call | tf_op jit(solution)/shard_map/pack/pallas_call | solution.py:256
  2.1 2.2 %collective-permute-start = (bf16[6,128,128]{2,1,0:T(8,128)(2,1)S(1)}, bf16[6,128,128]{2,1,0:T(8,128)(2,1)S(1)}, u32[]{:S(2)}, u32[]{:S(2)}) collective-permute-start(bf16[6,128,128]{2,1,0:T(8,128)(2,1)S(1)} %get-tuple-element.21), channel_id=1, source_target_pairs={{4,0},{6,2},{0,4},{1,5},{3,7},{13,9},{14,10},{15,11},{9,13},{10,14... | collective-permute-start | bytes 589832 | tf_op jit(solution)/shard_map/ppermute | solution.py:272
  4.4 3.5 %collective-permute-start.1 = (bf16[6,128,128]{2,1,0:T(8,128)(2,1)S(1)}, bf16[6,128,128]{2,1,0:T(8,128)(2,1)S(1)}, u32[]{:S(2)}, u32[]{:S(2)}) collective-permute-start(bf16[6,128,128]{2,1,0:T(8,128)(2,1)S(1)} %get-tuple-element.22), channel_id=1, source_target_pairs={{3,0},{1,2},{7,4},{6,5},{4,7},{10,9},{9,10},{8,11},{14,13},{13,14}... | collective-permute-start | bytes 589832 | tf_op jit(solution)/shard_map/ppermute | solution.py:272
  7.9 1.3 %collective-permute-start.2 = (bf16[6,128,128]{2,1,0:T(8,128)(2,1)S(1)}, bf16[6,128,128]{2,1,0:T(8,128)(2,1)S(1)}, u32[]{:S(2)}, u32[]{:S(2)}) collective-permute-start(bf16[6,128,128]{2,1,0:T(8,128)(2,1)S(1)} %get-tuple-element.23), channel_id=1, source_target_pairs={{5,0},{7,2},{1,4},{0,5},{2,7},{12,9},{15,10},{14,11},{8,13},{11,14... | collective-permute-start | bytes 589832 | tf_op jit(solution)/shard_map/ppermute | solution.py:272
  9.2 4.4 %collective-permute-start.3 = (bf16[6,128,128]{2,1,0:T(8,128)(2,1)S(1)}, bf16[6,128,128]{2,1,0:T(8,128)(2,1)S(1)}, u32[]{:S(2)}, u32[]{:S(2)}) collective-permute-start(bf16[6,128,128]{2,1,0:T(8,128)(2,1)S(1)} %get-tuple-element.24), channel_id=1, source_target_pairs={{1,0},{3,2},{5,4},{4,5},{6,7},{8,9},{11,10},{10,11},{12,13},{15,14... | collective-permute-start | bytes 589832 | tf_op jit(solution)/shard_map/ppermute | solution.py:272
  13.5 1.3 %collective-permute-start.4 = (bf16[6,128,128]{2,1,0:T(8,128)(2,1)S(1)}, bf16[6,128,128]{2,1,0:T(8,128)(2,1)S(1)}, u32[]{:S(2)}, u32[]{:S(2)}) collective-permute-start(bf16[6,128,128]{2,1,0:T(8,128)(2,1)S(1)} %get-tuple-element.25), channel_id=1, source_target_pairs={{7,0},{5,2},{3,4},{2,5},{0,7},{14,9},{13,10},{12,11},{10,13},{9,14... | collective-permute-start | bytes 589832 | tf_op jit(solution)/shard_map/ppermute | solution.py:272
  14.8 4.0 %collective-permute-start.5 = (bf16[6,128,128]{2,1,0:T(8,128)(2,1)S(1)}, bf16[6,128,128]{2,1,0:T(8,128)(2,1)S(1)}, u32[]{:S(2)}, u32[]{:S(2)}) collective-permute-start(bf16[6,128,128]{2,1,0:T(8,128)(2,1)S(1)} %get-tuple-element.26), channel_id=1, source_target_pairs={{6,0},{4,2},{2,4},{3,5},{1,7},{15,9},{12,10},{13,11},{11,13},{8,14... | collective-permute-start | bytes 589832 | tf_op jit(solution)/shard_map/ppermute | solution.py:272
  18.9 1.3 %collective-permute-start.6 = (bf16[6,128,128]{2,1,0:T(8,128)(2,1)S(1)}, bf16[6,128,128]{2,1,0:T(8,128)(2,1)S(1)}, u32[]{:S(2)}, u32[]{:S(2)}) collective-permute-start(bf16[6,128,128]{2,1,0:T(8,128)(2,1)S(1)} %get-tuple-element.27), channel_id=1, source_target_pairs={{2,0},{0,2},{6,4},{7,5},{5,7},{11,9},{8,10},{9,11},{15,13},{12,14}... | collective-permute-start | bytes 589832 | tf_op jit(solution)/shard_map/ppermute | solution.py:272
  20.2 2.6 %collective-permute-done.2.refs_3_ = bf16[6,128,128]{2,1,0:T(8,128)(2,1)S(1)} collective-permute-done((bf16[6,128,128]{2,1,0:T(8,128)(2,1)S(1)}, bf16[6,128,128]{2,1,0:T(8,128)(2,1)S(1)}, u32[]{:S(2)}, u32[]{:S(2)}) %collective-permute-start.2) | collective-permute-done | bytes 196640 | tf_op jit(solution)/shard_map/ppermute | solution.py:272
  22.8 6.1 %collective-permute-done.4.refs_5_ = bf16[6,128,128]{2,1,0:T(8,128)(2,1)S(1)} collective-permute-done((bf16[6,128,128]{2,1,0:T(8,128)(2,1)S(1)}, bf16[6,128,128]{2,1,0:T(8,128)(2,1)S(1)}, u32[]{:S(2)}, u32[]{:S(2)}) %collective-permute-start.4) | collective-permute-done | bytes 196640 | tf_op jit(solution)/shard_map/ppermute | solution.py:272
  28.9 1.1 %collective-permute-done.5.refs_6_ = bf16[6,128,128]{2,1,0:T(8,128)(2,1)S(1)} collective-permute-done((bf16[6,128,128]{2,1,0:T(8,128)(2,1)S(1)}, bf16[6,128,128]{2,1,0:T(8,128)(2,1)S(1)}, u32[]{:S(2)}, u32[]{:S(2)}) %collective-permute-start.5) | collective-permute-done | bytes 196640 | tf_op jit(solution)/shard_map/ppermute | solution.py:272
  30.1 6.9 %heads.1 = (bf16[528,128]{1,0:T(8,128)(2,1)S(1)}, bf16[528,128]{1,0:T(8,128)(2,1)S(1)}, bf16[528,128]{1,0:T(8,128)(2,1)S(1)}, bf16[528,128]{1,0:T(8,128)(2,1)S(1...) custom-call(s32[4]{0:T(128)S(1)} %copy-done, ...), custom_call_target="tpu_custom_call" | custom-call | tf_op jit(solution)/shard_map/heads/pallas_call | solution.py:292
  37.0 1.9 %collective-permute-start.7 = (bf16[528,128]{1,0:T(8,128)(2,1)S(1)}, bf16[528,128]{1,0:T(8,128)(2,1)S(1)}, u32[]{:S(2)}, u32[]{:S(2)}) collective-permute-start(bf16[528,128]{1,0:T(8,128)(2,1)S(1)} %get-tuple-element.29), channel_id=1, source_target_pairs={{0,4},{2,6},{4,0},{5,1},{7,3},{9,13},{10,14},{11,15},{13,9},{14,10... | collective-permute-start | bytes 405512 | tf_op jit(solution)/shard_map/ppermute | solution.py:310
  38.9 1.9 %collective-permute-start.8 = (bf16[528,128]{1,0:T(8,128)(2,1)S(1)}, bf16[528,128]{1,0:T(8,128)(2,1)S(1)}, u32[]{:S(2)}, u32[]{:S(2)}) collective-permute-start(bf16[528,128]{1,0:T(8,128)(2,1)S(1)} %get-tuple-element.30), channel_id=1, source_target_pairs={{0,3},{2,1},{4,7},{5,6},{7,4},{9,10},{10,9},{11,8},{13,14},{14,13}... | collective-permute-start | bytes 405512 | tf_op jit(solution)/shard_map/ppermute | solution.py:310
  40.8 1.3 %collective-permute-start.9 = (bf16[528,128]{1,0:T(8,128)(2,1)S(1)}, bf16[528,128]{1,0:T(8,128)(2,1)S(1)}, u32[]{:S(2)}, u32[]{:S(2)}) collective-permute-start(bf16[528,128]{1,0:T(8,128)(2,1)S(1)} %get-tuple-element.31), channel_id=1, source_target_pairs={{0,5},{2,7},{4,1},{5,0},{7,2},{9,12},{10,15},{11,14},{13,8},{14,11... | collective-permute-start | bytes 405512 | tf_op jit(solution)/shard_map/ppermute | solution.py:310
  42.1 1.3 %collective-permute-start.10 = (bf16[528,128]{1,0:T(8,128)(2,1)S(1)}, bf16[528,128]{1,0:T(8,128)(2,1)S(1)}, u32[]{:S(2)}, u32[]{:S(2)}) collective-permute-start(bf16[528,128]{1,0:T(8,128)(2,1)S(1)} %get-tuple-element.32), channel_id=1, source_target_pairs={{0,7},{2,5},{4,3},{5,2},{7,0},{9,14},{10,13},{11,12},{13,10},{14,9... | collective-permute-start | bytes 405512 | tf_op jit(solution)/shard_map/ppermute | solution.py:310
  43.4 8.3 %collective-permute-start.11 = (bf16[528,128]{1,0:T(8,128)(2,1)S(1)}, bf16[528,128]{1,0:T(8,128)(2,1)S(1)}, u32[]{:S(2)}, u32[]{:S(2)}) collective-permute-start(bf16[528,128]{1,0:T(8,128)(2,1)S(1)} %get-tuple-element.33), channel_id=1, source_target_pairs={{0,6},{2,4},{4,2},{5,3},{7,1},{9,15},{10,12},{11,13},{13,11},{14,8... | collective-permute-start | bytes 405512 | tf_op jit(solution)/shard_map/ppermute | solution.py:310
  51.8 1.3 %collective-permute-start.12 = (bf16[528,128]{1,0:T(8,128)(2,1)S(1)}, bf16[528,128]{1,0:T(8,128)(2,1)S(1)}, u32[]{:S(2)}, u32[]{:S(2)}) collective-permute-start(bf16[528,128]{1,0:T(8,128)(2,1)S(1)} %get-tuple-element.34), channel_id=1, source_target_pairs={{0,2},{2,0},{4,6},{5,7},{7,5},{9,11},{10,8},{11,9},{13,15},{14,12}... | collective-permute-start | bytes 405512 | tf_op jit(solution)/shard_map/ppermute | solution.py:310
  53.1 2.5 %collective-permute-start.13 = (bf16[528,128]{1,0:T(8,128)(2,1)S(1)}, bf16[528,128]{1,0:T(8,128)(2,1)S(1)}, u32[]{:S(2)}, u32[]{:S(2)}) collective-permute-start(bf16[528,128]{1,0:T(8,128)(2,1)S(1)} %get-tuple-element.35), channel_id=1, source_target_pairs={{0,1},{2,3},{4,5},{5,4},{7,6},{9,8},{10,11},{11,10},{13,12},{14,15... | collective-permute-start | bytes 405512 | tf_op jit(solution)/shard_map/ppermute | solution.py:310
  55.7 2.9 %collective-permute-done.11.refs_5_ = bf16[528,128]{1,0:T(8,128)(2,1)S(1)} collective-permute-done((bf16[528,128]{1,0:T(8,128)(2,1)S(1)}, bf16[528,128]{1,0:T(8,128)(2,1)S(1)}, u32[]{:S(2)}, u32[]{:S(2)}) %collective-permute-start.11) | collective-permute-done | bytes 135200 | tf_op jit(solution)/shard_map/ppermute | solution.py:310
  58.6 1.4 %collective-permute-done.13.refs_7_ = bf16[528,128]{1,0:T(8,128)(2,1)S(1)} collective-permute-done((bf16[528,128]{1,0:T(8,128)(2,1)S(1)}, bf16[528,128]{1,0:T(8,128)(2,1)S(1)}, u32[]{:S(2)}, u32[]{:S(2)}) %collective-permute-start.13) | collective-permute-done | bytes 135200 | tf_op jit(solution)/shard_map/ppermute | solution.py:310
  60.1 1.2 %collective-permute-done.14 = f32[8,128]{1,0:T(8,128)S(1)} collective-permute-done((f32[8,128]{1,0:T(8,128)S(1)}, f32[8,128]{1,0:T(8,128)S(1)}, u32[]{:S(2)}, u32[]{:S(2)}) %collective-permute-start.14) | collective-permute-done | bytes 4128 | tf_op jit(solution)/shard_map/ppermute | solution.py:335
  61.7 3.2 %collective-permute-done.15.other_ref = f32[8,128]{1,0:T(8,128)S(1)} collective-permute-done((f32[8,128]{1,0:T(8,128)S(1)}, f32[8,128]{1,0:T(8,128)S(1)}, u32[]{:S(2)}, u32[]{:S(2)}) %collective-permute-start.15) | collective-permute-done | bytes 4128 | tf_op jit(solution)/shard_map/ppermute | solution.py:335
  64.9 1.6 %finish.1 = (bf16[3,128,640]{2,1,0:T(8,128)(2,1)}, bf16[128,640]{1,0:T(8,128)(2,1)}) custom-call(s32[4]{0:T(128)S(1)} %copy-done, f32[8,128]{1,0:T(8,128)S(1)} %add.3.mine_ref, f32[8,128]{1,0:T(8,128)S(1)} %collective-permute-done.15.other_ref, bf16[528,128]{1,0:T(8,128)(2,1)S(1)} %get-tuple-element.28.refs_0_, ...), custom_call_target="tpu_custom_call" | custom-call | tf_op jit(solution)/shard_map/finish/pallas_call | solution.py:346
  (15 shorter events, 0.5 us)
Async XLA Ops:
  2.1 12.7 %collective-permute-start = (bf16[6,128,128]{2,1,0:T(8,128)(2,1)S(1)}, bf16[6,128,128]{2,1,0:T(8,128)(2,1)S(1)}, u32[]{:S(2)}, u32[]{:S(2)}) collective-permute-start(bf16[6,128,128]{2,1,0:T(8,128)(2,1)S(1)} %get-tuple-element.21), channel_id=1, source_target_pairs={{4,0},{6,2},{0,4},{1,5},{3,7},{13,9},{14,10},{15,11},{9,13},{10,14... | collective-permute-start | bytes 589832 | tf_op jit(solution)/shard_map/ppermute | solution.py:272
  4.4 14.5 %collective-permute-start.1 = (bf16[6,128,128]{2,1,0:T(8,128)(2,1)S(1)}, bf16[6,128,128]{2,1,0:T(8,128)(2,1)S(1)}, u32[]{:S(2)}, u32[]{:S(2)}) collective-permute-start(bf16[6,128,128]{2,1,0:T(8,128)(2,1)S(1)} %get-tuple-element.22), channel_id=1, source_target_pairs={{3,0},{1,2},{7,4},{6,5},{4,7},{10,9},{9,10},{8,11},{14,13},{13,14}... | collective-permute-start | bytes 589832 | tf_op jit(solution)/shard_map/ppermute | solution.py:272
  7.9 15.0 %collective-permute-start.2 = (bf16[6,128,128]{2,1,0:T(8,128)(2,1)S(1)}, bf16[6,128,128]{2,1,0:T(8,128)(2,1)S(1)}, u32[]{:S(2)}, u32[]{:S(2)}) collective-permute-start(bf16[6,128,128]{2,1,0:T(8,128)(2,1)S(1)} %get-tuple-element.23), channel_id=1, source_target_pairs={{5,0},{7,2},{1,4},{0,5},{2,7},{12,9},{15,10},{14,11},{8,13},{11,14... | collective-permute-start | bytes 589832 | tf_op jit(solution)/shard_map/ppermute | solution.py:272
  9.2 13.7 %collective-permute-start.3 = (bf16[6,128,128]{2,1,0:T(8,128)(2,1)S(1)}, bf16[6,128,128]{2,1,0:T(8,128)(2,1)S(1)}, u32[]{:S(2)}, u32[]{:S(2)}) collective-permute-start(bf16[6,128,128]{2,1,0:T(8,128)(2,1)S(1)} %get-tuple-element.24), channel_id=1, source_target_pairs={{1,0},{3,2},{5,4},{4,5},{6,7},{8,9},{11,10},{10,11},{12,13},{15,14... | collective-permute-start | bytes 589832 | tf_op jit(solution)/shard_map/ppermute | solution.py:272
  13.5 15.4 %collective-permute-start.4 = (bf16[6,128,128]{2,1,0:T(8,128)(2,1)S(1)}, bf16[6,128,128]{2,1,0:T(8,128)(2,1)S(1)}, u32[]{:S(2)}, u32[]{:S(2)}) collective-permute-start(bf16[6,128,128]{2,1,0:T(8,128)(2,1)S(1)} %get-tuple-element.25), channel_id=1, source_target_pairs={{7,0},{5,2},{3,4},{2,5},{0,7},{14,9},{13,10},{12,11},{10,13},{9,14... | collective-permute-start | bytes 589832 | tf_op jit(solution)/shard_map/ppermute | solution.py:272
  14.8 15.2 %collective-permute-start.5 = (bf16[6,128,128]{2,1,0:T(8,128)(2,1)S(1)}, bf16[6,128,128]{2,1,0:T(8,128)(2,1)S(1)}, u32[]{:S(2)}, u32[]{:S(2)}) collective-permute-start(bf16[6,128,128]{2,1,0:T(8,128)(2,1)S(1)} %get-tuple-element.26), channel_id=1, source_target_pairs={{6,0},{4,2},{2,4},{3,5},{1,7},{15,9},{12,10},{13,11},{11,13},{8,14... | collective-permute-start | bytes 589832 | tf_op jit(solution)/shard_map/ppermute | solution.py:272
  18.9 11.2 %copy-start = (s32[4]{0:T(128)S(1)}, s32[4]{0:T(128)}, u32[]{:S(2)}) copy-start(s32[4]{0:T(128)} %lengths_ref.3) | copy-start | bytes 52
  18.9 11.2 %collective-permute-start.6 = (bf16[6,128,128]{2,1,0:T(8,128)(2,1)S(1)}, bf16[6,128,128]{2,1,0:T(8,128)(2,1)S(1)}, u32[]{:S(2)}, u32[]{:S(2)}) collective-permute-start(bf16[6,128,128]{2,1,0:T(8,128)(2,1)S(1)} %get-tuple-element.27), channel_id=1, source_target_pairs={{2,0},{0,2},{6,4},{7,5},{5,7},{11,9},{8,10},{9,11},{15,13},{12,14}... | collective-permute-start | bytes 589832 | tf_op jit(solution)/shard_map/ppermute | solution.py:272
  37.0 14.8 %collective-permute-start.7 = (bf16[528,128]{1,0:T(8,128)(2,1)S(1)}, bf16[528,128]{1,0:T(8,128)(2,1)S(1)}, u32[]{:S(2)}, u32[]{:S(2)}) collective-permute-start(bf16[528,128]{1,0:T(8,128)(2,1)S(1)} %get-tuple-element.29), channel_id=1, source_target_pairs={{0,4},{2,6},{4,0},{5,1},{7,3},{9,13},{10,14},{11,15},{13,9},{14,10... | collective-permute-start | bytes 405512 | tf_op jit(solution)/shard_map/ppermute | solution.py:310
  38.9 14.2 %collective-permute-start.8 = (bf16[528,128]{1,0:T(8,128)(2,1)S(1)}, bf16[528,128]{1,0:T(8,128)(2,1)S(1)}, u32[]{:S(2)}, u32[]{:S(2)}) collective-permute-start(bf16[528,128]{1,0:T(8,128)(2,1)S(1)} %get-tuple-element.30), channel_id=1, source_target_pairs={{0,3},{2,1},{4,7},{5,6},{7,4},{9,10},{10,9},{11,8},{13,14},{14,13}... | collective-permute-start | bytes 405512 | tf_op jit(solution)/shard_map/ppermute | solution.py:310
  40.8 14.8 %collective-permute-start.9 = (bf16[528,128]{1,0:T(8,128)(2,1)S(1)}, bf16[528,128]{1,0:T(8,128)(2,1)S(1)}, u32[]{:S(2)}, u32[]{:S(2)}) collective-permute-start(bf16[528,128]{1,0:T(8,128)(2,1)S(1)} %get-tuple-element.31), channel_id=1, source_target_pairs={{0,5},{2,7},{4,1},{5,0},{7,2},{9,12},{10,15},{11,14},{13,8},{14,11... | collective-permute-start | bytes 405512 | tf_op jit(solution)/shard_map/ppermute | solution.py:310
  42.1 13.5 %collective-permute-start.10 = (bf16[528,128]{1,0:T(8,128)(2,1)S(1)}, bf16[528,128]{1,0:T(8,128)(2,1)S(1)}, u32[]{:S(2)}, u32[]{:S(2)}) collective-permute-start(bf16[528,128]{1,0:T(8,128)(2,1)S(1)} %get-tuple-element.32), channel_id=1, source_target_pairs={{0,7},{2,5},{4,3},{5,2},{7,0},{9,14},{10,13},{11,12},{13,10},{14,9... | collective-permute-start | bytes 405512 | tf_op jit(solution)/shard_map/ppermute | solution.py:310
  43.4 15.2 %collective-permute-start.11 = (bf16[528,128]{1,0:T(8,128)(2,1)S(1)}, bf16[528,128]{1,0:T(8,128)(2,1)S(1)}, u32[]{:S(2)}, u32[]{:S(2)}) collective-permute-start(bf16[528,128]{1,0:T(8,128)(2,1)S(1)} %get-tuple-element.33), channel_id=1, source_target_pairs={{0,6},{2,4},{4,2},{5,3},{7,1},{9,15},{10,12},{11,13},{13,11},{14,8... | collective-permute-start | bytes 405512 | tf_op jit(solution)/shard_map/ppermute | solution.py:310
  51.8 6.8 %collective-permute-start.12 = (bf16[528,128]{1,0:T(8,128)(2,1)S(1)}, bf16[528,128]{1,0:T(8,128)(2,1)S(1)}, u32[]{:S(2)}, u32[]{:S(2)}) collective-permute-start(bf16[528,128]{1,0:T(8,128)(2,1)S(1)} %get-tuple-element.34), channel_id=1, source_target_pairs={{0,2},{2,0},{4,6},{5,7},{7,5},{9,11},{10,8},{11,9},{13,15},{14,12}... | collective-permute-start | bytes 405512 | tf_op jit(solution)/shard_map/ppermute | solution.py:310
  53.1 6.9 %collective-permute-start.13 = (bf16[528,128]{1,0:T(8,128)(2,1)S(1)}, bf16[528,128]{1,0:T(8,128)(2,1)S(1)}, u32[]{:S(2)}, u32[]{:S(2)}) collective-permute-start(bf16[528,128]{1,0:T(8,128)(2,1)S(1)} %get-tuple-element.35), channel_id=1, source_target_pairs={{0,1},{2,3},{4,5},{5,4},{7,6},{9,8},{10,11},{11,10},{13,12},{14,15... | collective-permute-start | bytes 405512 | tf_op jit(solution)/shard_map/ppermute | solution.py:310
  60.0 1.2 %collective-permute-start.14 = (f32[8,128]{1,0:T(8,128)S(1)}, f32[8,128]{1,0:T(8,128)S(1)}, u32[]{:S(2)}, u32[]{:S(2)}) collective-permute-start(f32[8,128]{1,0:T(8,128)S(1)} %totals.1), channel_id=1, source_target_pairs={{0,8},{8,0},{16,24},{24,16},{1,9},{9,1},{17,25},{25,17},{2,10},{10... | collective-permute-start | bytes 12296 | tf_op jit(solution)/shard_map/ppermute | solution.py:335
  61.3 3.6 %collective-permute-start.15 = (f32[8,128]{1,0:T(8,128)S(1)}, f32[8,128]{1,0:T(8,128)S(1)}, u32[]{:S(2)}, u32[]{:S(2)}) collective-permute-start(f32[8,128]{1,0:T(8,128)S(1)} %add.3.mine_ref), channel_id=1, source_target_pairs={{0,16},{8,24},{16,0},{24,8},{1,17},{9,25},{17,1},{25,9},{2,18},{10... | collective-permute-start | bytes 12296 | tf_op jit(solution)/shard_map/ppermute | solution.py:335

commit v4 on v3

--- a/solution.py
+++ b/solution.py
@@ -16,7 +16,7 @@
 GROUP = 8
 OWNERS = ((0, 2, 4, 5, 7), (1, 2, 3, 5, 6))
 ROUNDS_IN = (4, 3, 5, 1, 7, 6, 2)
-ROUNDS_OUT = (4, 3, 5, 7, 6, 2, 1)
+ROUNDS_OUT = (7, 3, 5, 4, 2, 6, 1)
 QUERY_TILE = 512
 LANES = 128
 HEADS_VMEM = 40 * 1024 * 1024
@@ -96,40 +96,36 @@
         first = pl.multiple_of(lax.div(start, LANES) * LANES, LANES)
         window = pl.ds(first, size)
         start = start - first
-        key_row = lax.broadcasted_iota(jnp.int32, (LANES, LANES), 0)
         query_column = lax.broadcasted_iota(jnp.int32, (1, size), 1)
         inside = (query_column >= start) & (query_column < start + length)
 
-        def masked(scores):
-            parts = [scores[i * LANES : (i + 1) * LANES] for i in range(blocks)]
+        def masked(scores, axis):
+            parts = jnp.split(scores, blocks, axis=axis)
             for i in sorted({0, blocks - 1}):
-                row = key_row + i * LANES
-                allowed = (row >= start) & (row < start + length)
-                allowed = jnp.concatenate([allowed] * (scores.shape[1] // LANES), axis=1)
-                parts[i] = jnp.where(allowed, parts[i], -jnp.inf)
-            return jnp.concatenate(parts, axis=0) if blocks > 1 else parts[0]
-
-        def attend(part, turn, mine):
-            scores = lax.dot_general(
-                data[part + 1, window, :], data[part, mine, :], ROWS_BY_ROWS, preferred_element_type=F32
-            )
-            scores = masked(scores)
-            peak = jnp.max(scores, axis=0, keepdims=True)
+                key = lax.broadcasted_iota(jnp.int32, parts[i].shape, axis) + i * LANES
+                parts[i] = jnp.where((key >= start) & (key < start + length), parts[i], -jnp.inf)
+            return jnp.concatenate(parts, axis=axis)
+
+        def softmax(scores, axis):
+            peak = jnp.max(scores, axis=axis, keepdims=True)
             exponent = jnp.exp2((scores - peak) * to_log2)
-            inverse = 1.0 / jnp.sum(exponent, axis=0, keepdims=True)
-            weights = exponent.astype(BF16)
-            out = jnp.dot(turned[turn, :, window], weights, preferred_element_type=F32) * inverse
-            return out, exponent, weights, inverse
+            return exponent, 1.0 / jnp.sum(exponent, axis=axis, keepdims=True)
+
+        def product(a, b):
+            return lax.dot_general(a, b, ROWS_BY_ROWS, preferred_element_type=F32)
 
         dkey = dvalue = total = None
         for begin in range(0, size, QUERY_TILE):
             width = min(QUERY_TILE, size - begin)
             mine = pl.ds(first + begin, width)
             columns = slice(begin, begin + width)
-            target, _, _, _ = attend(3, 2, mine)
-            student, exponent, weights, inverse = attend(0, 1, mine)
-            target = jnp.where(inside[:, columns], target, 0.0)
-            diff = jnp.where(inside[:, columns], student - target, 0.0)
+            exponent, inverse = softmax(masked(product(data[3, mine, :], data[4, window, :]), 1), 1)
+            target = jnp.dot(exponent.astype(BF16), data[5, window, :], preferred_element_type=F32)
+            target = target * inverse
+            exponent, inverse = softmax(masked(product(data[1, window, :], data[0, mine, :]), 0), 0)
+            weights = exponent.astype(BF16)
+            student = jnp.dot(turned[1, :, window], weights, preferred_element_type=F32) * inverse
+            diff = jnp.where(inside[:, columns], student - target.T, 0.0)
             squares = jnp.sum(diff * diff, axis=1, keepdims=True)
             total = squares if total is None else total + squares
             gradient = (diff * inverse).astype(BF16)
@@ -138,9 +134,10 @@
             dscores = (exponent * (slope - delta)).astype(BF16)
             dquery = jnp.dot(turned[0, :, window], dscores, preferred_element_type=F32)
             key_part = jnp.dot(dscores, data[0, mine, :], preferred_element_type=F32)
-            value_part = lax.dot_general(weights, gradient, ROWS_BY_ROWS, preferred_element_type=F32)
+            value_part = product(weights, gradient)
             grads[0, mine, :] += (dquery * scale).T
-            grads[3, mine, :] += target.T
+            query = lax.broadcasted_iota(jnp.int32, (width, HS), 0) + begin
+            grads[3, mine, :] += jnp.where((query >= start) & (query < start + length), target, 0.0)
             dkey = key_part if dkey is None else dkey + key_part
             dvalue = value_part if dvalue is None else dvalue + value_part
         grads[1, window, :] += dkey * scale
@@ -156,7 +153,7 @@
             where = rows_of(slot)
             for part in range(6):
                 data[part, where, :] = slots[slot][part]
-            for turn, part in enumerate((1, 2, 5)):
+            for turn, part in enumerate((1, 2)):
                 turned[turn, :, where] = slots[slot][part].T
         grads[...] = jnp.zeros_like(grads)
 
@@ -198,11 +195,13 @@
     out[...] = total
 
 
-def finish_kernel(clip_count, head_count, extra, lengths_ref, mine_ref, other_ref, *refs):
-    slots, extras, (grads_ref, target_ref) = in_slot_order(refs, ROUNDS_OUT), refs[GROUP:-2], refs[-2:]
+def finish_kernel(clip_count, head_count, extra, sec_count, lengths_ref, *refs):
+    sums, refs = refs[:sec_count], refs[sec_count:]
+    slots, extras = in_slot_order(refs, ROUNDS_OUT), refs[GROUP:-5]
+    grads_out, target_out, grads_ref, target_ref, sems = refs[-5:]
     place, code = place_and_code()
     rows = target_ref.shape[0]
-    totals = mine_ref[...] + other_ref[...]
+    totals = sum((ref[...] for ref in sums[1:]), sums[0][...])
     first = lax.axis_index("seq") * rows
     token = first + lax.broadcasted_iota(jnp.int32, (rows, HS), 0)
     factor = jnp.zeros((rows, HS), F32)
@@ -213,17 +212,36 @@
         value = lax.rsqrt(totals[clip : clip + 1, :] / size + EPS)
         factor = jnp.where((token >= begin) & (token < begin + length), value, factor)
         begin = begin + length
-    for k in range(GROUP):
-        head = head_at(code, lax.bitwise_xor(place, k))
-
-        @pl.when(head >= 0)
-        def _():
-            cols = columns_of(head)
-            for part in range(3):
-                block = slots[k][part * rows : (part + 1) * rows].astype(F32)
-                grads_ref[part, :, cols] = (block * factor).astype(BF16)
-            target_ref[:, cols] = slots[k][3 * rows : 4 * rows]
-
+    def for_heads(visit):
+        for k in range(GROUP):
+            head = head_at(code, lax.bitwise_xor(place, k))
+            pl.when(head >= 0)(functools.partial(visit, k, columns_of(head)))
+
+    def copies(k, cols):
+        return (
+            pltpu.make_async_copy(
+                grads_ref.at[:, :, cols], grads_out.at[:, :, cols], sems.at[k, 0]
+            ),
+            pltpu.make_async_copy(target_ref.at[:, cols], target_out.at[:, cols], sems.at[k, 1]),
+        )
+
+    def start(k, cols):
+        for copy in copies(k, cols):
+            copy.start()
+
+    def wait(k, cols):
+        for copy in copies(k, cols):
+            copy.wait()
+
+    def scale(k, cols):
+        target_ref[:, cols] = slots[k][3 * rows : 4 * rows]
+        for part in range(3):
+            block = slots[k][part * rows : (part + 1) * rows].astype(F32)
+            grads_ref[part, :, cols] = (block * factor).astype(BF16)
+        if not extra:
+            start(k, cols)
+
+    for_heads(scale)
     for head in range(head_count if extra else 0):
         cols = slice(head * HS, (head + 1) * HS)
         for part in range(3):
@@ -231,6 +249,9 @@
             more = (more * factor).astype(BF16)
             grads_ref[part, :, cols] = grads_ref[part, :, cols] + more
         target_ref[:, cols] = target_ref[:, cols] + extras[head][3 * rows : 4 * rows]
+    if extra:
+        for_heads(start)
+    for_heads(wait)
 
 
 def both_axes(sec_count, seq_count, pairs_of):
@@ -296,7 +317,7 @@
         out_specs=[VMEM] * (GROUP + extra),
         scratch_shapes=[
             pltpu.VMEM((6, tokens, HS), BF16),
-            pltpu.VMEM((3, HS, tokens), BF16),
+            pltpu.VMEM((2, HS, tokens), BF16),
             pltpu.VMEM((4, tokens, HS), F32),
             pltpu.VMEM((clip_rows, HS), F32),
         ],
@@ -338,22 +359,24 @@
     while step < seq_count:
         totals = totals + over(totals, "seq", seq_count, step)
         step *= 2
-    step = 1
-    while 2 * step < sec_count:
-        totals = totals + over(totals, "sec", sec_count, step)
-        step *= 2
+    others = [over(totals, "sec", sec_count, step) for step in range(1, sec_count)]
 
     grads, target_out = pl.pallas_call(
-        functools.partial(finish_kernel, clip_count, head_count, extra),
+        functools.partial(finish_kernel, clip_count, head_count, extra, sec_count),
         out_shape=[
             jax.ShapeDtypeStruct((3, rows, width), BF16),
             jax.ShapeDtypeStruct((rows, width), BF16),
         ],
-        in_specs=[SMEM] + [VMEM] * (2 + GROUP + len(extras)),
-        out_specs=[VMEM] * 2,
+        in_specs=[SMEM] + [VMEM] * (sec_count + GROUP + len(extras)),
+        out_specs=[pl.BlockSpec(memory_space=pltpu.HBM)] * 2,
+        scratch_shapes=[
+            pltpu.VMEM((3, rows, width), BF16),
+            pltpu.VMEM((rows, width), BF16),
+            pltpu.SemaphoreType.DMA((GROUP, 2)),
+        ],
         compiler_params=small,
         name="finish",
-    )(clip_lengths, totals, over(totals, "sec", sec_count, step), *returned, *extras)
+    )(clip_lengths, totals, *others, *returned, *extras)
     return jnp.transpose(grads, (1, 0, 2)), target_out
 
 

time: 66.7 us -> 65.3 us (0.979); the launches traced: 66.5 us -> 64.1 us
  waiting for transfers between devices: 18.6 us -> 16.5 us
    ppermute x2 -> x3, waiting for transfers between devices: 4.38 us -> 1.83 us  [over(): return lax.ppermute(totals, axis, [(s, s ^ step) for s in range(count)])]
    ppermute x2 -> x3, starting transfers between devices: 0.44 us -> 1.92 us  [over(): return lax.ppermute(totals, axis, [(s, s ^ step) for s in range(count)])]
    ppermute x7, starting transfers between devices: 18.6 us -> 17.6 us  [per_device(): lax.ppermute(mine, axes, pairs(lambda owners, start: [(start + d, start +...]
  transfers between devices with their start and end apart: 16 -> 17, of which waited for: 7 -> 8; matrix products, arithmetic and copies ran while one was open for 0% -> 0% of each run, Pallas kernels for 0% -> 0%
where the time goes in v4:
time: 65.3 us; the launch traced here: 64.1 us
  starting transfers between devices  37.5 us (57%)
  waiting for transfers between devices  16.5 us (25%)
  Pallas kernels  9.36 us (14%)
  between operations  0.83 us (1%)
    ppermute x7, starting transfers between devices, per_device(): lax.ppermute(mine, axes, pairs(lambda owners, start: [(start + (d ^ k), s...  18 us
    ppermute x7, starting transfers between devices, per_device(): lax.ppermute(mine, axes, pairs(lambda owners, start: [(start + d, start +...  17.6 us
    ppermute x7, waiting for transfers between devices, per_device(): lax.ppermute(mine, axes, pairs(lambda owners, start: [(start + (d ^ k), s...  9.88 us
    pallas_call x1, Pallas kernels, per_device(): pl.pallas_call(functools.partial(head_kernel, clip_count, extra), out_sha...  6.3 us
    ppermute x7, waiting for transfers between devices, per_device(): lax.ppermute(mine, axes, pairs(lambda owners, start: [(start + d, start +...  4.76 us
    ppermute x3, starting transfers between devices, over(): return lax.ppermute(totals, axis, [(s, s ^ step) for s in range(count)])  1.92 us
    ppermute x3, waiting for transfers between devices, over(): return lax.ppermute(totals, axis, [(s, s ^ step) for s in range(count)])  1.83 us
    pallas_call x1, Pallas kernels, per_device(): pl.pallas_call(functools.partial(finish_kernel, clip_count, head_count, e...  1.58 us
  transfers between devices with their start and end apart: 17, of which 8 were waited for; matrix products, arithmetic and copies ran while one was open for 0% of the time, Pallas kernels for 0%

profile of v4, /device:TPU:18, one launch (start us, length us, event | category | flops | bytes accessed | tf_op | source)
XLA Modules:
  0.0 64.1 jit_solution(15583557403412630529)
XLA Ops:
  0.6 1.5 %pack.1 = (bf16[6,128,128]{2,1,0:T(8,128)(2,1)S(1)}, bf16[6,128,128]{2,1,0:T(8,128)(2,1)S(1)}, bf16[6,128,128]{2,1,0:T(8,128)(2,1)S(1)}, bf16[6,128,128]{2,1,0:T...) custom-call(bf16[3,128,640]{2,1,0:T(8,128)(2,1)} %bitcast.3, ...), custom_call_target="tpu_custom_call" | custom-call | tf_op jit(solution)/shard_map/pack/pallas_call | solution.py:277
  2.1 2.2 %collective-permute-start = (bf16[6,128,128]{2,1,0:T(8,128)(2,1)S(1)}, bf16[6,128,128]{2,1,0:T(8,128)(2,1)S(1)}, u32[]{:S(2)}, u32[]{:S(2)}) collective-permute-start(bf16[6,128,128]{2,1,0:T(8,128)(2,1)S(1)} %get-tuple-element.21), channel_id=1, source_target_pairs={{4,0},{6,2},{0,4},{1,5},{3,7},{13,9},{14,10},{15,11},{9,13},{10,14... | collective-permute-start | bytes 589832 | tf_op jit(solution)/shard_map/ppermute | solution.py:293
  4.4 3.5 %collective-permute-start.1 = (bf16[6,128,128]{2,1,0:T(8,128)(2,1)S(1)}, bf16[6,128,128]{2,1,0:T(8,128)(2,1)S(1)}, u32[]{:S(2)}, u32[]{:S(2)}) collective-permute-start(bf16[6,128,128]{2,1,0:T(8,128)(2,1)S(1)} %get-tuple-element.22), channel_id=1, source_target_pairs={{3,0},{1,2},{7,4},{6,5},{4,7},{10,9},{9,10},{8,11},{14,13},{13,14}... | collective-permute-start | bytes 589832 | tf_op jit(solution)/shard_map/ppermute | solution.py:293
  7.9 1.3 %collective-permute-start.2 = (bf16[6,128,128]{2,1,0:T(8,128)(2,1)S(1)}, bf16[6,128,128]{2,1,0:T(8,128)(2,1)S(1)}, u32[]{:S(2)}, u32[]{:S(2)}) collective-permute-start(bf16[6,128,128]{2,1,0:T(8,128)(2,1)S(1)} %get-tuple-element.23), channel_id=1, source_target_pairs={{5,0},{7,2},{1,4},{0,5},{2,7},{12,9},{15,10},{14,11},{8,13},{11,14... | collective-permute-start | bytes 589832 | tf_op jit(solution)/shard_map/ppermute | solution.py:293
  9.2 4.4 %collective-permute-start.3 = (bf16[6,128,128]{2,1,0:T(8,128)(2,1)S(1)}, bf16[6,128,128]{2,1,0:T(8,128)(2,1)S(1)}, u32[]{:S(2)}, u32[]{:S(2)}) collective-permute-start(bf16[6,128,128]{2,1,0:T(8,128)(2,1)S(1)} %get-tuple-element.24), channel_id=1, source_target_pairs={{1,0},{3,2},{5,4},{4,5},{6,7},{8,9},{11,10},{10,11},{12,13},{15,14... | collective-permute-start | bytes 589832 | tf_op jit(solution)/shard_map/ppermute | solution.py:293
  13.5 1.3 %collective-permute-start.4 = (bf16[6,128,128]{2,1,0:T(8,128)(2,1)S(1)}, bf16[6,128,128]{2,1,0:T(8,128)(2,1)S(1)}, u32[]{:S(2)}, u32[]{:S(2)}) collective-permute-start(bf16[6,128,128]{2,1,0:T(8,128)(2,1)S(1)} %get-tuple-element.25), channel_id=1, source_target_pairs={{7,0},{5,2},{3,4},{2,5},{0,7},{14,9},{13,10},{12,11},{10,13},{9,14... | collective-permute-start | bytes 589832 | tf_op jit(solution)/shard_map/ppermute | solution.py:293
  14.8 4.0 %collective-permute-start.5 = (bf16[6,128,128]{2,1,0:T(8,128)(2,1)S(1)}, bf16[6,128,128]{2,1,0:T(8,128)(2,1)S(1)}, u32[]{:S(2)}, u32[]{:S(2)}) collective-permute-start(bf16[6,128,128]{2,1,0:T(8,128)(2,1)S(1)} %get-tuple-element.26), channel_id=1, source_target_pairs={{6,0},{4,2},{2,4},{3,5},{1,7},{15,9},{12,10},{13,11},{11,13},{8,14... | collective-permute-start | bytes 589832 | tf_op jit(solution)/shard_map/ppermute | solution.py:293
  18.9 1.3 %collective-permute-start.6 = (bf16[6,128,128]{2,1,0:T(8,128)(2,1)S(1)}, bf16[6,128,128]{2,1,0:T(8,128)(2,1)S(1)}, u32[]{:S(2)}, u32[]{:S(2)}) collective-permute-start(bf16[6,128,128]{2,1,0:T(8,128)(2,1)S(1)} %get-tuple-element.27), channel_id=1, source_target_pairs={{2,0},{0,2},{6,4},{7,5},{5,7},{11,9},{8,10},{9,11},{15,13},{12,14}... | collective-permute-start | bytes 589832 | tf_op jit(solution)/shard_map/ppermute | solution.py:293
  20.2 2.6 %collective-permute-done.2.refs_3_ = bf16[6,128,128]{2,1,0:T(8,128)(2,1)S(1)} collective-permute-done((bf16[6,128,128]{2,1,0:T(8,128)(2,1)S(1)}, bf16[6,128,128]{2,1,0:T(8,128)(2,1)S(1)}, u32[]{:S(2)}, u32[]{:S(2)}) %collective-permute-start.2) | collective-permute-done | bytes 196640 | tf_op jit(solution)/shard_map/ppermute | solution.py:293
  22.8 6.1 %collective-permute-done.4.refs_5_ = bf16[6,128,128]{2,1,0:T(8,128)(2,1)S(1)} collective-permute-done((bf16[6,128,128]{2,1,0:T(8,128)(2,1)S(1)}, bf16[6,128,128]{2,1,0:T(8,128)(2,1)S(1)}, u32[]{:S(2)}, u32[]{:S(2)}) %collective-permute-start.4) | collective-permute-done | bytes 196640 | tf_op jit(solution)/shard_map/ppermute | solution.py:293
  28.9 1.1 %collective-permute-done.5.refs_6_ = bf16[6,128,128]{2,1,0:T(8,128)(2,1)S(1)} collective-permute-done((bf16[6,128,128]{2,1,0:T(8,128)(2,1)S(1)}, bf16[6,128,128]{2,1,0:T(8,128)(2,1)S(1)}, u32[]{:S(2)}, u32[]{:S(2)}) %collective-permute-start.5) | collective-permute-done | bytes 196640 | tf_op jit(solution)/shard_map/ppermute | solution.py:293
  30.1 6.3 %heads.1 = (bf16[528,128]{1,0:T(8,128)(2,1)S(1)}, bf16[528,128]{1,0:T(8,128)(2,1)S(1)}, bf16[528,128]{1,0:T(8,128)(2,1)S(1)}, bf16[528,128]{1,0:T(8,128)(2,1)S(1...) custom-call(s32[4]{0:T(128)S(1)} %copy-done, ...), custom_call_target="tpu_custom_call" | custom-call | tf_op jit(solution)/shard_map/heads/pallas_call | solution.py:313
  36.4 1.3 %collective-permute-start.7 = (bf16[528,128]{1,0:T(8,128)(2,1)S(1)}, bf16[528,128]{1,0:T(8,128)(2,1)S(1)}, u32[]{:S(2)}, u32[]{:S(2)}) collective-permute-start(bf16[528,128]{1,0:T(8,128)(2,1)S(1)} %get-tuple-element.29), channel_id=1, source_target_pairs={{0,7},{2,5},{4,3},{5,2},{7,0},{9,14},{10,13},{11,12},{13,10},{14,9... | collective-permute-start | bytes 405512 | tf_op jit(solution)/shard_map/ppermute | solution.py:331
  37.7 3.1 %collective-permute-start.8 = (bf16[528,128]{1,0:T(8,128)(2,1)S(1)}, bf16[528,128]{1,0:T(8,128)(2,1)S(1)}, u32[]{:S(2)}, u32[]{:S(2)}) collective-permute-start(bf16[528,128]{1,0:T(8,128)(2,1)S(1)} %get-tuple-element.30), channel_id=1, source_target_pairs={{0,3},{2,1},{4,7},{5,6},{7,4},{9,10},{10,9},{11,8},{13,14},{14,13}... | collective-permute-start | bytes 405512 | tf_op jit(solution)/shard_map/ppermute | solution.py:331
  40.8 1.3 %collective-permute-start.9 = (bf16[528,128]{1,0:T(8,128)(2,1)S(1)}, bf16[528,128]{1,0:T(8,128)(2,1)S(1)}, u32[]{:S(2)}, u32[]{:S(2)}) collective-permute-start(bf16[528,128]{1,0:T(8,128)(2,1)S(1)} %get-tuple-element.31), channel_id=1, source_target_pairs={{0,5},{2,7},{4,1},{5,0},{7,2},{9,12},{10,15},{11,14},{13,8},{14,11... | collective-permute-start | bytes 405512 | tf_op jit(solution)/shard_map/ppermute | solution.py:331
  42.1 5.3 %collective-permute-start.10 = (bf16[528,128]{1,0:T(8,128)(2,1)S(1)}, bf16[528,128]{1,0:T(8,128)(2,1)S(1)}, u32[]{:S(2)}, u32[]{:S(2)}) collective-permute-start(bf16[528,128]{1,0:T(8,128)(2,1)S(1)} %get-tuple-element.32), channel_id=1, source_target_pairs={{0,4},{2,6},{4,0},{5,1},{7,3},{9,13},{10,14},{11,15},{13,9},{14,10... | collective-permute-start | bytes 405512 | tf_op jit(solution)/shard_map/ppermute | solution.py:331
  47.4 1.3 %collective-permute-start.11 = (bf16[528,128]{1,0:T(8,128)(2,1)S(1)}, bf16[528,128]{1,0:T(8,128)(2,1)S(1)}, u32[]{:S(2)}, u32[]{:S(2)}) collective-permute-start(bf16[528,128]{1,0:T(8,128)(2,1)S(1)} %get-tuple-element.33), channel_id=1, source_target_pairs={{0,2},{2,0},{4,6},{5,7},{7,5},{9,11},{10,8},{11,9},{13,15},{14,12}... | collective-permute-start | bytes 405512 | tf_op jit(solution)/shard_map/ppermute | solution.py:331
  48.8 3.1 %collective-permute-start.12 = (bf16[528,128]{1,0:T(8,128)(2,1)S(1)}, bf16[528,128]{1,0:T(8,128)(2,1)S(1)}, u32[]{:S(2)}, u32[]{:S(2)}) collective-permute-start(bf16[528,128]{1,0:T(8,128)(2,1)S(1)} %get-tuple-element.34), channel_id=1, source_target_pairs={{0,6},{2,4},{4,2},{5,3},{7,1},{9,15},{10,12},{11,13},{13,11},{14,8... | collective-permute-start | bytes 405512 | tf_op jit(solution)/shard_map/ppermute | solution.py:331
  51.9 2.1 %collective-permute-start.13 = (bf16[528,128]{1,0:T(8,128)(2,1)S(1)}, bf16[528,128]{1,0:T(8,128)(2,1)S(1)}, u32[]{:S(2)}, u32[]{:S(2)}) collective-permute-start(bf16[528,128]{1,0:T(8,128)(2,1)S(1)} %get-tuple-element.35), channel_id=1, source_target_pairs={{0,1},{2,3},{4,5},{5,4},{7,6},{9,8},{10,11},{11,10},{13,12},{14,15... | collective-permute-start | bytes 405512 | tf_op jit(solution)/shard_map/ppermute | solution.py:331
  54.0 2.0 %collective-permute-done.11.refs_5_.refs_9_ = bf16[528,128]{1,0:T(8,128)(2,1)S(1)} collective-permute-done((bf16[528,128]{1,0:T(8,128)(2,1)S(1)}, bf16[528,128]{1,0:T(8,128)(2,1)S(1)}, u32[]{:S(2)}, u32[]{:S(2)}) %collective-permute-start.11) | collective-permute-done | bytes 135200 | tf_op jit(solution)/shard_map/ppermute | solution.py:331
  56.1 2.6 %collective-permute-done.12.refs_6_.refs_10_ = bf16[528,128]{1,0:T(8,128)(2,1)S(1)} collective-permute-done((bf16[528,128]{1,0:T(8,128)(2,1)S(1)}, bf16[528,128]{1,0:T(8,128)(2,1)S(1)}, u32[]{:S(2)}, u32[]{:S(2)}) %collective-permute-start.12) | collective-permute-done | bytes 135200 | tf_op jit(solution)/shard_map/ppermute | solution.py:331
  59.6 1.1 %collective-permute-start.14 = (f32[8,128]{1,0:T(8,128)S(1)}, f32[8,128]{1,0:T(8,128)S(1)}, u32[]{:S(2)}, u32[]{:S(2)}) collective-permute-start(f32[8,128]{1,0:T(8,128)S(1)} %totals.1.refs_0_), channel_id=1, source_target_pairs={{0,8},{8,0},{16,24},{24,16},{1,9},{9,1},{17,25},{25,17},{2,10},{10... | collective-permute-start | bytes 12296 | tf_op jit(solution)/shard_map/ppermute | solution.py:356
  60.7 1.2 %collective-permute-done.16.refs_3_ = f32[8,128]{1,0:T(8,128)S(1)} collective-permute-done((f32[8,128]{1,0:T(8,128)S(1)}, f32[8,128]{1,0:T(8,128)S(1)}, u32[]{:S(2)}, u32[]{:S(2)}) %collective-permute-start.16) | collective-permute-done | bytes 4128 | tf_op jit(solution)/shard_map/ppermute | solution.py:356
  62.5 1.6 %finish.1 = (bf16[3,128,640]{2,1,0:T(8,128)(2,1)}, bf16[128,640]{1,0:T(8,128)(2,1)}) custom-call(s32[4]{0:T(128)S(1)} %copy-done, f32[8,128]{1,0:T(8,128)S(1)} %totals.1.refs_0_, f32[8,128]{1,0:T(8,128)S(1)} %collective-permute-done.14.refs_1_, f32[8,128]{1,0:T(8,128)S(1)} %collective-permute-done.15.refs_2_, f32[8,128]{1,0:T(8,128)S(1)} %collective-permute-done.16.refs_3_, ...), custom_call_target="tpu_custom_call" | custom-call | tf_op jit(solution)/shard_map/finish/pallas_call | solution.py:364
  (16 shorter events, 1.6 us)
Async XLA Ops:
  2.1 12.7 %collective-permute-start = (bf16[6,128,128]{2,1,0:T(8,128)(2,1)S(1)}, bf16[6,128,128]{2,1,0:T(8,128)(2,1)S(1)}, u32[]{:S(2)}, u32[]{:S(2)}) collective-permute-start(bf16[6,128,128]{2,1,0:T(8,128)(2,1)S(1)} %get-tuple-element.21), channel_id=1, source_target_pairs={{4,0},{6,2},{0,4},{1,5},{3,7},{13,9},{14,10},{15,11},{9,13},{10,14... | collective-permute-start | bytes 589832 | tf_op jit(solution)/shard_map/ppermute | solution.py:293
  4.4 14.5 %collective-permute-start.1 = (bf16[6,128,128]{2,1,0:T(8,128)(2,1)S(1)}, bf16[6,128,128]{2,1,0:T(8,128)(2,1)S(1)}, u32[]{:S(2)}, u32[]{:S(2)}) collective-permute-start(bf16[6,128,128]{2,1,0:T(8,128)(2,1)S(1)} %get-tuple-element.22), channel_id=1, source_target_pairs={{3,0},{1,2},{7,4},{6,5},{4,7},{10,9},{9,10},{8,11},{14,13},{13,14}... | collective-permute-start | bytes 589832 | tf_op jit(solution)/shard_map/ppermute | solution.py:293
  7.9 15.0 %collective-permute-start.2 = (bf16[6,128,128]{2,1,0:T(8,128)(2,1)S(1)}, bf16[6,128,128]{2,1,0:T(8,128)(2,1)S(1)}, u32[]{:S(2)}, u32[]{:S(2)}) collective-permute-start(bf16[6,128,128]{2,1,0:T(8,128)(2,1)S(1)} %get-tuple-element.23), channel_id=1, source_target_pairs={{5,0},{7,2},{1,4},{0,5},{2,7},{12,9},{15,10},{14,11},{8,13},{11,14... | collective-permute-start | bytes 589832 | tf_op jit(solution)/shard_map/ppermute | solution.py:293
  9.2 13.7 %collective-permute-start.3 = (bf16[6,128,128]{2,1,0:T(8,128)(2,1)S(1)}, bf16[6,128,128]{2,1,0:T(8,128)(2,1)S(1)}, u32[]{:S(2)}, u32[]{:S(2)}) collective-permute-start(bf16[6,128,128]{2,1,0:T(8,128)(2,1)S(1)} %get-tuple-element.24), channel_id=1, source_target_pairs={{1,0},{3,2},{5,4},{4,5},{6,7},{8,9},{11,10},{10,11},{12,13},{15,14... | collective-permute-start | bytes 589832 | tf_op jit(solution)/shard_map/ppermute | solution.py:293
  13.5 15.4 %collective-permute-start.4 = (bf16[6,128,128]{2,1,0:T(8,128)(2,1)S(1)}, bf16[6,128,128]{2,1,0:T(8,128)(2,1)S(1)}, u32[]{:S(2)}, u32[]{:S(2)}) collective-permute-start(bf16[6,128,128]{2,1,0:T(8,128)(2,1)S(1)} %get-tuple-element.25), channel_id=1, source_target_pairs={{7,0},{5,2},{3,4},{2,5},{0,7},{14,9},{13,10},{12,11},{10,13},{9,14... | collective-permute-start | bytes 589832 | tf_op jit(solution)/shard_map/ppermute | solution.py:293
  14.8 15.2 %collective-permute-start.5 = (bf16[6,128,128]{2,1,0:T(8,128)(2,1)S(1)}, bf16[6,128,128]{2,1,0:T(8,128)(2,1)S(1)}, u32[]{:S(2)}, u32[]{:S(2)}) collective-permute-start(bf16[6,128,128]{2,1,0:T(8,128)(2,1)S(1)} %get-tuple-element.26), channel_id=1, source_target_pairs={{6,0},{4,2},{2,4},{3,5},{1,7},{15,9},{12,10},{13,11},{11,13},{8,14... | collective-permute-start | bytes 589832 | tf_op jit(solution)/shard_map/ppermute | solution.py:293
  18.9 11.2 %copy-start = (s32[4]{0:T(128)S(1)}, s32[4]{0:T(128)}, u32[]{:S(2)}) copy-start(s32[4]{0:T(128)} %lengths_ref.3) | copy-start | bytes 52
  18.9 11.2 %collective-permute-start.6 = (bf16[6,128,128]{2,1,0:T(8,128)(2,1)S(1)}, bf16[6,128,128]{2,1,0:T(8,128)(2,1)S(1)}, u32[]{:S(2)}, u32[]{:S(2)}) collective-permute-start(bf16[6,128,128]{2,1,0:T(8,128)(2,1)S(1)} %get-tuple-element.27), channel_id=1, source_target_pairs={{2,0},{0,2},{6,4},{7,5},{5,7},{11,9},{8,10},{9,11},{15,13},{12,14}... | collective-permute-start | bytes 589832 | tf_op jit(solution)/shard_map/ppermute | solution.py:293
  36.4 12.4 %collective-permute-start.7 = (bf16[528,128]{1,0:T(8,128)(2,1)S(1)}, bf16[528,128]{1,0:T(8,128)(2,1)S(1)}, u32[]{:S(2)}, u32[]{:S(2)}) collective-permute-start(bf16[528,128]{1,0:T(8,128)(2,1)S(1)} %get-tuple-element.29), channel_id=1, source_target_pairs={{0,7},{2,5},{4,3},{5,2},{7,0},{9,14},{10,13},{11,12},{13,10},{14,9... | collective-permute-start | bytes 405512 | tf_op jit(solution)/shard_map/ppermute | solution.py:331
  37.7 14.2 %collective-permute-start.8 = (bf16[528,128]{1,0:T(8,128)(2,1)S(1)}, bf16[528,128]{1,0:T(8,128)(2,1)S(1)}, u32[]{:S(2)}, u32[]{:S(2)}) collective-permute-start(bf16[528,128]{1,0:T(8,128)(2,1)S(1)} %get-tuple-element.30), channel_id=1, source_target_pairs={{0,3},{2,1},{4,7},{5,6},{7,4},{9,10},{10,9},{11,8},{13,14},{14,13}... | collective-permute-start | bytes 405512 | tf_op jit(solution)/shard_map/ppermute | solution.py:331
  40.8 13.2 %collective-permute-start.9 = (bf16[528,128]{1,0:T(8,128)(2,1)S(1)}, bf16[528,128]{1,0:T(8,128)(2,1)S(1)}, u32[]{:S(2)}, u32[]{:S(2)}) collective-permute-start(bf16[528,128]{1,0:T(8,128)(2,1)S(1)} %get-tuple-element.31), channel_id=1, source_target_pairs={{0,5},{2,7},{4,1},{5,0},{7,2},{9,12},{10,15},{11,14},{13,8},{14,11... | collective-permute-start | bytes 405512 | tf_op jit(solution)/shard_map/ppermute | solution.py:331
  42.1 11.9 %collective-permute-start.10 = (bf16[528,128]{1,0:T(8,128)(2,1)S(1)}, bf16[528,128]{1,0:T(8,128)(2,1)S(1)}, u32[]{:S(2)}, u32[]{:S(2)}) collective-permute-start(bf16[528,128]{1,0:T(8,128)(2,1)S(1)} %get-tuple-element.32), channel_id=1, source_target_pairs={{0,4},{2,6},{4,0},{5,1},{7,3},{9,13},{10,14},{11,15},{13,9},{14,10... | collective-permute-start | bytes 405512 | tf_op jit(solution)/shard_map/ppermute | solution.py:331
  47.4 8.6 %collective-permute-start.11 = (bf16[528,128]{1,0:T(8,128)(2,1)S(1)}, bf16[528,128]{1,0:T(8,128)(2,1)S(1)}, u32[]{:S(2)}, u32[]{:S(2)}) collective-permute-start(bf16[528,128]{1,0:T(8,128)(2,1)S(1)} %get-tuple-element.33), channel_id=1, source_target_pairs={{0,2},{2,0},{4,6},{5,7},{7,5},{9,11},{10,8},{11,9},{13,15},{14,12}... | collective-permute-start | bytes 405512 | tf_op jit(solution)/shard_map/ppermute | solution.py:331
  48.8 9.9 %collective-permute-start.12 = (bf16[528,128]{1,0:T(8,128)(2,1)S(1)}, bf16[528,128]{1,0:T(8,128)(2,1)S(1)}, u32[]{:S(2)}, u32[]{:S(2)}) collective-permute-start(bf16[528,128]{1,0:T(8,128)(2,1)S(1)} %get-tuple-element.34), channel_id=1, source_target_pairs={{0,6},{2,4},{4,2},{5,3},{7,1},{9,15},{10,12},{11,13},{13,11},{14,8... | collective-permute-start | bytes 405512 | tf_op jit(solution)/shard_map/ppermute | solution.py:331
  51.9 6.9 %collective-permute-start.13 = (bf16[528,128]{1,0:T(8,128)(2,1)S(1)}, bf16[528,128]{1,0:T(8,128)(2,1)S(1)}, u32[]{:S(2)}, u32[]{:S(2)}) collective-permute-start(bf16[528,128]{1,0:T(8,128)(2,1)S(1)} %get-tuple-element.35), channel_id=1, source_target_pairs={{0,1},{2,3},{4,5},{5,4},{7,6},{9,8},{10,11},{11,10},{13,12},{14,15... | collective-permute-start | bytes 405512 | tf_op jit(solution)/shard_map/ppermute | solution.py:331
  58.8 3.1 %collective-permute-start.16 = (f32[8,128]{1,0:T(8,128)S(1)}, f32[8,128]{1,0:T(8,128)S(1)}, u32[]{:S(2)}, u32[]{:S(2)}) collective-permute-start(f32[8,128]{1,0:T(8,128)S(1)} %totals.1.refs_0_), channel_id=1, source_target_pairs={{0,24},{8,16},{16,8},{24,0},{1,25},{9,17},{17,9},{25,1},{2,26},{10... | collective-permute-start | bytes 12296 | tf_op jit(solution)/shard_map/ppermute | solution.py:356
  58.9 3.7 %collective-permute-start.15 = (f32[8,128]{1,0:T(8,128)S(1)}, f32[8,128]{1,0:T(8,128)S(1)}, u32[]{:S(2)}, u32[]{:S(2)}) collective-permute-start(f32[8,128]{1,0:T(8,128)S(1)} %totals.1.refs_0_), channel_id=1, source_target_pairs={{0,16},{8,24},{16,0},{24,8},{1,17},{9,25},{17,1},{25,9},{2,18},{10... | collective-permute-start | bytes 12296 | tf_op jit(solution)/shard_map/ppermute | solution.py:356
  59.6 2.9 %collective-permute-start.14 = (f32[8,128]{1,0:T(8,128)S(1)}, f32[8,128]{1,0:T(8,128)S(1)}, u32[]{:S(2)}, u32[]{:S(2)}) collective-permute-start(f32[8,128]{1,0:T(8,128)S(1)} %totals.1.refs_0_), channel_id=1, source_target_pairs={{0,8},{8,0},{16,24},{24,16},{1,9},{9,1},{17,25},{25,17},{2,10},{10... | collective-permute-start | bytes 12296 | tf_op jit(solution)/shard_map/ppermute | solution.py:356

commit v5 on v4

--- a/solution.py
+++ b/solution.py
@@ -106,10 +106,9 @@
                 parts[i] = jnp.where((key >= start) & (key < start + length), parts[i], -jnp.inf)
             return jnp.concatenate(parts, axis=axis)
 
-        def softmax(scores, axis):
+        def powers(scores, axis):
             peak = jnp.max(scores, axis=axis, keepdims=True)
-            exponent = jnp.exp2((scores - peak) * to_log2)
-            return exponent, 1.0 / jnp.sum(exponent, axis=axis, keepdims=True)
+            return jnp.exp2((scores - peak) * to_log2)
 
         def product(a, b):
             return lax.dot_general(a, b, ROWS_BY_ROWS, preferred_element_type=F32)
@@ -119,11 +118,13 @@
             width = min(QUERY_TILE, size - begin)
             mine = pl.ds(first + begin, width)
             columns = slice(begin, begin + width)
-            exponent, inverse = softmax(masked(product(data[3, mine, :], data[4, window, :]), 1), 1)
-            target = jnp.dot(exponent.astype(BF16), data[5, window, :], preferred_element_type=F32)
-            target = target * inverse
-            exponent, inverse = softmax(masked(product(data[1, window, :], data[0, mine, :]), 0), 0)
+            exponent = powers(masked(product(data[3, mine, :], data[4, window, :]), 1), 1)
+            values = jnp.concatenate([data[5, window, :], jnp.ones((size, HS), BF16)], axis=1)
+            both = jnp.dot(exponent.astype(BF16), values, preferred_element_type=F32)
+            target = both[:, :HS] * (1.0 / both[:, HS:])
+            exponent = powers(masked(product(data[1, window, :], data[0, mine, :]), 0), 0)
             weights = exponent.astype(BF16)
+            inverse = 1.0 / jnp.sum(exponent, axis=0, keepdims=True)
             student = jnp.dot(turned[1, :, window], weights, preferred_element_type=F32) * inverse
             diff = jnp.where(inside[:, columns], student - target.T, 0.0)
             squares = jnp.sum(diff * diff, axis=1, keepdims=True)

time: 65.3 us -> 64.7 us (level)
  no operation moved by 1% of the time
where the time goes in v5:
time: 64.7 us; the launch traced here: 63.8 us
  starting transfers between devices  37.5 us (58%)
  waiting for transfers between devices  16.5 us (26%)
  Pallas kernels  9.06 us (14%)
  between operations  0.83 us (1%)
    ppermute x7, starting transfers between devices, per_device(): lax.ppermute(mine, axes, pairs(lambda owners, start: [(start + (d ^ k), s...  18 us
    ppermute x7, starting transfers between devices, per_device(): lax.ppermute(mine, axes, pairs(lambda owners, start: [(start + d, start +...  17.6 us
    ppermute x7, waiting for transfers between devices, per_device(): lax.ppermute(mine, axes, pairs(lambda owners, start: [(start + (d ^ k), s...  9.88 us
    pallas_call x1, Pallas kernels, per_device(): pl.pallas_call(functools.partial(head_kernel, clip_count, extra), out_sha...  6 us
    ppermute x7, waiting for transfers between devices, per_device(): lax.ppermute(mine, axes, pairs(lambda owners, start: [(start + d, start +...  4.76 us
    ppermute x3, starting transfers between devices, over(): return lax.ppermute(totals, axis, [(s, s ^ step) for s in range(count)])  1.92 us
    ppermute x3, waiting for transfers between devices, over(): return lax.ppermute(totals, axis, [(s, s ^ step) for s in range(count)])  1.83 us
    pallas_call x1, Pallas kernels, per_device(): pl.pallas_call(functools.partial(finish_kernel, clip_count, head_count, e...  1.58 us
  transfers between devices with their start and end apart: 17, of which 8 were waited for; matrix products, arithmetic and copies ran while one was open for 0% of the time, Pallas kernels for 0%

profile of v5, /device:TPU:18, one launch (start us, length us, event | category | flops | bytes accessed | tf_op | source)
XLA Modules:
  0.0 63.8 jit_solution(3771321189779148883)
XLA Ops:
  0.6 1.5 %pack.1 = (bf16[6,128,128]{2,1,0:T(8,128)(2,1)S(1)}, bf16[6,128,128]{2,1,0:T(8,128)(2,1)S(1)}, bf16[6,128,128]{2,1,0:T(8,128)(2,1)S(1)}, bf16[6,128,128]{2,1,0:T...) custom-call(bf16[3,128,640]{2,1,0:T(8,128)(2,1)} %bitcast.3, ...), custom_call_target="tpu_custom_call" | custom-call | tf_op jit(solution)/shard_map/pack/pallas_call | solution.py:278
  2.1 2.2 %collective-permute-start = (bf16[6,128,128]{2,1,0:T(8,128)(2,1)S(1)}, bf16[6,128,128]{2,1,0:T(8,128)(2,1)S(1)}, u32[]{:S(2)}, u32[]{:S(2)}) collective-permute-start(bf16[6,128,128]{2,1,0:T(8,128)(2,1)S(1)} %get-tuple-element.21), channel_id=1, source_target_pairs={{4,0},{6,2},{0,4},{1,5},{3,7},{13,9},{14,10},{15,11},{9,13},{10,14... | collective-permute-start | bytes 589832 | tf_op jit(solution)/shard_map/ppermute | solution.py:294
  4.4 3.5 %collective-permute-start.1 = (bf16[6,128,128]{2,1,0:T(8,128)(2,1)S(1)}, bf16[6,128,128]{2,1,0:T(8,128)(2,1)S(1)}, u32[]{:S(2)}, u32[]{:S(2)}) collective-permute-start(bf16[6,128,128]{2,1,0:T(8,128)(2,1)S(1)} %get-tuple-element.22), channel_id=1, source_target_pairs={{3,0},{1,2},{7,4},{6,5},{4,7},{10,9},{9,10},{8,11},{14,13},{13,14}... | collective-permute-start | bytes 589832 | tf_op jit(solution)/shard_map/ppermute | solution.py:294
  7.9 1.3 %collective-permute-start.2 = (bf16[6,128,128]{2,1,0:T(8,128)(2,1)S(1)}, bf16[6,128,128]{2,1,0:T(8,128)(2,1)S(1)}, u32[]{:S(2)}, u32[]{:S(2)}) collective-permute-start(bf16[6,128,128]{2,1,0:T(8,128)(2,1)S(1)} %get-tuple-element.23), channel_id=1, source_target_pairs={{5,0},{7,2},{1,4},{0,5},{2,7},{12,9},{15,10},{14,11},{8,13},{11,14... | collective-permute-start | bytes 589832 | tf_op jit(solution)/shard_map/ppermute | solution.py:294
  9.2 4.4 %collective-permute-start.3 = (bf16[6,128,128]{2,1,0:T(8,128)(2,1)S(1)}, bf16[6,128,128]{2,1,0:T(8,128)(2,1)S(1)}, u32[]{:S(2)}, u32[]{:S(2)}) collective-permute-start(bf16[6,128,128]{2,1,0:T(8,128)(2,1)S(1)} %get-tuple-element.24), channel_id=1, source_target_pairs={{1,0},{3,2},{5,4},{4,5},{6,7},{8,9},{11,10},{10,11},{12,13},{15,14... | collective-permute-start | bytes 589832 | tf_op jit(solution)/shard_map/ppermute | solution.py:294
  13.5 1.3 %collective-permute-start.4 = (bf16[6,128,128]{2,1,0:T(8,128)(2,1)S(1)}, bf16[6,128,128]{2,1,0:T(8,128)(2,1)S(1)}, u32[]{:S(2)}, u32[]{:S(2)}) collective-permute-start(bf16[6,128,128]{2,1,0:T(8,128)(2,1)S(1)} %get-tuple-element.25), channel_id=1, source_target_pairs={{7,0},{5,2},{3,4},{2,5},{0,7},{14,9},{13,10},{12,11},{10,13},{9,14... | collective-permute-start | bytes 589832 | tf_op jit(solution)/shard_map/ppermute | solution.py:294
  14.8 4.0 %collective-permute-start.5 = (bf16[6,128,128]{2,1,0:T(8,128)(2,1)S(1)}, bf16[6,128,128]{2,1,0:T(8,128)(2,1)S(1)}, u32[]{:S(2)}, u32[]{:S(2)}) collective-permute-start(bf16[6,128,128]{2,1,0:T(8,128)(2,1)S(1)} %get-tuple-element.26), channel_id=1, source_target_pairs={{6,0},{4,2},{2,4},{3,5},{1,7},{15,9},{12,10},{13,11},{11,13},{8,14... | collective-permute-start | bytes 589832 | tf_op jit(solution)/shard_map/ppermute | solution.py:294
  18.9 1.3 %collective-permute-start.6 = (bf16[6,128,128]{2,1,0:T(8,128)(2,1)S(1)}, bf16[6,128,128]{2,1,0:T(8,128)(2,1)S(1)}, u32[]{:S(2)}, u32[]{:S(2)}) collective-permute-start(bf16[6,128,128]{2,1,0:T(8,128)(2,1)S(1)} %get-tuple-element.27), channel_id=1, source_target_pairs={{2,0},{0,2},{6,4},{7,5},{5,7},{11,9},{8,10},{9,11},{15,13},{12,14}... | collective-permute-start | bytes 589832 | tf_op jit(solution)/shard_map/ppermute | solution.py:294
  20.2 2.6 %collective-permute-done.2.refs_3_ = bf16[6,128,128]{2,1,0:T(8,128)(2,1)S(1)} collective-permute-done((bf16[6,128,128]{2,1,0:T(8,128)(2,1)S(1)}, bf16[6,128,128]{2,1,0:T(8,128)(2,1)S(1)}, u32[]{:S(2)}, u32[]{:S(2)}) %collective-permute-start.2) | collective-permute-done | bytes 196640 | tf_op jit(solution)/shard_map/ppermute | solution.py:294
  22.8 6.1 %collective-permute-done.4.refs_5_ = bf16[6,128,128]{2,1,0:T(8,128)(2,1)S(1)} collective-permute-done((bf16[6,128,128]{2,1,0:T(8,128)(2,1)S(1)}, bf16[6,128,128]{2,1,0:T(8,128)(2,1)S(1)}, u32[]{:S(2)}, u32[]{:S(2)}) %collective-permute-start.4) | collective-permute-done | bytes 196640 | tf_op jit(solution)/shard_map/ppermute | solution.py:294
  28.9 1.1 %collective-permute-done.5.refs_6_ = bf16[6,128,128]{2,1,0:T(8,128)(2,1)S(1)} collective-permute-done((bf16[6,128,128]{2,1,0:T(8,128)(2,1)S(1)}, bf16[6,128,128]{2,1,0:T(8,128)(2,1)S(1)}, u32[]{:S(2)}, u32[]{:S(2)}) %collective-permute-start.5) | collective-permute-done | bytes 196640 | tf_op jit(solution)/shard_map/ppermute | solution.py:294
  30.1 6.0 %heads.1 = (bf16[528,128]{1,0:T(8,128)(2,1)S(1)}, bf16[528,128]{1,0:T(8,128)(2,1)S(1)}, bf16[528,128]{1,0:T(8,128)(2,1)S(1)}, bf16[528,128]{1,0:T(8,128)(2,1)S(1...) custom-call(s32[4]{0:T(128)S(1)} %copy-done, ...), custom_call_target="tpu_custom_call" | custom-call | tf_op jit(solution)/shard_map/heads/pallas_call | solution.py:314
  36.1 1.3 %collective-permute-start.7 = (bf16[528,128]{1,0:T(8,128)(2,1)S(1)}, bf16[528,128]{1,0:T(8,128)(2,1)S(1)}, u32[]{:S(2)}, u32[]{:S(2)}) collective-permute-start(bf16[528,128]{1,0:T(8,128)(2,1)S(1)} %get-tuple-element.29), channel_id=1, source_target_pairs={{0,7},{2,5},{4,3},{5,2},{7,0},{9,14},{10,13},{11,12},{13,10},{14,9... | collective-permute-start | bytes 405512 | tf_op jit(solution)/shard_map/ppermute | solution.py:332
  37.4 3.1 %collective-permute-start.8 = (bf16[528,128]{1,0:T(8,128)(2,1)S(1)}, bf16[528,128]{1,0:T(8,128)(2,1)S(1)}, u32[]{:S(2)}, u32[]{:S(2)}) collective-permute-start(bf16[528,128]{1,0:T(8,128)(2,1)S(1)} %get-tuple-element.30), channel_id=1, source_target_pairs={{0,3},{2,1},{4,7},{5,6},{7,4},{9,10},{10,9},{11,8},{13,14},{14,13}... | collective-permute-start | bytes 405512 | tf_op jit(solution)/shard_map/ppermute | solution.py:332
  40.5 1.3 %collective-permute-start.9 = (bf16[528,128]{1,0:T(8,128)(2,1)S(1)}, bf16[528,128]{1,0:T(8,128)(2,1)S(1)}, u32[]{:S(2)}, u32[]{:S(2)}) collective-permute-start(bf16[528,128]{1,0:T(8,128)(2,1)S(1)} %get-tuple-element.31), channel_id=1, source_target_pairs={{0,5},{2,7},{4,1},{5,0},{7,2},{9,12},{10,15},{11,14},{13,8},{14,11... | collective-permute-start | bytes 405512 | tf_op jit(solution)/shard_map/ppermute | solution.py:332
  41.8 5.3 %collective-permute-start.10 = (bf16[528,128]{1,0:T(8,128)(2,1)S(1)}, bf16[528,128]{1,0:T(8,128)(2,1)S(1)}, u32[]{:S(2)}, u32[]{:S(2)}) collective-permute-start(bf16[528,128]{1,0:T(8,128)(2,1)S(1)} %get-tuple-element.32), channel_id=1, source_target_pairs={{0,4},{2,6},{4,0},{5,1},{7,3},{9,13},{10,14},{11,15},{13,9},{14,10... | collective-permute-start | bytes 405512 | tf_op jit(solution)/shard_map/ppermute | solution.py:332
  47.1 1.3 %collective-permute-start.11 = (bf16[528,128]{1,0:T(8,128)(2,1)S(1)}, bf16[528,128]{1,0:T(8,128)(2,1)S(1)}, u32[]{:S(2)}, u32[]{:S(2)}) collective-permute-start(bf16[528,128]{1,0:T(8,128)(2,1)S(1)} %get-tuple-element.33), channel_id=1, source_target_pairs={{0,2},{2,0},{4,6},{5,7},{7,5},{9,11},{10,8},{11,9},{13,15},{14,12}... | collective-permute-start | bytes 405512 | tf_op jit(solution)/shard_map/ppermute | solution.py:332
  48.5 3.1 %collective-permute-start.12 = (bf16[528,128]{1,0:T(8,128)(2,1)S(1)}, bf16[528,128]{1,0:T(8,128)(2,1)S(1)}, u32[]{:S(2)}, u32[]{:S(2)}) collective-permute-start(bf16[528,128]{1,0:T(8,128)(2,1)S(1)} %get-tuple-element.34), channel_id=1, source_target_pairs={{0,6},{2,4},{4,2},{5,3},{7,1},{9,15},{10,12},{11,13},{13,11},{14,8... | collective-permute-start | bytes 405512 | tf_op jit(solution)/shard_map/ppermute | solution.py:332
  51.6 2.1 %collective-permute-start.13 = (bf16[528,128]{1,0:T(8,128)(2,1)S(1)}, bf16[528,128]{1,0:T(8,128)(2,1)S(1)}, u32[]{:S(2)}, u32[]{:S(2)}) collective-permute-start(bf16[528,128]{1,0:T(8,128)(2,1)S(1)} %get-tuple-element.35), channel_id=1, source_target_pairs={{0,1},{2,3},{4,5},{5,4},{7,6},{9,8},{10,11},{11,10},{13,12},{14,15... | collective-permute-start | bytes 405512 | tf_op jit(solution)/shard_map/ppermute | solution.py:332
  53.7 2.0 %collective-permute-done.11.refs_5_.refs_9_ = bf16[528,128]{1,0:T(8,128)(2,1)S(1)} collective-permute-done((bf16[528,128]{1,0:T(8,128)(2,1)S(1)}, bf16[528,128]{1,0:T(8,128)(2,1)S(1)}, u32[]{:S(2)}, u32[]{:S(2)}) %collective-permute-start.11) | collective-permute-done | bytes 135200 | tf_op jit(solution)/shard_map/ppermute | solution.py:332
  55.8 2.6 %collective-permute-done.12.refs_6_.refs_10_ = bf16[528,128]{1,0:T(8,128)(2,1)S(1)} collective-permute-done((bf16[528,128]{1,0:T(8,128)(2,1)S(1)}, bf16[528,128]{1,0:T(8,128)(2,1)S(1)}, u32[]{:S(2)}, u32[]{:S(2)}) %collective-permute-start.12) | collective-permute-done | bytes 135200 | tf_op jit(solution)/shard_map/ppermute | solution.py:332
  59.3 1.1 %collective-permute-start.14 = (f32[8,128]{1,0:T(8,128)S(1)}, f32[8,128]{1,0:T(8,128)S(1)}, u32[]{:S(2)}, u32[]{:S(2)}) collective-permute-start(f32[8,128]{1,0:T(8,128)S(1)} %totals.1.refs_0_), channel_id=1, source_target_pairs={{0,8},{8,0},{16,24},{24,16},{1,9},{9,1},{17,25},{25,17},{2,10},{10... | collective-permute-start | bytes 12296 | tf_op jit(solution)/shard_map/ppermute | solution.py:357
  60.4 1.2 %collective-permute-done.16.refs_3_ = f32[8,128]{1,0:T(8,128)S(1)} collective-permute-done((f32[8,128]{1,0:T(8,128)S(1)}, f32[8,128]{1,0:T(8,128)S(1)}, u32[]{:S(2)}, u32[]{:S(2)}) %collective-permute-start.16) | collective-permute-done | bytes 4128 | tf_op jit(solution)/shard_map/ppermute | solution.py:357
  62.2 1.6 %finish.1 = (bf16[3,128,640]{2,1,0:T(8,128)(2,1)}, bf16[128,640]{1,0:T(8,128)(2,1)}) custom-call(s32[4]{0:T(128)S(1)} %copy-done, f32[8,128]{1,0:T(8,128)S(1)} %totals.1.refs_0_, f32[8,128]{1,0:T(8,128)S(1)} %collective-permute-done.14.refs_1_, f32[8,128]{1,0:T(8,128)S(1)} %collective-permute-done.15.refs_2_, f32[8,128]{1,0:T(8,128)S(1)} %collective-permute-done.16.refs_3_, ...), custom_call_target="tpu_custom_call" | custom-call | tf_op jit(solution)/shard_map/finish/pallas_call | solution.py:365
  (16 shorter events, 1.6 us)
Async XLA Ops:
  2.1 12.7 %collective-permute-start = (bf16[6,128,128]{2,1,0:T(8,128)(2,1)S(1)}, bf16[6,128,128]{2,1,0:T(8,128)(2,1)S(1)}, u32[]{:S(2)}, u32[]{:S(2)}) collective-permute-start(bf16[6,128,128]{2,1,0:T(8,128)(2,1)S(1)} %get-tuple-element.21), channel_id=1, source_target_pairs={{4,0},{6,2},{0,4},{1,5},{3,7},{13,9},{14,10},{15,11},{9,13},{10,14... | collective-permute-start | bytes 589832 | tf_op jit(solution)/shard_map/ppermute | solution.py:294
  4.4 14.5 %collective-permute-start.1 = (bf16[6,128,128]{2,1,0:T(8,128)(2,1)S(1)}, bf16[6,128,128]{2,1,0:T(8,128)(2,1)S(1)}, u32[]{:S(2)}, u32[]{:S(2)}) collective-permute-start(bf16[6,128,128]{2,1,0:T(8,128)(2,1)S(1)} %get-tuple-element.22), channel_id=1, source_target_pairs={{3,0},{1,2},{7,4},{6,5},{4,7},{10,9},{9,10},{8,11},{14,13},{13,14}... | collective-permute-start | bytes 589832 | tf_op jit(solution)/shard_map/ppermute | solution.py:294
  7.9 15.0 %collective-permute-start.2 = (bf16[6,128,128]{2,1,0:T(8,128)(2,1)S(1)}, bf16[6,128,128]{2,1,0:T(8,128)(2,1)S(1)}, u32[]{:S(2)}, u32[]{:S(2)}) collective-permute-start(bf16[6,128,128]{2,1,0:T(8,128)(2,1)S(1)} %get-tuple-element.23), channel_id=1, source_target_pairs={{5,0},{7,2},{1,4},{0,5},{2,7},{12,9},{15,10},{14,11},{8,13},{11,14... | collective-permute-start | bytes 589832 | tf_op jit(solution)/shard_map/ppermute | solution.py:294
  9.2 13.7 %collective-permute-start.3 = (bf16[6,128,128]{2,1,0:T(8,128)(2,1)S(1)}, bf16[6,128,128]{2,1,0:T(8,128)(2,1)S(1)}, u32[]{:S(2)}, u32[]{:S(2)}) collective-permute-start(bf16[6,128,128]{2,1,0:T(8,128)(2,1)S(1)} %get-tuple-element.24), channel_id=1, source_target_pairs={{1,0},{3,2},{5,4},{4,5},{6,7},{8,9},{11,10},{10,11},{12,13},{15,14... | collective-permute-start | bytes 589832 | tf_op jit(solution)/shard_map/ppermute | solution.py:294
  13.5 15.4 %collective-permute-start.4 = (bf16[6,128,128]{2,1,0:T(8,128)(2,1)S(1)}, bf16[6,128,128]{2,1,0:T(8,128)(2,1)S(1)}, u32[]{:S(2)}, u32[]{:S(2)}) collective-permute-start(bf16[6,128,128]{2,1,0:T(8,128)(2,1)S(1)} %get-tuple-element.25), channel_id=1, source_target_pairs={{7,0},{5,2},{3,4},{2,5},{0,7},{14,9},{13,10},{12,11},{10,13},{9,14... | collective-permute-start | bytes 589832 | tf_op jit(solution)/shard_map/ppermute | solution.py:294
  14.8 15.2 %collective-permute-start.5 = (bf16[6,128,128]{2,1,0:T(8,128)(2,1)S(1)}, bf16[6,128,128]{2,1,0:T(8,128)(2,1)S(1)}, u32[]{:S(2)}, u32[]{:S(2)}) collective-permute-start(bf16[6,128,128]{2,1,0:T(8,128)(2,1)S(1)} %get-tuple-element.26), channel_id=1, source_target_pairs={{6,0},{4,2},{2,4},{3,5},{1,7},{15,9},{12,10},{13,11},{11,13},{8,14... | collective-permute-start | bytes 589832 | tf_op jit(solution)/shard_map/ppermute | solution.py:294
  18.9 11.2 %copy-start = (s32[4]{0:T(128)S(1)}, s32[4]{0:T(128)}, u32[]{:S(2)}) copy-start(s32[4]{0:T(128)} %lengths_ref.3) | copy-start | bytes 52
  18.9 11.2 %collective-permute-start.6 = (bf16[6,128,128]{2,1,0:T(8,128)(2,1)S(1)}, bf16[6,128,128]{2,1,0:T(8,128)(2,1)S(1)}, u32[]{:S(2)}, u32[]{:S(2)}) collective-permute-start(bf16[6,128,128]{2,1,0:T(8,128)(2,1)S(1)} %get-tuple-element.27), channel_id=1, source_target_pairs={{2,0},{0,2},{6,4},{7,5},{5,7},{11,9},{8,10},{9,11},{15,13},{12,14}... | collective-permute-start | bytes 589832 | tf_op jit(solution)/shard_map/ppermute | solution.py:294
  36.1 12.4 %collective-permute-start.7 = (bf16[528,128]{1,0:T(8,128)(2,1)S(1)}, bf16[528,128]{1,0:T(8,128)(2,1)S(1)}, u32[]{:S(2)}, u32[]{:S(2)}) collective-permute-start(bf16[528,128]{1,0:T(8,128)(2,1)S(1)} %get-tuple-element.29), channel_id=1, source_target_pairs={{0,7},{2,5},{4,3},{5,2},{7,0},{9,14},{10,13},{11,12},{13,10},{14,9... | collective-permute-start | bytes 405512 | tf_op jit(solution)/shard_map/ppermute | solution.py:332
  37.4 14.2 %collective-permute-start.8 = (bf16[528,128]{1,0:T(8,128)(2,1)S(1)}, bf16[528,128]{1,0:T(8,128)(2,1)S(1)}, u32[]{:S(2)}, u32[]{:S(2)}) collective-permute-start(bf16[528,128]{1,0:T(8,128)(2,1)S(1)} %get-tuple-element.30), channel_id=1, source_target_pairs={{0,3},{2,1},{4,7},{5,6},{7,4},{9,10},{10,9},{11,8},{13,14},{14,13}... | collective-permute-start | bytes 405512 | tf_op jit(solution)/shard_map/ppermute | solution.py:332
  40.5 13.2 %collective-permute-start.9 = (bf16[528,128]{1,0:T(8,128)(2,1)S(1)}, bf16[528,128]{1,0:T(8,128)(2,1)S(1)}, u32[]{:S(2)}, u32[]{:S(2)}) collective-permute-start(bf16[528,128]{1,0:T(8,128)(2,1)S(1)} %get-tuple-element.31), channel_id=1, source_target_pairs={{0,5},{2,7},{4,1},{5,0},{7,2},{9,12},{10,15},{11,14},{13,8},{14,11... | collective-permute-start | bytes 405512 | tf_op jit(solution)/shard_map/ppermute | solution.py:332
  41.8 11.9 %collective-permute-start.10 = (bf16[528,128]{1,0:T(8,128)(2,1)S(1)}, bf16[528,128]{1,0:T(8,128)(2,1)S(1)}, u32[]{:S(2)}, u32[]{:S(2)}) collective-permute-start(bf16[528,128]{1,0:T(8,128)(2,1)S(1)} %get-tuple-element.32), channel_id=1, source_target_pairs={{0,4},{2,6},{4,0},{5,1},{7,3},{9,13},{10,14},{11,15},{13,9},{14,10... | collective-permute-start | bytes 405512 | tf_op jit(solution)/shard_map/ppermute | solution.py:332
  47.1 8.6 %collective-permute-start.11 = (bf16[528,128]{1,0:T(8,128)(2,1)S(1)}, bf16[528,128]{1,0:T(8,128)(2,1)S(1)}, u32[]{:S(2)}, u32[]{:S(2)}) collective-permute-start(bf16[528,128]{1,0:T(8,128)(2,1)S(1)} %get-tuple-element.33), channel_id=1, source_target_pairs={{0,2},{2,0},{4,6},{5,7},{7,5},{9,11},{10,8},{11,9},{13,15},{14,12}... | collective-permute-start | bytes 405512 | tf_op jit(solution)/shard_map/ppermute | solution.py:332
  48.5 9.9 %collective-permute-start.12 = (bf16[528,128]{1,0:T(8,128)(2,1)S(1)}, bf16[528,128]{1,0:T(8,128)(2,1)S(1)}, u32[]{:S(2)}, u32[]{:S(2)}) collective-permute-start(bf16[528,128]{1,0:T(8,128)(2,1)S(1)} %get-tuple-element.34), channel_id=1, source_target_pairs={{0,6},{2,4},{4,2},{5,3},{7,1},{9,15},{10,12},{11,13},{13,11},{14,8... | collective-permute-start | bytes 405512 | tf_op jit(solution)/shard_map/ppermute | solution.py:332
  51.6 6.9 %collective-permute-start.13 = (bf16[528,128]{1,0:T(8,128)(2,1)S(1)}, bf16[528,128]{1,0:T(8,128)(2,1)S(1)}, u32[]{:S(2)}, u32[]{:S(2)}) collective-permute-start(bf16[528,128]{1,0:T(8,128)(2,1)S(1)} %get-tuple-element.35), channel_id=1, source_target_pairs={{0,1},{2,3},{4,5},{5,4},{7,6},{9,8},{10,11},{11,10},{13,12},{14,15... | collective-permute-start | bytes 405512 | tf_op jit(solution)/shard_map/ppermute | solution.py:332
  58.5 3.1 %collective-permute-start.16 = (f32[8,128]{1,0:T(8,128)S(1)}, f32[8,128]{1,0:T(8,128)S(1)}, u32[]{:S(2)}, u32[]{:S(2)}) collective-permute-start(f32[8,128]{1,0:T(8,128)S(1)} %totals.1.refs_0_), channel_id=1, source_target_pairs={{0,24},{8,16},{16,8},{24,0},{1,25},{9,17},{17,9},{25,1},{2,26},{10... | collective-permute-start | bytes 12296 | tf_op jit(solution)/shard_map/ppermute | solution.py:357
  58.6 3.7 %collective-permute-start.15 = (f32[8,128]{1,0:T(8,128)S(1)}, f32[8,128]{1,0:T(8,128)S(1)}, u32[]{:S(2)}, u32[]{:S(2)}) collective-permute-start(f32[8,128]{1,0:T(8,128)S(1)} %totals.1.refs_0_), channel_id=1, source_target_pairs={{0,16},{8,24},{16,0},{24,8},{1,17},{9,25},{17,1},{25,9},{2,18},{10... | collective-permute-start | bytes 12296 | tf_op jit(solution)/shard_map/ppermute | solution.py:357
  59.3 2.9 %collective-permute-start.14 = (f32[8,128]{1,0:T(8,128)S(1)}, f32[8,128]{1,0:T(8,128)S(1)}, u32[]{:S(2)}, u32[]{:S(2)}) collective-permute-start(f32[8,128]{1,0:T(8,128)S(1)} %totals.1.refs_0_), channel_id=1, source_target_pairs={{0,8},{8,0},{16,24},{24,16},{1,9},{9,1},{17,25},{25,17},{2,10},{10... | collective-permute-start | bytes 12296 | tf_op jit(solution)/shard_map/ppermute | solution.py:357

commit v6 on v5

--- a/solution.py
+++ b/solution.py
@@ -102,8 +102,12 @@
         def masked(scores, axis):
             parts = jnp.split(scores, blocks, axis=axis)
             for i in sorted({0, blocks - 1}):
-                key = lax.broadcasted_iota(jnp.int32, parts[i].shape, axis) + i * LANES
-                parts[i] = jnp.where((key >= start) & (key < start + length), parts[i], -jnp.inf)
+                shape = (1, LANES) if axis == 1 else (LANES, LANES)
+                key = lax.broadcasted_iota(jnp.int32, shape, axis) + i * LANES
+                bias = jnp.where((key >= start) & (key < start + length), 0.0, -jnp.inf)
+                if axis == 0:
+                    bias = jnp.concatenate([bias] * (scores.shape[1] // LANES), axis=1)
+                parts[i] = parts[i] + bias
             return jnp.concatenate(parts, axis=axis)
 
         def powers(scores, axis):
@@ -137,8 +141,13 @@
             key_part = jnp.dot(dscores, data[0, mine, :], preferred_element_type=F32)
             value_part = product(weights, gradient)
             grads[0, mine, :] += (dquery * scale).T
-            query = lax.broadcasted_iota(jnp.int32, (width, HS), 0) + begin
-            grads[3, mine, :] += jnp.where((query >= start) & (query < start + length), target, 0.0)
+            parts = jnp.split(target, width // LANES, axis=0)
+            for i in {0, blocks - 1} & {i + begin // LANES for i in range(width // LANES)}:
+                query = lax.broadcasted_iota(jnp.int32, (LANES, HS), 0) + i * LANES
+                keep = (query >= start) & (query < start + length)
+                i = i - begin // LANES
+                parts[i] = jnp.where(keep, parts[i], 0.0)
+            grads[3, mine, :] += jnp.concatenate(parts, axis=0)
             dkey = key_part if dkey is None else dkey + key_part
             dvalue = value_part if dvalue is None else dvalue + value_part
         grads[1, window, :] += dkey * scale

time: 64.7 us -> 64.7 us (level)
  no operation moved by 1% of the time
where the time goes in v6:
time: 64.7 us; the launch traced here: 63.5 us
  starting transfers between devices  37.5 us (58%)
  waiting for transfers between devices  16.5 us (26%)
  Pallas kernels  8.7 us (13%)
  between operations  0.83 us (1%)
    ppermute x7, starting transfers between devices, per_device(): lax.ppermute(mine, axes, pairs(lambda owners, start: [(start + (d ^ k), s...  18 us
    ppermute x7, starting transfers between devices, per_device(): lax.ppermute(mine, axes, pairs(lambda owners, start: [(start + d, start +...  17.6 us
    ppermute x7, waiting for transfers between devices, per_device(): lax.ppermute(mine, axes, pairs(lambda owners, start: [(start + (d ^ k), s...  9.88 us
    pallas_call x1, Pallas kernels, per_device(): pl.pallas_call(functools.partial(head_kernel, clip_count, extra), out_sha...  5.64 us
    ppermute x7, waiting for transfers between devices, per_device(): lax.ppermute(mine, axes, pairs(lambda owners, start: [(start + d, start +...  4.76 us
    ppermute x3, starting transfers between devices, over(): return lax.ppermute(totals, axis, [(s, s ^ step) for s in range(count)])  1.92 us
    ppermute x3, waiting for transfers between devices, over(): return lax.ppermute(totals, axis, [(s, s ^ step) for s in range(count)])  1.83 us
    pallas_call x1, Pallas kernels, per_device(): pl.pallas_call(functools.partial(finish_kernel, clip_count, head_count, e...  1.58 us
  transfers between devices with their start and end apart: 17, of which 8 were waited for; matrix products, arithmetic and copies ran while one was open for 0% of the time, Pallas kernels for 0%

profile of v6, /device:TPU:18, one launch (start us, length us, event | category | flops | bytes accessed | tf_op | source)
XLA Modules:
  0.0 63.5 jit_solution(6141284248430779340)
XLA Ops:
  0.6 1.5 %pack.1 = (bf16[6,128,128]{2,1,0:T(8,128)(2,1)S(1)}, bf16[6,128,128]{2,1,0:T(8,128)(2,1)S(1)}, bf16[6,128,128]{2,1,0:T(8,128)(2,1)S(1)}, bf16[6,128,128]{2,1,0:T...) custom-call(bf16[3,128,640]{2,1,0:T(8,128)(2,1)} %bitcast.3, ...), custom_call_target="tpu_custom_call" | custom-call | tf_op jit(solution)/shard_map/pack/pallas_call | solution.py:287
  2.1 2.2 %collective-permute-start = (bf16[6,128,128]{2,1,0:T(8,128)(2,1)S(1)}, bf16[6,128,128]{2,1,0:T(8,128)(2,1)S(1)}, u32[]{:S(2)}, u32[]{:S(2)}) collective-permute-start(bf16[6,128,128]{2,1,0:T(8,128)(2,1)S(1)} %get-tuple-element.21), channel_id=1, source_target_pairs={{4,0},{6,2},{0,4},{1,5},{3,7},{13,9},{14,10},{15,11},{9,13},{10,14... | collective-permute-start | bytes 589832 | tf_op jit(solution)/shard_map/ppermute | solution.py:303
  4.4 3.5 %collective-permute-start.1 = (bf16[6,128,128]{2,1,0:T(8,128)(2,1)S(1)}, bf16[6,128,128]{2,1,0:T(8,128)(2,1)S(1)}, u32[]{:S(2)}, u32[]{:S(2)}) collective-permute-start(bf16[6,128,128]{2,1,0:T(8,128)(2,1)S(1)} %get-tuple-element.22), channel_id=1, source_target_pairs={{3,0},{1,2},{7,4},{6,5},{4,7},{10,9},{9,10},{8,11},{14,13},{13,14}... | collective-permute-start | bytes 589832 | tf_op jit(solution)/shard_map/ppermute | solution.py:303
  7.9 1.3 %collective-permute-start.2 = (bf16[6,128,128]{2,1,0:T(8,128)(2,1)S(1)}, bf16[6,128,128]{2,1,0:T(8,128)(2,1)S(1)}, u32[]{:S(2)}, u32[]{:S(2)}) collective-permute-start(bf16[6,128,128]{2,1,0:T(8,128)(2,1)S(1)} %get-tuple-element.23), channel_id=1, source_target_pairs={{5,0},{7,2},{1,4},{0,5},{2,7},{12,9},{15,10},{14,11},{8,13},{11,14... | collective-permute-start | bytes 589832 | tf_op jit(solution)/shard_map/ppermute | solution.py:303
  9.2 4.4 %collective-permute-start.3 = (bf16[6,128,128]{2,1,0:T(8,128)(2,1)S(1)}, bf16[6,128,128]{2,1,0:T(8,128)(2,1)S(1)}, u32[]{:S(2)}, u32[]{:S(2)}) collective-permute-start(bf16[6,128,128]{2,1,0:T(8,128)(2,1)S(1)} %get-tuple-element.24), channel_id=1, source_target_pairs={{1,0},{3,2},{5,4},{4,5},{6,7},{8,9},{11,10},{10,11},{12,13},{15,14... | collective-permute-start | bytes 589832 | tf_op jit(solution)/shard_map/ppermute | solution.py:303
  13.5 1.3 %collective-permute-start.4 = (bf16[6,128,128]{2,1,0:T(8,128)(2,1)S(1)}, bf16[6,128,128]{2,1,0:T(8,128)(2,1)S(1)}, u32[]{:S(2)}, u32[]{:S(2)}) collective-permute-start(bf16[6,128,128]{2,1,0:T(8,128)(2,1)S(1)} %get-tuple-element.25), channel_id=1, source_target_pairs={{7,0},{5,2},{3,4},{2,5},{0,7},{14,9},{13,10},{12,11},{10,13},{9,14... | collective-permute-start | bytes 589832 | tf_op jit(solution)/shard_map/ppermute | solution.py:303
  14.8 4.0 %collective-permute-start.5 = (bf16[6,128,128]{2,1,0:T(8,128)(2,1)S(1)}, bf16[6,128,128]{2,1,0:T(8,128)(2,1)S(1)}, u32[]{:S(2)}, u32[]{:S(2)}) collective-permute-start(bf16[6,128,128]{2,1,0:T(8,128)(2,1)S(1)} %get-tuple-element.26), channel_id=1, source_target_pairs={{6,0},{4,2},{2,4},{3,5},{1,7},{15,9},{12,10},{13,11},{11,13},{8,14... | collective-permute-start | bytes 589832 | tf_op jit(solution)/shard_map/ppermute | solution.py:303
  18.9 1.3 %collective-permute-start.6 = (bf16[6,128,128]{2,1,0:T(8,128)(2,1)S(1)}, bf16[6,128,128]{2,1,0:T(8,128)(2,1)S(1)}, u32[]{:S(2)}, u32[]{:S(2)}) collective-permute-start(bf16[6,128,128]{2,1,0:T(8,128)(2,1)S(1)} %get-tuple-element.27), channel_id=1, source_target_pairs={{2,0},{0,2},{6,4},{7,5},{5,7},{11,9},{8,10},{9,11},{15,13},{12,14}... | collective-permute-start | bytes 589832 | tf_op jit(solution)/shard_map/ppermute | solution.py:303
  20.2 2.6 %collective-permute-done.2.refs_3_ = bf16[6,128,128]{2,1,0:T(8,128)(2,1)S(1)} collective-permute-done((bf16[6,128,128]{2,1,0:T(8,128)(2,1)S(1)}, bf16[6,128,128]{2,1,0:T(8,128)(2,1)S(1)}, u32[]{:S(2)}, u32[]{:S(2)}) %collective-permute-start.2) | collective-permute-done | bytes 196640 | tf_op jit(solution)/shard_map/ppermute | solution.py:303
  22.8 6.1 %collective-permute-done.4.refs_5_ = bf16[6,128,128]{2,1,0:T(8,128)(2,1)S(1)} collective-permute-done((bf16[6,128,128]{2,1,0:T(8,128)(2,1)S(1)}, bf16[6,128,128]{2,1,0:T(8,128)(2,1)S(1)}, u32[]{:S(2)}, u32[]{:S(2)}) %collective-permute-start.4) | collective-permute-done | bytes 196640 | tf_op jit(solution)/shard_map/ppermute | solution.py:303
  28.9 1.1 %collective-permute-done.5.refs_6_ = bf16[6,128,128]{2,1,0:T(8,128)(2,1)S(1)} collective-permute-done((bf16[6,128,128]{2,1,0:T(8,128)(2,1)S(1)}, bf16[6,128,128]{2,1,0:T(8,128)(2,1)S(1)}, u32[]{:S(2)}, u32[]{:S(2)}) %collective-permute-start.5) | collective-permute-done | bytes 196640 | tf_op jit(solution)/shard_map/ppermute | solution.py:303
  30.1 5.6 %heads.1 = (bf16[528,128]{1,0:T(8,128)(2,1)S(1)}, bf16[528,128]{1,0:T(8,128)(2,1)S(1)}, bf16[528,128]{1,0:T(8,128)(2,1)S(1)}, bf16[528,128]{1,0:T(8,128)(2,1)S(1...) custom-call(s32[4]{0:T(128)S(1)} %copy-done, ...), custom_call_target="tpu_custom_call" | custom-call | tf_op jit(solution)/shard_map/heads/pallas_call | solution.py:323
  35.7 1.3 %collective-permute-start.7 = (bf16[528,128]{1,0:T(8,128)(2,1)S(1)}, bf16[528,128]{1,0:T(8,128)(2,1)S(1)}, u32[]{:S(2)}, u32[]{:S(2)}) collective-permute-start(bf16[528,128]{1,0:T(8,128)(2,1)S(1)} %get-tuple-element.29), channel_id=1, source_target_pairs={{0,7},{2,5},{4,3},{5,2},{7,0},{9,14},{10,13},{11,12},{13,10},{14,9... | collective-permute-start | bytes 405512 | tf_op jit(solution)/shard_map/ppermute | solution.py:341
  37.0 3.1 %collective-permute-start.8 = (bf16[528,128]{1,0:T(8,128)(2,1)S(1)}, bf16[528,128]{1,0:T(8,128)(2,1)S(1)}, u32[]{:S(2)}, u32[]{:S(2)}) collective-permute-start(bf16[528,128]{1,0:T(8,128)(2,1)S(1)} %get-tuple-element.30), channel_id=1, source_target_pairs={{0,3},{2,1},{4,7},{5,6},{7,4},{9,10},{10,9},{11,8},{13,14},{14,13}... | collective-permute-start | bytes 405512 | tf_op jit(solution)/shard_map/ppermute | solution.py:341
  40.1 1.3 %collective-permute-start.9 = (bf16[528,128]{1,0:T(8,128)(2,1)S(1)}, bf16[528,128]{1,0:T(8,128)(2,1)S(1)}, u32[]{:S(2)}, u32[]{:S(2)}) collective-permute-start(bf16[528,128]{1,0:T(8,128)(2,1)S(1)} %get-tuple-element.31), channel_id=1, source_target_pairs={{0,5},{2,7},{4,1},{5,0},{7,2},{9,12},{10,15},{11,14},{13,8},{14,11... | collective-permute-start | bytes 405512 | tf_op jit(solution)/shard_map/ppermute | solution.py:341
  41.4 5.3 %collective-permute-start.10 = (bf16[528,128]{1,0:T(8,128)(2,1)S(1)}, bf16[528,128]{1,0:T(8,128)(2,1)S(1)}, u32[]{:S(2)}, u32[]{:S(2)}) collective-permute-start(bf16[528,128]{1,0:T(8,128)(2,1)S(1)} %get-tuple-element.32), channel_id=1, source_target_pairs={{0,4},{2,6},{4,0},{5,1},{7,3},{9,13},{10,14},{11,15},{13,9},{14,10... | collective-permute-start | bytes 405512 | tf_op jit(solution)/shard_map/ppermute | solution.py:341
  46.8 1.3 %collective-permute-start.11 = (bf16[528,128]{1,0:T(8,128)(2,1)S(1)}, bf16[528,128]{1,0:T(8,128)(2,1)S(1)}, u32[]{:S(2)}, u32[]{:S(2)}) collective-permute-start(bf16[528,128]{1,0:T(8,128)(2,1)S(1)} %get-tuple-element.33), channel_id=1, source_target_pairs={{0,2},{2,0},{4,6},{5,7},{7,5},{9,11},{10,8},{11,9},{13,15},{14,12}... | collective-permute-start | bytes 405512 | tf_op jit(solution)/shard_map/ppermute | solution.py:341
  48.1 3.1 %collective-permute-start.12 = (bf16[528,128]{1,0:T(8,128)(2,1)S(1)}, bf16[528,128]{1,0:T(8,128)(2,1)S(1)}, u32[]{:S(2)}, u32[]{:S(2)}) collective-permute-start(bf16[528,128]{1,0:T(8,128)(2,1)S(1)} %get-tuple-element.34), channel_id=1, source_target_pairs={{0,6},{2,4},{4,2},{5,3},{7,1},{9,15},{10,12},{11,13},{13,11},{14,8... | collective-permute-start | bytes 405512 | tf_op jit(solution)/shard_map/ppermute | solution.py:341
  51.2 2.1 %collective-permute-start.13 = (bf16[528,128]{1,0:T(8,128)(2,1)S(1)}, bf16[528,128]{1,0:T(8,128)(2,1)S(1)}, u32[]{:S(2)}, u32[]{:S(2)}) collective-permute-start(bf16[528,128]{1,0:T(8,128)(2,1)S(1)} %get-tuple-element.35), channel_id=1, source_target_pairs={{0,1},{2,3},{4,5},{5,4},{7,6},{9,8},{10,11},{11,10},{13,12},{14,15... | collective-permute-start | bytes 405512 | tf_op jit(solution)/shard_map/ppermute | solution.py:341
  53.4 2.0 %collective-permute-done.11.refs_5_.refs_9_ = bf16[528,128]{1,0:T(8,128)(2,1)S(1)} collective-permute-done((bf16[528,128]{1,0:T(8,128)(2,1)S(1)}, bf16[528,128]{1,0:T(8,128)(2,1)S(1)}, u32[]{:S(2)}, u32[]{:S(2)}) %collective-permute-start.11) | collective-permute-done | bytes 135200 | tf_op jit(solution)/shard_map/ppermute | solution.py:341
  55.4 2.6 %collective-permute-done.12.refs_6_.refs_10_ = bf16[528,128]{1,0:T(8,128)(2,1)S(1)} collective-permute-done((bf16[528,128]{1,0:T(8,128)(2,1)S(1)}, bf16[528,128]{1,0:T(8,128)(2,1)S(1)}, u32[]{:S(2)}, u32[]{:S(2)}) %collective-permute-start.12) | collective-permute-done | bytes 135200 | tf_op jit(solution)/shard_map/ppermute | solution.py:341
  59.0 1.1 %collective-permute-start.14 = (f32[8,128]{1,0:T(8,128)S(1)}, f32[8,128]{1,0:T(8,128)S(1)}, u32[]{:S(2)}, u32[]{:S(2)}) collective-permute-start(f32[8,128]{1,0:T(8,128)S(1)} %totals.1.refs_0_), channel_id=1, source_target_pairs={{0,8},{8,0},{16,24},{24,16},{1,9},{9,1},{17,25},{25,17},{2,10},{10... | collective-permute-start | bytes 12296 | tf_op jit(solution)/shard_map/ppermute | solution.py:366
  60.1 1.2 %collective-permute-done.16.refs_3_ = f32[8,128]{1,0:T(8,128)S(1)} collective-permute-done((f32[8,128]{1,0:T(8,128)S(1)}, f32[8,128]{1,0:T(8,128)S(1)}, u32[]{:S(2)}, u32[]{:S(2)}) %collective-permute-start.16) | collective-permute-done | bytes 4128 | tf_op jit(solution)/shard_map/ppermute | solution.py:366
  61.9 1.6 %finish.1 = (bf16[3,128,640]{2,1,0:T(8,128)(2,1)}, bf16[128,640]{1,0:T(8,128)(2,1)}) custom-call(s32[4]{0:T(128)S(1)} %copy-done, f32[8,128]{1,0:T(8,128)S(1)} %totals.1.refs_0_, f32[8,128]{1,0:T(8,128)S(1)} %collective-permute-done.14.refs_1_, f32[8,128]{1,0:T(8,128)S(1)} %collective-permute-done.15.refs_2_, f32[8,128]{1,0:T(8,128)S(1)} %collective-permute-done.16.refs_3_, ...), custom_call_target="tpu_custom_call" | custom-call | tf_op jit(solution)/shard_map/finish/pallas_call | solution.py:374
  (16 shorter events, 1.6 us)
Async XLA Ops:
  2.1 12.7 %collective-permute-start = (bf16[6,128,128]{2,1,0:T(8,128)(2,1)S(1)}, bf16[6,128,128]{2,1,0:T(8,128)(2,1)S(1)}, u32[]{:S(2)}, u32[]{:S(2)}) collective-permute-start(bf16[6,128,128]{2,1,0:T(8,128)(2,1)S(1)} %get-tuple-element.21), channel_id=1, source_target_pairs={{4,0},{6,2},{0,4},{1,5},{3,7},{13,9},{14,10},{15,11},{9,13},{10,14... | collective-permute-start | bytes 589832 | tf_op jit(solution)/shard_map/ppermute | solution.py:303
  4.4 14.5 %collective-permute-start.1 = (bf16[6,128,128]{2,1,0:T(8,128)(2,1)S(1)}, bf16[6,128,128]{2,1,0:T(8,128)(2,1)S(1)}, u32[]{:S(2)}, u32[]{:S(2)}) collective-permute-start(bf16[6,128,128]{2,1,0:T(8,128)(2,1)S(1)} %get-tuple-element.22), channel_id=1, source_target_pairs={{3,0},{1,2},{7,4},{6,5},{4,7},{10,9},{9,10},{8,11},{14,13},{13,14}... | collective-permute-start | bytes 589832 | tf_op jit(solution)/shard_map/ppermute | solution.py:303
  7.9 15.0 %collective-permute-start.2 = (bf16[6,128,128]{2,1,0:T(8,128)(2,1)S(1)}, bf16[6,128,128]{2,1,0:T(8,128)(2,1)S(1)}, u32[]{:S(2)}, u32[]{:S(2)}) collective-permute-start(bf16[6,128,128]{2,1,0:T(8,128)(2,1)S(1)} %get-tuple-element.23), channel_id=1, source_target_pairs={{5,0},{7,2},{1,4},{0,5},{2,7},{12,9},{15,10},{14,11},{8,13},{11,14... | collective-permute-start | bytes 589832 | tf_op jit(solution)/shard_map/ppermute | solution.py:303
  9.2 13.7 %collective-permute-start.3 = (bf16[6,128,128]{2,1,0:T(8,128)(2,1)S(1)}, bf16[6,128,128]{2,1,0:T(8,128)(2,1)S(1)}, u32[]{:S(2)}, u32[]{:S(2)}) collective-permute-start(bf16[6,128,128]{2,1,0:T(8,128)(2,1)S(1)} %get-tuple-element.24), channel_id=1, source_target_pairs={{1,0},{3,2},{5,4},{4,5},{6,7},{8,9},{11,10},{10,11},{12,13},{15,14... | collective-permute-start | bytes 589832 | tf_op jit(solution)/shard_map/ppermute | solution.py:303
  13.5 15.4 %collective-permute-start.4 = (bf16[6,128,128]{2,1,0:T(8,128)(2,1)S(1)}, bf16[6,128,128]{2,1,0:T(8,128)(2,1)S(1)}, u32[]{:S(2)}, u32[]{:S(2)}) collective-permute-start(bf16[6,128,128]{2,1,0:T(8,128)(2,1)S(1)} %get-tuple-element.25), channel_id=1, source_target_pairs={{7,0},{5,2},{3,4},{2,5},{0,7},{14,9},{13,10},{12,11},{10,13},{9,14... | collective-permute-start | bytes 589832 | tf_op jit(solution)/shard_map/ppermute | solution.py:303
  14.8 15.2 %collective-permute-start.5 = (bf16[6,128,128]{2,1,0:T(8,128)(2,1)S(1)}, bf16[6,128,128]{2,1,0:T(8,128)(2,1)S(1)}, u32[]{:S(2)}, u32[]{:S(2)}) collective-permute-start(bf16[6,128,128]{2,1,0:T(8,128)(2,1)S(1)} %get-tuple-element.26), channel_id=1, source_target_pairs={{6,0},{4,2},{2,4},{3,5},{1,7},{15,9},{12,10},{13,11},{11,13},{8,14... | collective-permute-start | bytes 589832 | tf_op jit(solution)/shard_map/ppermute | solution.py:303
  18.9 11.2 %copy-start = (s32[4]{0:T(128)S(1)}, s32[4]{0:T(128)}, u32[]{:S(2)}) copy-start(s32[4]{0:T(128)} %lengths_ref.3) | copy-start | bytes 52
  18.9 11.2 %collective-permute-start.6 = (bf16[6,128,128]{2,1,0:T(8,128)(2,1)S(1)}, bf16[6,128,128]{2,1,0:T(8,128)(2,1)S(1)}, u32[]{:S(2)}, u32[]{:S(2)}) collective-permute-start(bf16[6,128,128]{2,1,0:T(8,128)(2,1)S(1)} %get-tuple-element.27), channel_id=1, source_target_pairs={{2,0},{0,2},{6,4},{7,5},{5,7},{11,9},{8,10},{9,11},{15,13},{12,14}... | collective-permute-start | bytes 589832 | tf_op jit(solution)/shard_map/ppermute | solution.py:303
  35.7 12.4 %collective-permute-start.7 = (bf16[528,128]{1,0:T(8,128)(2,1)S(1)}, bf16[528,128]{1,0:T(8,128)(2,1)S(1)}, u32[]{:S(2)}, u32[]{:S(2)}) collective-permute-start(bf16[528,128]{1,0:T(8,128)(2,1)S(1)} %get-tuple-element.29), channel_id=1, source_target_pairs={{0,7},{2,5},{4,3},{5,2},{7,0},{9,14},{10,13},{11,12},{13,10},{14,9... | collective-permute-start | bytes 405512 | tf_op jit(solution)/shard_map/ppermute | solution.py:341
  37.0 14.2 %collective-permute-start.8 = (bf16[528,128]{1,0:T(8,128)(2,1)S(1)}, bf16[528,128]{1,0:T(8,128)(2,1)S(1)}, u32[]{:S(2)}, u32[]{:S(2)}) collective-permute-start(bf16[528,128]{1,0:T(8,128)(2,1)S(1)} %get-tuple-element.30), channel_id=1, source_target_pairs={{0,3},{2,1},{4,7},{5,6},{7,4},{9,10},{10,9},{11,8},{13,14},{14,13}... | collective-permute-start | bytes 405512 | tf_op jit(solution)/shard_map/ppermute | solution.py:341
  40.1 13.2 %collective-permute-start.9 = (bf16[528,128]{1,0:T(8,128)(2,1)S(1)}, bf16[528,128]{1,0:T(8,128)(2,1)S(1)}, u32[]{:S(2)}, u32[]{:S(2)}) collective-permute-start(bf16[528,128]{1,0:T(8,128)(2,1)S(1)} %get-tuple-element.31), channel_id=1, source_target_pairs={{0,5},{2,7},{4,1},{5,0},{7,2},{9,12},{10,15},{11,14},{13,8},{14,11... | collective-permute-start | bytes 405512 | tf_op jit(solution)/shard_map/ppermute | solution.py:341
  41.4 11.9 %collective-permute-start.10 = (bf16[528,128]{1,0:T(8,128)(2,1)S(1)}, bf16[528,128]{1,0:T(8,128)(2,1)S(1)}, u32[]{:S(2)}, u32[]{:S(2)}) collective-permute-start(bf16[528,128]{1,0:T(8,128)(2,1)S(1)} %get-tuple-element.32), channel_id=1, source_target_pairs={{0,4},{2,6},{4,0},{5,1},{7,3},{9,13},{10,14},{11,15},{13,9},{14,10... | collective-permute-start | bytes 405512 | tf_op jit(solution)/shard_map/ppermute | solution.py:341
  46.8 8.6 %collective-permute-start.11 = (bf16[528,128]{1,0:T(8,128)(2,1)S(1)}, bf16[528,128]{1,0:T(8,128)(2,1)S(1)}, u32[]{:S(2)}, u32[]{:S(2)}) collective-permute-start(bf16[528,128]{1,0:T(8,128)(2,1)S(1)} %get-tuple-element.33), channel_id=1, source_target_pairs={{0,2},{2,0},{4,6},{5,7},{7,5},{9,11},{10,8},{11,9},{13,15},{14,12}... | collective-permute-start | bytes 405512 | tf_op jit(solution)/shard_map/ppermute | solution.py:341
  48.1 9.9 %collective-permute-start.12 = (bf16[528,128]{1,0:T(8,128)(2,1)S(1)}, bf16[528,128]{1,0:T(8,128)(2,1)S(1)}, u32[]{:S(2)}, u32[]{:S(2)}) collective-permute-start(bf16[528,128]{1,0:T(8,128)(2,1)S(1)} %get-tuple-element.34), channel_id=1, source_target_pairs={{0,6},{2,4},{4,2},{5,3},{7,1},{9,15},{10,12},{11,13},{13,11},{14,8... | collective-permute-start | bytes 405512 | tf_op jit(solution)/shard_map/ppermute | solution.py:341
  51.2 6.9 %collective-permute-start.13 = (bf16[528,128]{1,0:T(8,128)(2,1)S(1)}, bf16[528,128]{1,0:T(8,128)(2,1)S(1)}, u32[]{:S(2)}, u32[]{:S(2)}) collective-permute-start(bf16[528,128]{1,0:T(8,128)(2,1)S(1)} %get-tuple-element.35), channel_id=1, source_target_pairs={{0,1},{2,3},{4,5},{5,4},{7,6},{9,8},{10,11},{11,10},{13,12},{14,15... | collective-permute-start | bytes 405512 | tf_op jit(solution)/shard_map/ppermute | solution.py:341
  58.1 3.1 %collective-permute-start.16 = (f32[8,128]{1,0:T(8,128)S(1)}, f32[8,128]{1,0:T(8,128)S(1)}, u32[]{:S(2)}, u32[]{:S(2)}) collective-permute-start(f32[8,128]{1,0:T(8,128)S(1)} %totals.1.refs_0_), channel_id=1, source_target_pairs={{0,24},{8,16},{16,8},{24,0},{1,25},{9,17},{17,9},{25,1},{2,26},{10... | collective-permute-start | bytes 12296 | tf_op jit(solution)/shard_map/ppermute | solution.py:366
  58.2 3.7 %collective-permute-start.15 = (f32[8,128]{1,0:T(8,128)S(1)}, f32[8,128]{1,0:T(8,128)S(1)}, u32[]{:S(2)}, u32[]{:S(2)}) collective-permute-start(f32[8,128]{1,0:T(8,128)S(1)} %totals.1.refs_0_), channel_id=1, source_target_pairs={{0,16},{8,24},{16,0},{24,8},{1,17},{9,25},{17,1},{25,9},{2,18},{10... | collective-permute-start | bytes 12296 | tf_op jit(solution)/shard_map/ppermute | solution.py:366
  59.0 2.9 %collective-permute-start.14 = (f32[8,128]{1,0:T(8,128)S(1)}, f32[8,128]{1,0:T(8,128)S(1)}, u32[]{:S(2)}, u32[]{:S(2)}) collective-permute-start(f32[8,128]{1,0:T(8,128)S(1)} %totals.1.refs_0_), channel_id=1, source_target_pairs={{0,8},{8,0},{16,24},{24,16},{1,9},{9,1},{17,25},{25,17},{2,10},{10... | collective-permute-start | bytes 12296 | tf_op jit(solution)/shard_map/ppermute | solution.py:366

commit v7 on v5

--- a/solution.py
+++ b/solution.py
@@ -102,8 +102,12 @@
         def masked(scores, axis):
             parts = jnp.split(scores, blocks, axis=axis)
             for i in sorted({0, blocks - 1}):
-                key = lax.broadcasted_iota(jnp.int32, parts[i].shape, axis) + i * LANES
-                parts[i] = jnp.where((key >= start) & (key < start + length), parts[i], -jnp.inf)
+                shape = (1, LANES) if axis == 1 else (LANES, LANES)
+                key = lax.broadcasted_iota(jnp.int32, shape, axis) + i * LANES
+                bias = jnp.where((key >= start) & (key < start + length), 0.0, -jnp.inf)
+                if axis == 0:
+                    bias = jnp.concatenate([bias] * (scores.shape[1] // LANES), axis=1)
+                parts[i] = parts[i] + bias
             return jnp.concatenate(parts, axis=axis)
 
         def powers(scores, axis):
@@ -113,34 +117,52 @@
         def product(a, b):
             return lax.dot_general(a, b, ROWS_BY_ROWS, preferred_element_type=F32)
 
-        dkey = dvalue = total = None
-        for begin in range(0, size, QUERY_TILE):
-            width = min(QUERY_TILE, size - begin)
-            mine = pl.ds(first + begin, width)
-            columns = slice(begin, begin + width)
-            exponent = powers(masked(product(data[3, mine, :], data[4, window, :]), 1), 1)
-            values = jnp.concatenate([data[5, window, :], jnp.ones((size, HS), BF16)], axis=1)
-            both = jnp.dot(exponent.astype(BF16), values, preferred_element_type=F32)
-            target = both[:, :HS] * (1.0 / both[:, HS:])
-            exponent = powers(masked(product(data[1, window, :], data[0, mine, :]), 0), 0)
-            weights = exponent.astype(BF16)
-            inverse = 1.0 / jnp.sum(exponent, axis=0, keepdims=True)
-            student = jnp.dot(turned[1, :, window], weights, preferred_element_type=F32) * inverse
-            diff = jnp.where(inside[:, columns], student - target.T, 0.0)
-            squares = jnp.sum(diff * diff, axis=1, keepdims=True)
-            total = squares if total is None else total + squares
-            gradient = (diff * inverse).astype(BF16)
-            delta = jnp.sum(gradient.astype(F32) * student, axis=0, keepdims=True)
-            slope = jnp.dot(data[2, window, :], gradient, preferred_element_type=F32)
-            dscores = (exponent * (slope - delta)).astype(BF16)
-            dquery = jnp.dot(turned[0, :, window], dscores, preferred_element_type=F32)
-            key_part = jnp.dot(dscores, data[0, mine, :], preferred_element_type=F32)
-            value_part = product(weights, gradient)
+        tiles = range(0, size, QUERY_TILE)
+        widths = [min(QUERY_TILE, size - begin) for begin in tiles]
+        mines = [pl.ds(first + begin, width) for begin, width in zip(tiles, widths)]
+        insides = [inside[:, begin : begin + width] for begin, width in zip(tiles, widths)]
+        values = jnp.concatenate([data[5, window, :], jnp.ones((size, HS), BF16)], axis=1)
+
+        def each(function, *lists):
+            return [function(*items) for items in zip(*lists)]
+
+        target_scores = each(lambda mine: product(data[3, mine, :], data[4, window, :]), mines)
+        student_scores = each(lambda mine: product(data[1, window, :], data[0, mine, :]), mines)
+        mixed = each(lambda scores: powers(masked(scores, 1), 1).astype(BF16), target_scores)
+        exponents = each(lambda scores: powers(masked(scores, 0), 0), student_scores)
+        boths = each(lambda a: jnp.dot(a, values, preferred_element_type=F32), mixed)
+        targets = each(lambda both: both[:, :HS] * (1.0 / both[:, HS:]), boths)
+        weights = each(lambda exponent: exponent.astype(BF16), exponents)
+        inverses = each(lambda e: 1.0 / jnp.sum(e, axis=0, keepdims=True), exponents)
+        outs_t = each(
+            lambda a: jnp.dot(turned[1, :, window], a, preferred_element_type=F32), weights
+        )
+        students = each(lambda out, inverse: out * inverse, outs_t, inverses)
+        diffs = each(
+            lambda s, o, keep: jnp.where(keep, s - o.T, 0.0), students, targets, insides
+        )
+        total = sum(each(lambda diff: jnp.sum(diff * diff, axis=1, keepdims=True), diffs))
+        gradients = each(lambda diff, inverse: (diff * inverse).astype(BF16), diffs, inverses)
+        deltas = each(
+            lambda g, s: jnp.sum(g.astype(F32) * s, axis=0, keepdims=True), gradients, students
+        )
+        slopes = each(
+            lambda g: jnp.dot(data[2, window, :], g, preferred_element_type=F32), gradients
+        )
+        dscores = each(lambda e, s, d: (e * (s - d)).astype(BF16), exponents, slopes, deltas)
+        dqueries = each(
+            lambda d: jnp.dot(turned[0, :, window], d, preferred_element_type=F32), dscores
+        )
+        dkey = sum(
+            each(
+                lambda d, mine: jnp.dot(d, data[0, mine, :], preferred_element_type=F32), dscores, mines
+            )
+        )
+        dvalue = sum(each(product, weights, gradients))
+        for begin, width, mine, dquery, target in zip(tiles, widths, mines, dqueries, targets):
             grads[0, mine, :] += (dquery * scale).T
             query = lax.broadcasted_iota(jnp.int32, (width, HS), 0) + begin
             grads[3, mine, :] += jnp.where((query >= start) & (query < start + length), target, 0.0)
-            dkey = key_part if dkey is None else dkey + key_part
-            dvalue = value_part if dvalue is None else dvalue + value_part
         grads[1, window, :] += dkey * scale
         grads[2, window, :] += dvalue
         clip_iota = lax.broadcasted_iota(jnp.int32, (clip_rows, 1), 0)

time: 64.7 us -> 64.7 us (level)
  no operation moved by 1% of the time
where the time goes in v7:
time: 64.7 us; the launch traced here: 63.9 us
  starting transfers between devices  37.5 us (58%)
  waiting for transfers between devices  16.5 us (26%)
  Pallas kernels  9.13 us (14%)
  between operations  0.83 us (1%)
    ppermute x7, starting transfers between devices, per_device(): lax.ppermute(mine, axes, pairs(lambda owners, start: [(start + (d ^ k), s...  18 us
    ppermute x7, starting transfers between devices, per_device(): lax.ppermute(mine, axes, pairs(lambda owners, start: [(start + d, start +...  17.6 us
    ppermute x7, waiting for transfers between devices, per_device(): lax.ppermute(mine, axes, pairs(lambda owners, start: [(start + (d ^ k), s...  9.88 us
    pallas_call x1, Pallas kernels, per_device(): pl.pallas_call(functools.partial(head_kernel, clip_count, extra), out_sha...  6.07 us
    ppermute x7, waiting for transfers between devices, per_device(): lax.ppermute(mine, axes, pairs(lambda owners, start: [(start + d, start +...  4.76 us
    ppermute x3, starting transfers between devices, over(): return lax.ppermute(totals, axis, [(s, s ^ step) for s in range(count)])  1.92 us
    ppermute x3, waiting for transfers between devices, over(): return lax.ppermute(totals, axis, [(s, s ^ step) for s in range(count)])  1.83 us
    pallas_call x1, Pallas kernels, per_device(): pl.pallas_call(functools.partial(finish_kernel, clip_count, head_count, e...  1.58 us
  transfers between devices with their start and end apart: 17, of which 8 were waited for; matrix products, arithmetic and copies ran while one was open for 0% of the time, Pallas kernels for 0%

profile of v7, /device:TPU:18, one launch (start us, length us, event | category | flops | bytes accessed | tf_op | source)
XLA Modules:
  0.0 63.9 jit_solution(9125558547953837844)
XLA Ops:
  0.6 1.5 %pack.1 = (bf16[6,128,128]{2,1,0:T(8,128)(2,1)S(1)}, bf16[6,128,128]{2,1,0:T(8,128)(2,1)S(1)}, bf16[6,128,128]{2,1,0:T(8,128)(2,1)S(1)}, bf16[6,128,128]{2,1,0:T...) custom-call(bf16[3,128,640]{2,1,0:T(8,128)(2,1)} %bitcast.3, ...), custom_call_target="tpu_custom_call" | custom-call | tf_op jit(solution)/shard_map/pack/pallas_call | solution.py:300
  2.1 2.2 %collective-permute-start = (bf16[6,128,128]{2,1,0:T(8,128)(2,1)S(1)}, bf16[6,128,128]{2,1,0:T(8,128)(2,1)S(1)}, u32[]{:S(2)}, u32[]{:S(2)}) collective-permute-start(bf16[6,128,128]{2,1,0:T(8,128)(2,1)S(1)} %get-tuple-element.21), channel_id=1, source_target_pairs={{4,0},{6,2},{0,4},{1,5},{3,7},{13,9},{14,10},{15,11},{9,13},{10,14... | collective-permute-start | bytes 589832 | tf_op jit(solution)/shard_map/ppermute | solution.py:316
  4.4 3.5 %collective-permute-start.1 = (bf16[6,128,128]{2,1,0:T(8,128)(2,1)S(1)}, bf16[6,128,128]{2,1,0:T(8,128)(2,1)S(1)}, u32[]{:S(2)}, u32[]{:S(2)}) collective-permute-start(bf16[6,128,128]{2,1,0:T(8,128)(2,1)S(1)} %get-tuple-element.22), channel_id=1, source_target_pairs={{3,0},{1,2},{7,4},{6,5},{4,7},{10,9},{9,10},{8,11},{14,13},{13,14}... | collective-permute-start | bytes 589832 | tf_op jit(solution)/shard_map/ppermute | solution.py:316
  7.9 1.3 %collective-permute-start.2 = (bf16[6,128,128]{2,1,0:T(8,128)(2,1)S(1)}, bf16[6,128,128]{2,1,0:T(8,128)(2,1)S(1)}, u32[]{:S(2)}, u32[]{:S(2)}) collective-permute-start(bf16[6,128,128]{2,1,0:T(8,128)(2,1)S(1)} %get-tuple-element.23), channel_id=1, source_target_pairs={{5,0},{7,2},{1,4},{0,5},{2,7},{12,9},{15,10},{14,11},{8,13},{11,14... | collective-permute-start | bytes 589832 | tf_op jit(solution)/shard_map/ppermute | solution.py:316
  9.2 4.4 %collective-permute-start.3 = (bf16[6,128,128]{2,1,0:T(8,128)(2,1)S(1)}, bf16[6,128,128]{2,1,0:T(8,128)(2,1)S(1)}, u32[]{:S(2)}, u32[]{:S(2)}) collective-permute-start(bf16[6,128,128]{2,1,0:T(8,128)(2,1)S(1)} %get-tuple-element.24), channel_id=1, source_target_pairs={{1,0},{3,2},{5,4},{4,5},{6,7},{8,9},{11,10},{10,11},{12,13},{15,14... | collective-permute-start | bytes 589832 | tf_op jit(solution)/shard_map/ppermute | solution.py:316
  13.5 1.3 %collective-permute-start.4 = (bf16[6,128,128]{2,1,0:T(8,128)(2,1)S(1)}, bf16[6,128,128]{2,1,0:T(8,128)(2,1)S(1)}, u32[]{:S(2)}, u32[]{:S(2)}) collective-permute-start(bf16[6,128,128]{2,1,0:T(8,128)(2,1)S(1)} %get-tuple-element.25), channel_id=1, source_target_pairs={{7,0},{5,2},{3,4},{2,5},{0,7},{14,9},{13,10},{12,11},{10,13},{9,14... | collective-permute-start | bytes 589832 | tf_op jit(solution)/shard_map/ppermute | solution.py:316
  14.8 4.0 %collective-permute-start.5 = (bf16[6,128,128]{2,1,0:T(8,128)(2,1)S(1)}, bf16[6,128,128]{2,1,0:T(8,128)(2,1)S(1)}, u32[]{:S(2)}, u32[]{:S(2)}) collective-permute-start(bf16[6,128,128]{2,1,0:T(8,128)(2,1)S(1)} %get-tuple-element.26), channel_id=1, source_target_pairs={{6,0},{4,2},{2,4},{3,5},{1,7},{15,9},{12,10},{13,11},{11,13},{8,14... | collective-permute-start | bytes 589832 | tf_op jit(solution)/shard_map/ppermute | solution.py:316
  18.9 1.3 %collective-permute-start.6 = (bf16[6,128,128]{2,1,0:T(8,128)(2,1)S(1)}, bf16[6,128,128]{2,1,0:T(8,128)(2,1)S(1)}, u32[]{:S(2)}, u32[]{:S(2)}) collective-permute-start(bf16[6,128,128]{2,1,0:T(8,128)(2,1)S(1)} %get-tuple-element.27), channel_id=1, source_target_pairs={{2,0},{0,2},{6,4},{7,5},{5,7},{11,9},{8,10},{9,11},{15,13},{12,14}... | collective-permute-start | bytes 589832 | tf_op jit(solution)/shard_map/ppermute | solution.py:316
  20.2 2.6 %collective-permute-done.2.refs_3_ = bf16[6,128,128]{2,1,0:T(8,128)(2,1)S(1)} collective-permute-done((bf16[6,128,128]{2,1,0:T(8,128)(2,1)S(1)}, bf16[6,128,128]{2,1,0:T(8,128)(2,1)S(1)}, u32[]{:S(2)}, u32[]{:S(2)}) %collective-permute-start.2) | collective-permute-done | bytes 196640 | tf_op jit(solution)/shard_map/ppermute | solution.py:316
  22.8 6.1 %collective-permute-done.4.refs_5_ = bf16[6,128,128]{2,1,0:T(8,128)(2,1)S(1)} collective-permute-done((bf16[6,128,128]{2,1,0:T(8,128)(2,1)S(1)}, bf16[6,128,128]{2,1,0:T(8,128)(2,1)S(1)}, u32[]{:S(2)}, u32[]{:S(2)}) %collective-permute-start.4) | collective-permute-done | bytes 196640 | tf_op jit(solution)/shard_map/ppermute | solution.py:316
  28.9 1.1 %collective-permute-done.5.refs_6_ = bf16[6,128,128]{2,1,0:T(8,128)(2,1)S(1)} collective-permute-done((bf16[6,128,128]{2,1,0:T(8,128)(2,1)S(1)}, bf16[6,128,128]{2,1,0:T(8,128)(2,1)S(1)}, u32[]{:S(2)}, u32[]{:S(2)}) %collective-permute-start.5) | collective-permute-done | bytes 196640 | tf_op jit(solution)/shard_map/ppermute | solution.py:316
  30.1 6.1 %heads.1 = (bf16[528,128]{1,0:T(8,128)(2,1)S(1)}, bf16[528,128]{1,0:T(8,128)(2,1)S(1)}, bf16[528,128]{1,0:T(8,128)(2,1)S(1)}, bf16[528,128]{1,0:T(8,128)(2,1)S(1...) custom-call(s32[4]{0:T(128)S(1)} %copy-done, ...), custom_call_target="tpu_custom_call" | custom-call | tf_op jit(solution)/shard_map/heads/pallas_call | solution.py:336
  36.1 1.3 %collective-permute-start.7 = (bf16[528,128]{1,0:T(8,128)(2,1)S(1)}, bf16[528,128]{1,0:T(8,128)(2,1)S(1)}, u32[]{:S(2)}, u32[]{:S(2)}) collective-permute-start(bf16[528,128]{1,0:T(8,128)(2,1)S(1)} %get-tuple-element.29), channel_id=1, source_target_pairs={{0,7},{2,5},{4,3},{5,2},{7,0},{9,14},{10,13},{11,12},{13,10},{14,9... | collective-permute-start | bytes 405512 | tf_op jit(solution)/shard_map/ppermute | solution.py:354
  37.4 3.1 %collective-permute-start.8 = (bf16[528,128]{1,0:T(8,128)(2,1)S(1)}, bf16[528,128]{1,0:T(8,128)(2,1)S(1)}, u32[]{:S(2)}, u32[]{:S(2)}) collective-permute-start(bf16[528,128]{1,0:T(8,128)(2,1)S(1)} %get-tuple-element.30), channel_id=1, source_target_pairs={{0,3},{2,1},{4,7},{5,6},{7,4},{9,10},{10,9},{11,8},{13,14},{14,13}... | collective-permute-start | bytes 405512 | tf_op jit(solution)/shard_map/ppermute | solution.py:354
  40.5 1.3 %collective-permute-start.9 = (bf16[528,128]{1,0:T(8,128)(2,1)S(1)}, bf16[528,128]{1,0:T(8,128)(2,1)S(1)}, u32[]{:S(2)}, u32[]{:S(2)}) collective-permute-start(bf16[528,128]{1,0:T(8,128)(2,1)S(1)} %get-tuple-element.31), channel_id=1, source_target_pairs={{0,5},{2,7},{4,1},{5,0},{7,2},{9,12},{10,15},{11,14},{13,8},{14,11... | collective-permute-start | bytes 405512 | tf_op jit(solution)/shard_map/ppermute | solution.py:354
  41.8 5.4 %collective-permute-start.10 = (bf16[528,128]{1,0:T(8,128)(2,1)S(1)}, bf16[528,128]{1,0:T(8,128)(2,1)S(1)}, u32[]{:S(2)}, u32[]{:S(2)}) collective-permute-start(bf16[528,128]{1,0:T(8,128)(2,1)S(1)} %get-tuple-element.32), channel_id=1, source_target_pairs={{0,4},{2,6},{4,0},{5,1},{7,3},{9,13},{10,14},{11,15},{13,9},{14,10... | collective-permute-start | bytes 405512 | tf_op jit(solution)/shard_map/ppermute | solution.py:354
  47.2 1.3 %collective-permute-start.11 = (bf16[528,128]{1,0:T(8,128)(2,1)S(1)}, bf16[528,128]{1,0:T(8,128)(2,1)S(1)}, u32[]{:S(2)}, u32[]{:S(2)}) collective-permute-start(bf16[528,128]{1,0:T(8,128)(2,1)S(1)} %get-tuple-element.33), channel_id=1, source_target_pairs={{0,2},{2,0},{4,6},{5,7},{7,5},{9,11},{10,8},{11,9},{13,15},{14,12}... | collective-permute-start | bytes 405512 | tf_op jit(solution)/shard_map/ppermute | solution.py:354
  48.5 3.1 %collective-permute-start.12 = (bf16[528,128]{1,0:T(8,128)(2,1)S(1)}, bf16[528,128]{1,0:T(8,128)(2,1)S(1)}, u32[]{:S(2)}, u32[]{:S(2)}) collective-permute-start(bf16[528,128]{1,0:T(8,128)(2,1)S(1)} %get-tuple-element.34), channel_id=1, source_target_pairs={{0,6},{2,4},{4,2},{5,3},{7,1},{9,15},{10,12},{11,13},{13,11},{14,8... | collective-permute-start | bytes 405512 | tf_op jit(solution)/shard_map/ppermute | solution.py:354
  51.6 2.1 %collective-permute-start.13 = (bf16[528,128]{1,0:T(8,128)(2,1)S(1)}, bf16[528,128]{1,0:T(8,128)(2,1)S(1)}, u32[]{:S(2)}, u32[]{:S(2)}) collective-permute-start(bf16[528,128]{1,0:T(8,128)(2,1)S(1)} %get-tuple-element.35), channel_id=1, source_target_pairs={{0,1},{2,3},{4,5},{5,4},{7,6},{9,8},{10,11},{11,10},{13,12},{14,15... | collective-permute-start | bytes 405512 | tf_op jit(solution)/shard_map/ppermute | solution.py:354
  53.8 2.0 %collective-permute-done.11.refs_5_.refs_9_ = bf16[528,128]{1,0:T(8,128)(2,1)S(1)} collective-permute-done((bf16[528,128]{1,0:T(8,128)(2,1)S(1)}, bf16[528,128]{1,0:T(8,128)(2,1)S(1)}, u32[]{:S(2)}, u32[]{:S(2)}) %collective-permute-start.11) | collective-permute-done | bytes 135200 | tf_op jit(solution)/shard_map/ppermute | solution.py:354
  55.8 2.6 %collective-permute-done.12.refs_6_.refs_10_ = bf16[528,128]{1,0:T(8,128)(2,1)S(1)} collective-permute-done((bf16[528,128]{1,0:T(8,128)(2,1)S(1)}, bf16[528,128]{1,0:T(8,128)(2,1)S(1)}, u32[]{:S(2)}, u32[]{:S(2)}) %collective-permute-start.12) | collective-permute-done | bytes 135200 | tf_op jit(solution)/shard_map/ppermute | solution.py:354
  59.4 1.1 %collective-permute-start.14 = (f32[8,128]{1,0:T(8,128)S(1)}, f32[8,128]{1,0:T(8,128)S(1)}, u32[]{:S(2)}, u32[]{:S(2)}) collective-permute-start(f32[8,128]{1,0:T(8,128)S(1)} %totals.1.refs_0_), channel_id=1, source_target_pairs={{0,8},{8,0},{16,24},{24,16},{1,9},{9,1},{17,25},{25,17},{2,10},{10... | collective-permute-start | bytes 12296 | tf_op jit(solution)/shard_map/ppermute | solution.py:379
  60.5 1.2 %collective-permute-done.16.refs_3_ = f32[8,128]{1,0:T(8,128)S(1)} collective-permute-done((f32[8,128]{1,0:T(8,128)S(1)}, f32[8,128]{1,0:T(8,128)S(1)}, u32[]{:S(2)}, u32[]{:S(2)}) %collective-permute-start.16) | collective-permute-done | bytes 4128 | tf_op jit(solution)/shard_map/ppermute | solution.py:379
  62.3 1.6 %finish.1 = (bf16[3,128,640]{2,1,0:T(8,128)(2,1)}, bf16[128,640]{1,0:T(8,128)(2,1)}) custom-call(s32[4]{0:T(128)S(1)} %copy-done, f32[8,128]{1,0:T(8,128)S(1)} %totals.1.refs_0_, f32[8,128]{1,0:T(8,128)S(1)} %collective-permute-done.14.refs_1_, f32[8,128]{1,0:T(8,128)S(1)} %collective-permute-done.15.refs_2_, f32[8,128]{1,0:T(8,128)S(1)} %collective-permute-done.16.refs_3_, ...), custom_call_target="tpu_custom_call" | custom-call | tf_op jit(solution)/shard_map/finish/pallas_call | solution.py:387
  (16 shorter events, 1.6 us)
Async XLA Ops:
  2.1 12.7 %collective-permute-start = (bf16[6,128,128]{2,1,0:T(8,128)(2,1)S(1)}, bf16[6,128,128]{2,1,0:T(8,128)(2,1)S(1)}, u32[]{:S(2)}, u32[]{:S(2)}) collective-permute-start(bf16[6,128,128]{2,1,0:T(8,128)(2,1)S(1)} %get-tuple-element.21), channel_id=1, source_target_pairs={{4,0},{6,2},{0,4},{1,5},{3,7},{13,9},{14,10},{15,11},{9,13},{10,14... | collective-permute-start | bytes 589832 | tf_op jit(solution)/shard_map/ppermute | solution.py:316
  4.4 14.5 %collective-permute-start.1 = (bf16[6,128,128]{2,1,0:T(8,128)(2,1)S(1)}, bf16[6,128,128]{2,1,0:T(8,128)(2,1)S(1)}, u32[]{:S(2)}, u32[]{:S(2)}) collective-permute-start(bf16[6,128,128]{2,1,0:T(8,128)(2,1)S(1)} %get-tuple-element.22), channel_id=1, source_target_pairs={{3,0},{1,2},{7,4},{6,5},{4,7},{10,9},{9,10},{8,11},{14,13},{13,14}... | collective-permute-start | bytes 589832 | tf_op jit(solution)/shard_map/ppermute | solution.py:316
  7.9 15.0 %collective-permute-start.2 = (bf16[6,128,128]{2,1,0:T(8,128)(2,1)S(1)}, bf16[6,128,128]{2,1,0:T(8,128)(2,1)S(1)}, u32[]{:S(2)}, u32[]{:S(2)}) collective-permute-start(bf16[6,128,128]{2,1,0:T(8,128)(2,1)S(1)} %get-tuple-element.23), channel_id=1, source_target_pairs={{5,0},{7,2},{1,4},{0,5},{2,7},{12,9},{15,10},{14,11},{8,13},{11,14... | collective-permute-start | bytes 589832 | tf_op jit(solution)/shard_map/ppermute | solution.py:316
  9.2 13.7 %collective-permute-start.3 = (bf16[6,128,128]{2,1,0:T(8,128)(2,1)S(1)}, bf16[6,128,128]{2,1,0:T(8,128)(2,1)S(1)}, u32[]{:S(2)}, u32[]{:S(2)}) collective-permute-start(bf16[6,128,128]{2,1,0:T(8,128)(2,1)S(1)} %get-tuple-element.24), channel_id=1, source_target_pairs={{1,0},{3,2},{5,4},{4,5},{6,7},{8,9},{11,10},{10,11},{12,13},{15,14... | collective-permute-start | bytes 589832 | tf_op jit(solution)/shard_map/ppermute | solution.py:316
  13.5 15.4 %collective-permute-start.4 = (bf16[6,128,128]{2,1,0:T(8,128)(2,1)S(1)}, bf16[6,128,128]{2,1,0:T(8,128)(2,1)S(1)}, u32[]{:S(2)}, u32[]{:S(2)}) collective-permute-start(bf16[6,128,128]{2,1,0:T(8,128)(2,1)S(1)} %get-tuple-element.25), channel_id=1, source_target_pairs={{7,0},{5,2},{3,4},{2,5},{0,7},{14,9},{13,10},{12,11},{10,13},{9,14... | collective-permute-start | bytes 589832 | tf_op jit(solution)/shard_map/ppermute | solution.py:316
  14.8 15.2 %collective-permute-start.5 = (bf16[6,128,128]{2,1,0:T(8,128)(2,1)S(1)}, bf16[6,128,128]{2,1,0:T(8,128)(2,1)S(1)}, u32[]{:S(2)}, u32[]{:S(2)}) collective-permute-start(bf16[6,128,128]{2,1,0:T(8,128)(2,1)S(1)} %get-tuple-element.26), channel_id=1, source_target_pairs={{6,0},{4,2},{2,4},{3,5},{1,7},{15,9},{12,10},{13,11},{11,13},{8,14... | collective-permute-start | bytes 589832 | tf_op jit(solution)/shard_map/ppermute | solution.py:316
  18.9 11.2 %copy-start = (s32[4]{0:T(128)S(1)}, s32[4]{0:T(128)}, u32[]{:S(2)}) copy-start(s32[4]{0:T(128)} %lengths_ref.3) | copy-start | bytes 52
  18.9 11.2 %collective-permute-start.6 = (bf16[6,128,128]{2,1,0:T(8,128)(2,1)S(1)}, bf16[6,128,128]{2,1,0:T(8,128)(2,1)S(1)}, u32[]{:S(2)}, u32[]{:S(2)}) collective-permute-start(bf16[6,128,128]{2,1,0:T(8,128)(2,1)S(1)} %get-tuple-element.27), channel_id=1, source_target_pairs={{2,0},{0,2},{6,4},{7,5},{5,7},{11,9},{8,10},{9,11},{15,13},{12,14}... | collective-permute-start | bytes 589832 | tf_op jit(solution)/shard_map/ppermute | solution.py:316
  36.1 12.4 %collective-permute-start.7 = (bf16[528,128]{1,0:T(8,128)(2,1)S(1)}, bf16[528,128]{1,0:T(8,128)(2,1)S(1)}, u32[]{:S(2)}, u32[]{:S(2)}) collective-permute-start(bf16[528,128]{1,0:T(8,128)(2,1)S(1)} %get-tuple-element.29), channel_id=1, source_target_pairs={{0,7},{2,5},{4,3},{5,2},{7,0},{9,14},{10,13},{11,12},{13,10},{14,9... | collective-permute-start | bytes 405512 | tf_op jit(solution)/shard_map/ppermute | solution.py:354
  37.4 14.2 %collective-permute-start.8 = (bf16[528,128]{1,0:T(8,128)(2,1)S(1)}, bf16[528,128]{1,0:T(8,128)(2,1)S(1)}, u32[]{:S(2)}, u32[]{:S(2)}) collective-permute-start(bf16[528,128]{1,0:T(8,128)(2,1)S(1)} %get-tuple-element.30), channel_id=1, source_target_pairs={{0,3},{2,1},{4,7},{5,6},{7,4},{9,10},{10,9},{11,8},{13,14},{14,13}... | collective-permute-start | bytes 405512 | tf_op jit(solution)/shard_map/ppermute | solution.py:354
  40.5 13.2 %collective-permute-start.9 = (bf16[528,128]{1,0:T(8,128)(2,1)S(1)}, bf16[528,128]{1,0:T(8,128)(2,1)S(1)}, u32[]{:S(2)}, u32[]{:S(2)}) collective-permute-start(bf16[528,128]{1,0:T(8,128)(2,1)S(1)} %get-tuple-element.31), channel_id=1, source_target_pairs={{0,5},{2,7},{4,1},{5,0},{7,2},{9,12},{10,15},{11,14},{13,8},{14,11... | collective-permute-start | bytes 405512 | tf_op jit(solution)/shard_map/ppermute | solution.py:354
  41.8 11.9 %collective-permute-start.10 = (bf16[528,128]{1,0:T(8,128)(2,1)S(1)}, bf16[528,128]{1,0:T(8,128)(2,1)S(1)}, u32[]{:S(2)}, u32[]{:S(2)}) collective-permute-start(bf16[528,128]{1,0:T(8,128)(2,1)S(1)} %get-tuple-element.32), channel_id=1, source_target_pairs={{0,4},{2,6},{4,0},{5,1},{7,3},{9,13},{10,14},{11,15},{13,9},{14,10... | collective-permute-start | bytes 405512 | tf_op jit(solution)/shard_map/ppermute | solution.py:354
  47.2 8.6 %collective-permute-start.11 = (bf16[528,128]{1,0:T(8,128)(2,1)S(1)}, bf16[528,128]{1,0:T(8,128)(2,1)S(1)}, u32[]{:S(2)}, u32[]{:S(2)}) collective-permute-start(bf16[528,128]{1,0:T(8,128)(2,1)S(1)} %get-tuple-element.33), channel_id=1, source_target_pairs={{0,2},{2,0},{4,6},{5,7},{7,5},{9,11},{10,8},{11,9},{13,15},{14,12}... | collective-permute-start | bytes 405512 | tf_op jit(solution)/shard_map/ppermute | solution.py:354
  48.5 9.9 %collective-permute-start.12 = (bf16[528,128]{1,0:T(8,128)(2,1)S(1)}, bf16[528,128]{1,0:T(8,128)(2,1)S(1)}, u32[]{:S(2)}, u32[]{:S(2)}) collective-permute-start(bf16[528,128]{1,0:T(8,128)(2,1)S(1)} %get-tuple-element.34), channel_id=1, source_target_pairs={{0,6},{2,4},{4,2},{5,3},{7,1},{9,15},{10,12},{11,13},{13,11},{14,8... | collective-permute-start | bytes 405512 | tf_op jit(solution)/shard_map/ppermute | solution.py:354
  51.6 6.9 %collective-permute-start.13 = (bf16[528,128]{1,0:T(8,128)(2,1)S(1)}, bf16[528,128]{1,0:T(8,128)(2,1)S(1)}, u32[]{:S(2)}, u32[]{:S(2)}) collective-permute-start(bf16[528,128]{1,0:T(8,128)(2,1)S(1)} %get-tuple-element.35), channel_id=1, source_target_pairs={{0,1},{2,3},{4,5},{5,4},{7,6},{9,8},{10,11},{11,10},{13,12},{14,15... | collective-permute-start | bytes 405512 | tf_op jit(solution)/shard_map/ppermute | solution.py:354
  58.6 3.1 %collective-permute-start.16 = (f32[8,128]{1,0:T(8,128)S(1)}, f32[8,128]{1,0:T(8,128)S(1)}, u32[]{:S(2)}, u32[]{:S(2)}) collective-permute-start(f32[8,128]{1,0:T(8,128)S(1)} %totals.1.refs_0_), channel_id=1, source_target_pairs={{0,24},{8,16},{16,8},{24,0},{1,25},{9,17},{17,9},{25,1},{2,26},{10... | collective-permute-start | bytes 12296 | tf_op jit(solution)/shard_map/ppermute | solution.py:379
  58.6 3.7 %collective-permute-start.15 = (f32[8,128]{1,0:T(8,128)S(1)}, f32[8,128]{1,0:T(8,128)S(1)}, u32[]{:S(2)}, u32[]{:S(2)}) collective-permute-start(f32[8,128]{1,0:T(8,128)S(1)} %totals.1.refs_0_), channel_id=1, source_target_pairs={{0,16},{8,24},{16,0},{24,8},{1,17},{9,25},{17,1},{25,9},{2,18},{10... | collective-permute-start | bytes 12296 | tf_op jit(solution)/shard_map/ppermute | solution.py:379
  59.4 2.9 %collective-permute-start.14 = (f32[8,128]{1,0:T(8,128)S(1)}, f32[8,128]{1,0:T(8,128)S(1)}, u32[]{:S(2)}, u32[]{:S(2)}) collective-permute-start(f32[8,128]{1,0:T(8,128)S(1)} %totals.1.refs_0_), channel_id=1, source_target_pairs={{0,8},{8,0},{16,24},{24,16},{1,9},{9,1},{17,25},{25,17},{2,10},{10... | collective-permute-start | bytes 12296 | tf_op jit(solution)/shard_map/ppermute | solution.py:379
